TPU v7x, 32 devices: a whole 2x2x4 slice. The times are simulated.
32 devices in a mesh: group: 2 (over y), chan: 4 (over z), band: 2 (over x), beam: 2 (over core).
Axes of the slice: x: 2, y: 2, z: 4, core: 2. Of those that a mesh axis runs over, the one named last changes fastest.
Arguments:
- voltages: bfloat16 [2, 1024, 2, 8, 512], P(None, 'chan', 'band', None, 'group'), parts along dimension 4, may hold values from -6 to 6
- gains: float32 [2, 2, 8, 1024], P(None, 'band', 'chan'), may hold values from -5 to 5
- positions: float32 [3, 1024], replicated, may hold values from -4 to 4
- directions: float32 [3, 2048], P(None, ('group', 'beam')), parts along dimension 1, may hold values from -1 to 1
- antenna_row_lookup: int32 [1024], replicated, may hold values from 0 to 1023, each once
- chan_order: int32 [16], replicated, may hold values from 0 to 15, each once
- delays: int32 [4, 2, 8], replicated, may hold values from 0 to 31
Outputs:
- dedispersed: float32 [2, 8, 32, 2048], P('band', 'chan', None, ('group', 'beam')), parts along dimension 3
There are 2 independent parts, one for each index of `group`. A program takes and returns all parts, laid end to end along the dimension named above; an argument that names none is the same for every part. Nothing has to cross between parts.
Inputs may be any that keep to these rules, and one draw needn't show every extreme that they name: `antenna_row_lookup`: each antenna appears once. `chan_order`: each frequency index appears once.
All inputs are finite; a program needn't handle non-finite values.
Results may differ from a plain program's by a relative error of at most 0.004.
Values may be sent and summed in bfloat16 or wider, within the bound.
No kernel may reach another device: no remote copies, remote signals or barrier semaphores. Data moves between devices by JAX's collectives and lax.ppermute only.
A program may use at most 64 MiB of HBM per device.

v0:
```python
import math

import jax
import jax.numpy as jnp
from jax import lax
from jax.sharding import PartitionSpec as P

INTEG = 8


def partner_2(value, axis, distance):
    mask = 2**distance
    pairs = [(source, source ^ mask) for source in range(lax.axis_size(axis))]
    return lax.ppermute(value, axis, pairs)


def roll_rows(state, shifts):
    length = state.shape[1]
    doubled = jnp.concatenate([state, state], axis=1)

    def one_row(row, shift):
        return lax.dynamic_slice_in_dim(row, length - shift, length, 0)

    return jax.vmap(one_row)(doubled, shifts)


def pair_round(state, shifts, stride):
    count, length, width = state.shape
    grouped = state.reshape(count // (2 * stride), 2, stride, length, width)
    lower = jnp.broadcast_to(grouped[:, 0:1], grouped.shape).reshape(state.shape)
    upper = jnp.broadcast_to(grouped[:, 1:2], grouped.shape).reshape(state.shape)
    return lower + roll_rows(upper, shifts)


def partner_round(state, partner, upper_side, shifts):
    lower = jnp.where(upper_side, partner, state)
    upper = jnp.where(upper_side, state, partner)
    return lower + roll_rows(upper, shifts)


def beam_weights(gain_pair, freq, pos_rows, dirs):
    geometry = pos_rows[0][:, None] * dirs[0][None, :]
    geometry = geometry + pos_rows[1][:, None] * dirs[1][None, :]
    geometry = geometry + pos_rows[2][:, None] * dirs[2][None, :]
    phase = (2.0 * math.pi * freq)[:, None, None] * geometry[None]
    cosine = jnp.cos(phase)
    sine = jnp.sin(phase)
    g_re = gain_pair[0][:, :, None]
    g_im = gain_pair[1][:, :, None]
    factor = 1.0 / math.sqrt(pos_rows.shape[1])
    w_re = ((g_re * cosine + g_im * sine) * factor).astype(jnp.bfloat16)
    w_im = ((g_im * cosine - g_re * sine) * factor).astype(jnp.bfloat16)
    upper_rows = jnp.concatenate([w_re, w_im], axis=2)
    lower_rows = jnp.concatenate([-w_im, w_re], axis=2)
    return jnp.stack([upper_rows, lower_rows], axis=1)


def integrate(power, chans):
    count, samples, width = power.shape
    binned = jnp.mean(power.reshape(count, samples // INTEG, INTEG, width), axis=2)
    centred = binned - jnp.mean(binned, axis=1, keepdims=True)
    return centred * (1.0 / math.sqrt(chans))


def shards(voltages, gains, positions, directions, antenna_row_lookup, chan_order, delays):
    chan_count = lax.axis_size("chan")
    band_count = lax.axis_size("band")
    per_dev = gains.shape[2]
    in_band = per_dev * chan_count
    total = in_band * band_count
    chan_index = lax.axis_index("chan")
    band_index = lax.axis_index("band")
    base = band_index * in_band + chan_index * per_dev
    freq = 1.0 + lax.dynamic_slice_in_dim(chan_order, base, per_dev).astype(jnp.float32) / total
    pos_rows = positions[:, antenna_row_lookup]
    weights = beam_weights(gains[:, 0], freq, pos_rows, directions)
    turned = lax.all_to_all(voltages, "chan", split_axis=3, concat_axis=1, tiled=True)
    flat = turned.reshape(turned.shape[0], turned.shape[1], turned.shape[3], turned.shape[4])
    beams = jnp.einsum("pacn,cpaq->cnq", flat, weights, preferred_element_type=jnp.float32)
    half = beams.shape[2] // 2
    power = beams[:, :, :half] * beams[:, :, :half] + beams[:, :, half:] * beams[:, :, half:]
    state = integrate(power, total)
    flat_delays = delays.reshape(delays.shape[0], total)
    local_bits = per_dev.bit_length() - 1
    chan_bits = chan_count.bit_length() - 1
    band_bits = band_count.bit_length() - 1
    bit = 0
    shifts = lax.dynamic_slice_in_dim(flat_delays[bit], base, per_dev)
    state = pair_round(state, shifts, 1 << bit)
    for bit in range(chan_bits):
        level_no = local_bits + bit
        shifts = lax.dynamic_slice_in_dim(flat_delays[level_no], base, per_dev)
        partner = partner_2(state, "chan", bit)
        upper_side = chan_index // (1 << bit) % 2 == 1
        state = partner_round(state, partner, upper_side, shifts)
    for bit in range(band_bits):
        level_no = local_bits + chan_bits + bit
        shifts = lax.dynamic_slice_in_dim(flat_delays[level_no], base, per_dev)
        partner = partner_2(state, "band", bit)
        upper_side = band_index // (1 << bit) % 2 == 1
        state = partner_round(state, partner, upper_side, shifts)
    return state.reshape(1, per_dev, state.shape[1], state.shape[2])


def solution(mesh):
    placed = (
        P(None, "chan", "band", None, "group"),
        P(None, "band", "chan", None),
        P(),
        P(None, ("group", "beam")),
        P(),
        P(),
        P(),
    )
    return jax.shard_map(
        shards,
        mesh=mesh,
        in_specs=placed,
        out_specs=P("band", "chan", None, ("group", "beam")),
        check_vma=False,
    )
```

profile of v0, /device:TPU:0, one launch (start us, length us, event | category | flops | bytes accessed | tf_op | source)
XLA Modules:
  0.0 94.2 jit_solution(8014257760844754673)
XLA Ops:
  0.0 3.5 %copy.29 = bf16[2,256,1,8,256]{4,1,2,0,3:T(8,128)(2,1)} copy(bf16[2,256,1,8,256]{4,3,2,1,0:T(8,128)(2,1)} %param.7) | data formatting | bytes 4194304 | tf_op args[0]
  3.5 6.4 %all-to-all-start = ((bf16[2,256,1,8,256]{4,1,2,0,3:T(8,128)(2,1)}), bf16[2,256,1,8,256]{4,1,2,0,3:T(8,128)(2,1)S(1)}, u32[]{:S(2)}, u32[]{:S(2)}) async-start(bf16[2,256,1,8,256]{4,1,2,0,3:T(8,128)(2,1)} %copy.29), calls=%async_computation | async-start | bytes 4194304 | tf_op jit(solution)/shard_map/all_to_all | solution.py:77
  9.9 0.2 copy.27
  10.3 2.8 %gather_fusion = f32[1024,3]{1,0:T(8,128)S(1)} fusion(f32[3,1024]{0,1:T(8,128)S(1)} %copy.27, s32[1024]{0:T(1024)S(1)} %fusion.21), kind=kCustom, calls=%fused_computation | custom fusion | bytes 28672 | tf_op jit(solution)/shard_map/gather | solution.py:75
  13.3 0.8 slice_reduce_fusion.2
  14.1 0.5 multiply_add_fusion
  14.6 15.9 %fusion.10 = bf16[2,1024,512]{2,1,0:T(8,128)(2,1)S(1)} fusion(f32[2,1024]{1,0:T(2,128)S(1)} %get-tuple-element.15, f32[1024,512]{1,0:T(8,128)S(1)} %multiply_add_fusion, f32[2]{0:T(128)S(1)} %add_multiply_fusion, f32[2,1024]{1,0:T(2,128)S(1)} %get-tuple-element.14), kind=kLoop, calls=%fused_computation.17 | loop fusion | flops 6291456 | bytes 4210696 | tf_op jit(solution)/shard_map/convert_element_type | solution.py:51
  30.4 16.1 %fusion.31 = (bf16[2,1024,512]{2,1,0:T(8,128)(2,1)S(1)}, bf16[2,1024,512]{2,1,0:T(8,128)(2,1)S(1)}) fusion(f32[2,1024]{1,0:T(2,128)S(1)} %get-tuple-element.14, f32[1024,512]{1,0:T(8,128)S(1)} %multiply_add_fusion, f32[2]{0:T(128)S(1)} %add_multiply_fusion, f32[2,1024]{1,0:T(2,128)S(1)} %get-tuple-element.15), kind=kLoop, calls=%fused_computation.73 | loop fusion | flops 9437184 | bytes 6307848 | tf_op jit(solution)/shard_map/neg | solution.py:54
  46.6 3.9 %maximum_bitcast_fusion = (bf16[2,1,1024,1024]{3,2,1,0:T(8,128)(2,1)}, bf16[2,1,1024,1024]{3,2,1,0:T(8,128)(2,1)}) fusion(bf16[2,1024,512]{2,1,0:T(8,128)(2,1)S(1)} %get-tuple-element.9, bf16[2,1024,512]{2,1,0:T(8,128)(2,1)S(1)} %fusion.10, bf16[2,1024,512]{2,1,0:T(8,128)(2,1)S(1)} %get-tuple-element.8), kind=kLoop, calls=%fused_computation.21 | loop fusion | flops 16777216 | bytes 14680064 | tf_op jit(solution)/shard_map/stack | solution.py:55
  50.5 7.6 %all-to-all-done = bf16[2,256,1,8,256]{4,1,2,0,3:T(8,128)(2,1)S(1)} async-done(((bf16[2,256,1,8,256]{4,1,2,0,3:T(8,128)(2,1)}), bf16[2,256,1,8,256]{4,1,2,0,3:T(8,128)(2,1)S(1)}, u32[]{:S(2)}, u32[]{:S(2)}) %all-to-all-start) | async-done | bytes 2097184 | tf_op jit(solution)/shard_map/all_to_all | solution.py:77
  58.1 1.5 %copy.30 = bf16[2,256,1,8,256]{4,1,3,0,2:T(8,128)(2,1)} copy(bf16[2,256,1,8,256]{4,1,2,0,3:T(8,128)(2,1)S(1)} %all-to-all-done) | data formatting | bytes 4194304 | tf_op jit(solution)/shard_map/all_to_all | solution.py:77
  59.6 3.1 %copy.31 = bf16[2,4,256,1,2,256]{2,1,5,0,4,3:T(4,128)(2,1)S(1)} copy(bf16[2,4,256,1,2,256]{5,2,4,1,0,3:T(8,128)(2,1)} %bitcast.73) | data formatting | bytes 4194304 | tf_op jit(solution)/shard_map/all_to_all | solution.py:77
  62.7 2.7 %reshape.148 = bf16[2,1024,2,256]{1,3,0,2:T(8,128)(2,1)} reshape(bf16[2,4,256,1,2,256]{2,1,5,0,4,3:T(4,128)(2,1)S(1)} %copy.31) | data formatting | bytes 4194304 | tf_op jit(solution)/shard_map/reshape | solution.py:78
  65.4 5.4 %fusion.14 = f32[2,256,1024]{2,1,0:T(8,128)S(1)} fusion(bf16[2,1024,2,256]{1,3,0,2:T(8,128)(2,1)} %reshape.148, bf16[2,1,1024,1024]{3,2,1,0:T(8,128)(2,1)} %get-tuple-element.11, bf16[2,1,1024,1024]{3,2,1,0:T(8,128)(2,1)} %get-tuple-element.10), kind=kOutput, calls=%fused_computation.24 | convolution fusion | flops 2164260864 | bytes 12582912 | tf_op jit(solution)/shard_map/pacn,cpaq->cnq/dot_general | solution.py:79
  70.9 0.5 fusion.19
  71.6 1.1 %gather_fusion.1 = f32[2,32,512]{2,0,1:T(2,128)S(1)} fusion(f32[2,64,512]{2,0,1:T(2,128)S(1)} %pad_maximum_fusion, s32[2]{0:T(128)S(1)} %fusion.29), kind=kCustom, calls=%fused_computation.1 | custom fusion | bytes 262168 | tf_op jit(solution)/shard_map/vmap()/gather | solution.py:22
  73.0 4.8 %collective-permute-done = f32[2,32,512]{2,0,1:T(2,128)S(1)} collective-permute-done((f32[2,32,512]{2,0,1:T(2,128)S(1)}, f32[2,32,512]{2,0,1:T(2,128)S(1)}, u32[]{:S(2)}, u32[]{:S(2)}) %collective-permute-start) | collective-permute-done | bytes 131104 | tf_op jit(solution)/shard_map/ppermute | solution.py:14
  78.0 1.1 %gather_fusion.2 = f32[2,32,512]{2,0,1:T(2,128)S(1)} fusion(f32[2,64,512]{2,0,1:T(2,128)S(1)} %pad_maximum_fusion.1, s32[2]{0:T(128)S(1)} %fusion.28), kind=kCustom, calls=%fused_computation.2 | custom fusion | bytes 262168 | tf_op jit(solution)/shard_map/vmap()/gather | solution.py:22
  79.5 6.5 %collective-permute-done.1 = f32[2,32,512]{2,0,1:T(2,128)S(1)} collective-permute-done((f32[2,32,512]{2,0,1:T(2,128)S(1)}, f32[2,32,512]{2,0,1:T(2,128)S(1)}, u32[]{:S(2)}, u32[]{:S(2)}) %collective-permute-start.1) | collective-permute-done | bytes 131104 | tf_op jit(solution)/shard_map/ppermute | solution.py:14
  86.1 1.1 %gather_fusion.3 = f32[2,32,512]{2,0,1:T(2,128)S(1)} fusion(f32[2,64,512]{2,0,1:T(2,128)S(1)} %pad_maximum_fusion.2, s32[2]{0:T(128)S(1)} %fusion.27), kind=kCustom, calls=%fused_computation.3 | custom fusion | bytes 262168 | tf_op jit(solution)/shard_map/vmap()/gather | solution.py:22
  87.2 1.6 %collective-permute-start.2 = (f32[2,32,512]{2,0,1:T(2,128)S(1)}, f32[2,32,512]{2,0,1:T(2,128)S(1)}, u32[]{:S(2)}, u32[]{:S(2)}) collective-permute-start(f32[2,32,512]{2,0,1:T(2,128)S(1)} %bitcast.75), channel_id=1, source_target_pairs={{0,2},{2,0},{1,3},{3,1},{4,6},{6,4},{5,7},{7,5},{8,10},{10,8},{9,1... | collective-permute-start | bytes 393224 | tf_op jit(solution)/shard_map/ppermute | solution.py:14
  88.9 3.3 %collective-permute-done.2 = f32[2,32,512]{2,0,1:T(2,128)S(1)} collective-permute-done((f32[2,32,512]{2,0,1:T(2,128)S(1)}, f32[2,32,512]{2,0,1:T(2,128)S(1)}, u32[]{:S(2)}, u32[]{:S(2)}) %collective-permute-start.2) | collective-permute-done | bytes 131104 | tf_op jit(solution)/shard_map/ppermute | solution.py:14
  92.4 1.1 %gather_fusion.4 = f32[2,32,512]{2,0,1:T(2,128)S(1)} fusion(f32[2,64,512]{2,0,1:T(2,128)S(1)} %pad_maximum_fusion.3, s32[2]{0:T(128)S(1)} %fusion.26), kind=kCustom, calls=%fused_computation.4 | custom fusion | bytes 262168 | tf_op jit(solution)/shard_map/vmap()/gather | solution.py:22
  93.5 0.7 copy.32
  (43 shorter events, 1.8 us)
Async XLA Ops:
  0.0 9.9 %copy-start = (f32[3,1024]{1,0:T(4,128)S(1)}, f32[3,1024]{1,0:T(4,128)}, u32[]{:S(2)}) copy-start(f32[3,1024]{1,0:T(4,128)} %param.9) | copy-start | bytes 36868
  0.0 10.2 %copy-start.3 = (s32[4,2,8]{2,1,0:T(2,128)S(1)}, s32[4,2,8]{2,1,0:T(2,128)}, u32[]{:S(2)}) copy-start(s32[4,2,8]{2,1,0:T(2,128)} %param.13) | copy-start | bytes 772
  0.0 10.3 %copy-start.4 = (s32[1024]{0:T(1024)S(1)}, s32[1024]{0:T(1024)}, u32[]{:S(2)}) copy-start(s32[1024]{0:T(1024)} %param.11) | copy-start | bytes 12292
  0.0 13.1 %copy-start.5 = (s32[16]{0:T(128)S(1)}, s32[16]{0:T(128)}, u32[]{:S(2)}) copy-start(s32[16]{0:T(128)} %param.12) | copy-start | bytes 196
  3.5 10.6 %copy-start.2 = (f32[3,512]{1,0:T(4,128)S(1)}, f32[3,512]{1,0:T(4,128)}, u32[]{:S(2)}) copy-start(f32[3,512]{1,0:T(4,128)} %param.10) | copy-start | bytes 18436
  3.5 10.6 %copy-start.1 = (f32[2,1,2,1024]{3,2,1,0:T(2,128)S(1)}, f32[2,1,2,1024]{3,2,1,0:T(2,128)}, u32[]{:S(2)}) copy-start(f32[2,1,2,1024]{3,2,1,0:T(2,128)} %param.8) | copy-start | bytes 49156
  3.5 54.6 %all-to-all-start = ((bf16[2,256,1,8,256]{4,1,2,0,3:T(8,128)(2,1)}), bf16[2,256,1,8,256]{4,1,2,0,3:T(8,128)(2,1)S(1)}, u32[]{:S(2)}, u32[]{:S(2)}) async-start(bf16[2,256,1,8,256]{4,1,2,0,3:T(8,128)(2,1)} %copy.29), calls=%async_computation | async-start | bytes 4194304 | tf_op jit(solution)/shard_map/all_to_all | solution.py:77
  72.8 5.0 %collective-permute-start = (f32[2,32,512]{2,0,1:T(2,128)S(1)}, f32[2,32,512]{2,0,1:T(2,128)S(1)}, u32[]{:S(2)}, u32[]{:S(2)}) collective-permute-start(f32[2,32,512]{2,0,1:T(2,128)S(1)} %broadcast_add_fusion), channel_id=1, source_target_pairs={{0,4},{4,0},{8,12},{12,8},{1,5},{5,1},{9,13},{13,9},{2,6},{6,2},{1... | collective-permute-start | bytes 393224 | tf_op jit(solution)/shard_map/ppermute | solution.py:14
  79.2 6.8 %collective-permute-start.1 = (f32[2,32,512]{2,0,1:T(2,128)S(1)}, f32[2,32,512]{2,0,1:T(2,128)S(1)}, u32[]{:S(2)}, u32[]{:S(2)}) collective-permute-start(f32[2,32,512]{2,0,1:T(2,128)S(1)} %select_add_fusion.1), channel_id=1, source_target_pairs={{0,8},{4,12},{8,0},{12,4},{1,9},{5,13},{9,1},{13,5},{2,10},{6,14},... | collective-permute-start | bytes 393224 | tf_op jit(solution)/shard_map/ppermute | solution.py:14
  87.2 5.0 %collective-permute-start.2 = (f32[2,32,512]{2,0,1:T(2,128)S(1)}, f32[2,32,512]{2,0,1:T(2,128)S(1)}, u32[]{:S(2)}, u32[]{:S(2)}) collective-permute-start(f32[2,32,512]{2,0,1:T(2,128)S(1)} %bitcast.75), channel_id=1, source_target_pairs={{0,2},{2,0},{1,3},{3,1},{4,6},{6,4},{5,7},{7,5},{8,10},{10,8},{9,1... | collective-permute-start | bytes 393224 | tf_op jit(solution)/shard_map/ppermute | solution.py:14
where the time goes:
time: 94.5 us; the launch traced here: 94.2 us
  other arithmetic  38.1 us (40%)
  waiting for transfers between devices  22.3 us (24%)
  local copies, waits for them, and re-layouts  20 us (21%)
  starting transfers between devices  8.15 us (9%)
  matrix products  5.44 us (6%)
    neg x1, other arithmetic, beam_weights(): lower_rows = jnp.concatenate([-w_im, w_re], axis=2)  16.1 us
    convert_element_type x1, other arithmetic, beam_weights(): w_re = ((g_re * cosine + g_im * sine) * factor).astype(jnp.bfloat16)  15.9 us
    ppermute x3, waiting for transfers between devices, partner_2(): return lax.ppermute(value, axis, pairs)  14.6 us
    all_to_all x1, waiting for transfers between devices, shards(): lax.all_to_all(voltages, 'chan', split_axis=3, concat_axis=1, tiled=True)  7.65 us
    all_to_all x1, starting transfers between devices, shards(): lax.all_to_all(voltages, 'chan', split_axis=3, concat_axis=1, tiled=True)  6.45 us
    dot_general x1, matrix products, shards(): jnp.einsum('pacn,cpaq->cnq', flat, weights, preferred_element_type=jnp.fl...  5.44 us
    all_to_all x2, local copies, waits for them, and re-layouts, shards(): lax.all_to_all(voltages, 'chan', split_axis=3, concat_axis=1, tiled=True)  4.56 us
    gather x4, local copies, waits for them, and re-layouts, one_row(): return lax.dynamic_slice_in_dim(row, length - shift, length, 0)  4.3 us
  transfers between devices with their start and end apart: 4, of which 4 were waited for; matrix products, arithmetic and copies ran while one was open for 43% of the time, Pallas kernels for 0%

commit v1 on v0

v1 whole, which is shorter than its diff:
```python
import math

import jax
import jax.numpy as jnp
from jax import lax
from jax.experimental import pallas as pl
from jax.experimental.pallas import tpu as pltpu
from jax.sharding import PartitionSpec as P

INTEG = 8
VMEM = pl.BlockSpec(memory_space=pltpu.VMEM)
SMEM = pl.BlockSpec(memory_space=pltpu.SMEM)
PARAMS = pltpu.CompilerParams(vmem_limit_bytes=40 * 1024 * 1024)
SIN = (6.283184915580925, -41.34158901325128, 81.59993513909575, -76.61436771142901, 41.342343389037076, -12.470285565721209)
COS = (0.9999992089426497, -19.738979914331107, 64.92864094416844, -85.27141067260794, 58.789407905427666, -21.069178520245686)
ROUNDER = 1.5 * 2.0**23
PHASE_ROWS = 32


def partner(value, axis, mask):
    pairs = [(source, source ^ mask) for source in range(lax.axis_size(axis))]
    return lax.ppermute(value, axis, pairs)


def split_channels(voltages, masks):
    parts, ants, _, chans, samples = voltages.shape
    per_dev = lax.axis_size("beam")

    def kernel(v_ref, *refs):
        outs, wide = refs[: len(masks)], refs[len(masks) :]
        for lane, half in enumerate(wide):
            half[...] = v_ref[0, :, pl.ds(lane * 128, 128)].astype(jnp.float32)
        z = lax.axis_index("chan")
        e = lax.axis_index("beam")
        for mask, out in zip(masks, outs):
            chan = (z ^ mask) * per_dev + e
            for lane, half in enumerate(wide):
                out[0, :, pl.ds(lane * 128, 128)] = half[pl.ds(chan, ants, stride=chans), :].astype(jnp.bfloat16)

    return pl.pallas_call(
        kernel,
        grid=(parts,),
        in_specs=[pl.BlockSpec((1, ants * chans, samples), lambda p: (p, 0, 0))],
        out_specs=[pl.BlockSpec((1, ants, samples), lambda p: (p, 0, 0))] * len(masks),
        out_shape=[jax.ShapeDtypeStruct((parts, ants, samples), jnp.bfloat16)] * len(masks),
        scratch_shapes=[pltpu.VMEM((ants * chans, 128), jnp.float32)] * (samples // 128),
        compiler_params=PARAMS,
        name="split_channels",
    )(voltages.reshape(parts, ants * chans, samples))


def horner(coefs, u):
    total = coefs[-1] * u + coefs[-2]
    for coef in coefs[-3::-1]:
        total = total * u + coef
    return total


def bf16_parts(x):
    first = x.astype(jnp.bfloat16).astype(jnp.float32)
    rest = x - first
    second = rest.astype(jnp.bfloat16).astype(jnp.float32)
    return first, second, rest - second


def make_weights(pos, gain, dirs, chan_order, total, in_band):
    ants, beams = pos.shape[1], dirs.shape[1]
    per_dev = lax.axis_size("beam")
    block = min(beams, 128)
    lanes = min(ants, 512)

    def kernel(order_ref, pos_ref, gain_ref, dir_ref, out, left, right, size, turns):
        @pl.when(pl.program_id(0) == 0)
        def _():
            slot = lax.axis_index("band") * in_band + lax.axis_index("chan") * per_dev + lax.axis_index("beam")
            freq = 1.0 + order_ref[slot].astype(jnp.float32) * (1.0 / total)
            g_re, g_im = gain_ref[0:1, :], gain_ref[1:2, :]
            top = jnp.maximum(jnp.abs(g_re), jnp.abs(g_im))
            low = jnp.minimum(jnp.abs(g_re), jnp.abs(g_im))
            ratio = low / jnp.where(top > 0.0, top, 1.0)
            size[...] = top * jnp.sqrt(1.0 + ratio * ratio) * (1.0 / math.sqrt(ants))
            right[...] = jnp.zeros_like(right)
            left[...] = jnp.zeros_like(left)
            pos_parts = bf16_parts(pos_ref[...] * -freq)
            dir_parts = bf16_parts(dir_ref[...])
            row = 0
            for pos_part in pos_parts:
                for dir_part in dir_parts:
                    right[row : row + 3, :] = pos_part
                    left[row : row + 3, :] = dir_part
                    row += 3
            for part in bf16_parts(jnp.arctan2(g_im, g_re) * (0.5 / math.pi)):
                right[row : row + 1, :] = part
                left[row : row + 1, :] = jnp.ones((1, beams), jnp.float32)
                row += 1

        start = pl.multiple_of(pl.program_id(0) * block, block)
        turns[...] = lax.dot_general(
            left[:, pl.ds(start, block)].astype(jnp.bfloat16),
            right[...].astype(jnp.bfloat16),
            (((0,), (0,)), ((), ())),
            preferred_element_type=jnp.float32,
        )

        def rows(step, carry):
            at = pl.ds(pl.multiple_of(step * 16, 16), 16)
            for lane in range(0, ants, lanes):
                cols = pl.ds(lane, lanes)
                x = turns[at, cols]
                t = x - ((x + ROUNDER) - ROUNDER)
                u = t * t
                scale = size[:, cols]
                out[0, at, cols] = (horner(COS, u) * scale).astype(jnp.bfloat16)
                out[1, at, cols] = (horner(SIN, u) * (t * scale)).astype(jnp.bfloat16)
            return carry

        lax.fori_loop(0, block // 16, rows, 0)

    return pl.pallas_call(
        kernel,
        grid=(beams // block,),
        in_specs=[
            SMEM,
            pl.BlockSpec((3, ants), lambda i: (0, 0)),
            pl.BlockSpec((2, ants), lambda i: (0, 0)),
            pl.BlockSpec((3, beams), lambda i: (0, 0)),
        ],
        out_specs=pl.BlockSpec((2, block, ants), lambda i: (0, i, 0)),
        out_shape=jax.ShapeDtypeStruct((2, beams, ants), jnp.bfloat16),
        scratch_shapes=[
            pltpu.VMEM((PHASE_ROWS, beams), jnp.float32),
            pltpu.VMEM((PHASE_ROWS, ants), jnp.float32),
            pltpu.VMEM((1, ants), jnp.float32),
            pltpu.VMEM((block, ants), jnp.float32),
        ],
        compiler_params=PARAMS,
        name="make_weights",
    )(chan_order, pos, gain, dirs)


def chunk_product(w_ref, chunks, first, beam_rows):
    re = jnp.concatenate([chunk[0] for chunk in chunks], axis=0)
    im = jnp.concatenate([chunk[1] for chunk in chunks], axis=0)
    straight = jnp.concatenate([re, im], axis=1)
    turned = jnp.concatenate([-im, re], axis=1)
    cols = pl.ds(first, re.shape[0])
    dot = lambda a, b: jnp.dot(a, b, preferred_element_type=jnp.float32)
    return dot(w_ref[0, beam_rows, cols], straight) + dot(w_ref[1, beam_rows, cols], turned)


def early_beams(weights, chunks):
    beams = weights.shape[1]
    samples = chunks[0].shape[2]
    step = min(beams, 256)

    def kernel(w_ref, *refs):
        for row in range(0, beams, step):
            rows = pl.ds(row, step)
            refs[-1][rows, :] = chunk_product(w_ref, refs[:-1], 0, rows)

    return pl.pallas_call(
        kernel,
        in_specs=[VMEM] * (1 + len(chunks)),
        out_specs=VMEM,
        out_shape=jax.ShapeDtypeStruct((beams, 2 * samples), jnp.float32),
        compiler_params=PARAMS,
        name="early_beams",
    )(weights, *chunks)


def last_levels(weights, chunks, first, partial, total):
    beams = weights.shape[1]
    samples = chunks[0].shape[2]
    bins = samples // INTEG
    step = min(beams // 2, 256)

    def kernel(w_ref, part_ref, *refs):
        ours, theirs = refs[-2:]
        bin_no = lax.broadcasted_iota(jnp.int32, (bins, samples), 0)
        time = lax.broadcasted_iota(jnp.int32, (bins, samples), 1)
        centre = jnp.where(time // INTEG == bin_no, 1.0 / INTEG, 0.0) - 1.0 / samples
        centre = centre.astype(jnp.bfloat16)
        for row in range(0, beams, step):
            rows = pl.ds(row, step)
            beam = part_ref[rows, :] + chunk_product(w_ref, refs[:-2], first, rows)
            re, im = beam[:, :samples], beam[:, samples:]
            power = re * re + im * im
            high = power.astype(jnp.bfloat16)
            low = (power - high.astype(jnp.float32)).astype(jnp.bfloat16)
            dot = lambda b: lax.dot_general(centre, b, (((1,), (1,)), ((), ())), preferred_element_type=jnp.float32)
            level = (dot(high) + dot(low)) * (1.0 / math.sqrt(total))
            if row < beams // 2:
                ours[:, pl.ds(row, step)] = level
            else:
                theirs[:, pl.ds(row - beams // 2, step)] = level

    return pl.pallas_call(
        kernel,
        in_specs=[VMEM] * (2 + len(chunks)),
        out_specs=[VMEM, VMEM],
        out_shape=[jax.ShapeDtypeStruct((bins, beams // 2), jnp.float32)] * 2,
        compiler_params=PARAMS,
        name="last_levels",
    )(weights, partial, *chunks)


def pick(cond, a, b):
    return jnp.where(cond, a, b), jnp.where(cond, b, a)


def tree_call(kernel, delays, arrays, shape, final, name):
    outs = [jax.ShapeDtypeStruct(shape, jnp.float32)]
    if not final:
        outs.append(jax.ShapeDtypeStruct(shape, jnp.bfloat16))
    return pl.pallas_call(
        kernel,
        in_specs=[SMEM] + [VMEM] * len(arrays),
        out_specs=[VMEM] * len(outs),
        out_shape=outs,
        compiler_params=PARAMS,
        name=name,
    )(delays, *arrays)


def store(outs, slot, value):
    for out in outs:
        out[slot] = value.astype(out.dtype)


def core_round(own, other, delays, in_band):
    per_dev = lax.axis_size("beam")

    def kernel(delay_ref, own_ref, other_ref, *outs):
        base = lax.axis_index("band") * in_band + lax.axis_index("chan") * per_dev
        lower, upper = pick(lax.axis_index("beam") == 0, own_ref[...], other_ref[...])
        for slot in range(per_dev):
            store(outs, slot, lower + pltpu.roll(upper, delay_ref[0, base + slot], 0))

    return tree_call(kernel, delays, [own, other], (per_dev,) + own.shape, False, "core_round")


def axis_rounds(own, sent, axis, bits, level_no, delays, in_band, final):
    per_dev = own.shape[0]
    masks = [1 << bits[0]]
    if len(bits) == 2:
        masks += [2 << bits[0], 3 << bits[0]]
    others = [partner(sent, axis, mask) for mask in masks]

    def kernel(delay_ref, *refs):
        states, outs = refs[: 1 + len(masks)], refs[1 + len(masks) :]
        here = lax.axis_index(axis)
        first_bit = (here >> bits[0]) & 1 == 0
        second_bit = (here >> (bits[0] + 1)) & 1 == 0

        def base(index):
            if axis == "chan":
                return lax.axis_index("band") * in_band + index * per_dev
            return index * in_band + lax.axis_index("chan") * per_dev

        def one_round(a, b, cond, round_no, slot):
            lower, upper = pick(cond, a, b)
            return lower + pltpu.roll(upper, delay_ref[round_no, slot], 0)

        for slot in range(per_dev):
            load = lambda m: states[m][slot].astype(jnp.float32)
            value = one_round(load(0), load(1), first_bit, level_no, base(here) + slot)
            if len(bits) == 2:
                far = base(here ^ masks[1]) + slot
                other = one_round(load(2), load(3), first_bit, level_no, far)
                value = one_round(value, other, second_bit, level_no + 1, base(here) + slot)
            store(outs, slot, value)

    return tree_call(kernel, delays, [own] + others, own.shape, final, "rounds_" + axis)


def shards(voltages, gains, positions, directions, antenna_row_lookup, chan_order, delays):
    chan_count = lax.axis_size("chan")
    band_count = lax.axis_size("band")
    per_dev = gains.shape[2]
    assert per_dev == lax.axis_size("beam") == 2
    in_band = per_dev * chan_count
    total = in_band * band_count
    ants = voltages.shape[1]
    chan_index = lax.axis_index("chan")
    beam_index = lax.axis_index("beam")

    masks = [0] + [m for m in range(1, chan_count) if m != chan_count // 2] + [chan_count // 2]
    blocks = split_channels(voltages, masks)
    far = {m: partner(blocks[masks.index(m)], "chan", m) for m in reversed(masks[1:])}
    chunks = [blocks[0]] + [far[m] for m in masks[1:]]

    order = chan_index ^ jnp.array(masks, jnp.int32)
    rows = antenna_row_lookup.reshape(chan_count, ants)[order].reshape(-1)
    gain = lax.dynamic_index_in_dim(gains[:, 0], beam_index, 1, keepdims=False)
    gain = gain.reshape(2, chan_count, ants)[:, order].reshape(2, -1)
    dirs = jnp.concatenate([directions, partner(directions, "beam", 1)], axis=1)
    weights = make_weights(positions[:, rows], gain, dirs, chan_order, total, in_band)

    partial = early_beams(weights, chunks[:-1])
    ours, theirs = last_levels(weights, chunks[-1:], ants * (chan_count - 1), partial, total)

    flat_delays = delays.reshape(delays.shape[0], total)
    state, sent = core_round(ours, partner(theirs, "beam", 1), flat_delays, in_band)
    level_no = 1
    steps = []
    for axis, count in (("chan", chan_count), ("band", band_count)):
        bits = list(range(count.bit_length() - 1))
        steps += [(axis, bits[i : i + 2]) for i in range(0, len(bits), 2)]
    for number, (axis, bits) in enumerate(steps):
        final = number == len(steps) - 1
        result = axis_rounds(state, sent, axis, bits, level_no, flat_delays, in_band, final)
        if final:
            state = result[0]
        else:
            state, sent = result
        level_no += len(bits)
    return state.reshape(1, per_dev, state.shape[1], state.shape[2])


def solution(mesh):
    placed = (
        P(None, "chan", "band", None, "group"),
        P(None, "band", "chan", None),
        P(),
        P(None, ("group", "beam")),
        P(),
        P(),
        P(),
    )
    return jax.shard_map(
        shards,
        mesh=mesh,
        in_specs=placed,
        out_specs=P("band", "chan", None, ("group", "beam")),
        check_vma=False,
    )
```

time: 94.5 us -> 51 us (0.54)
  other arithmetic: 38.1 us -> 0.04 us
  Pallas kernels: 0 us -> 14 us
  local copies, waits for them, and re-layouts: 20 us -> 6.11 us
  matrix products: 5.44 us -> 0 us
  starting transfers between devices: 8.15 us -> 11.8 us
  waiting for transfers between devices: 22.3 us -> 18.7 us
    neg x1 -> x0, other arithmetic: 16.1 us -> none  [beam_weights(): lower_rows = jnp.concatenate([-w_im, w_re], axis=2)]
    convert_element_type x1 -> x0, other arithmetic: 15.9 us -> none  [beam_weights(): w_re = ((g_re * cosine + g_im * sine) * factor).astype(jnp.bfloat16)]
    pallas_call x0 -> x7, Pallas kernels: none -> 14 us  [the longest x1 7.38 us: make_weights(): pl.pallas_call(kernel, grid=(beams // block,), in_specs=[SMEM, pl.BlockSp...]
    ppermute x3 -> x9, starting transfers between devices: 1.7 us -> 11.8 us  [partner(): return lax.ppermute(value, axis, pairs)]
    all_to_all x1 -> x0, waiting for transfers between devices: 7.65 us -> none  [shards(): lax.all_to_all(voltages, 'chan', split_axis=3, concat_axis=1, tiled=True)]
    all_to_all x1 -> x0, starting transfers between devices: 6.45 us -> none  [shards(): lax.all_to_all(voltages, 'chan', split_axis=3, concat_axis=1, tiled=True)]
    dot_general x1 -> x0, matrix products: 5.44 us -> none  [shards(): jnp.einsum('pacn,cpaq->cnq', flat, weights, preferred_element_type=jnp.fl...]
    all_to_all x2 -> x0, local copies, waits for them, and re-layouts: 4.56 us -> none  [shards(): lax.all_to_all(voltages, 'chan', split_axis=3, concat_axis=1, tiled=True)]
  transfers between devices with their start and end apart: 4 -> 9, of which waited for: 4 -> 7; matrix products, arithmetic and copies ran while one was open for 43% -> 9% of each run, Pallas kernels for 0% -> 20%
where the time goes in v1:
time: 51 us; the launch traced here: 50.8 us
  waiting for transfers between devices  18.7 us (37%)
  Pallas kernels  14 us (27%)
  starting transfers between devices  11.8 us (23%)
  local copies, waits for them, and re-layouts  6.11 us (12%)
    ppermute x9, waiting for transfers between devices, partner(): return lax.ppermute(value, axis, pairs)  18.7 us
    ppermute x9, starting transfers between devices, partner(): return lax.ppermute(value, axis, pairs)  11.8 us
    pallas_call x1, Pallas kernels, make_weights(): pl.pallas_call(kernel, grid=(beams // block,), in_specs=[SMEM, pl.BlockSp...  7.38 us
    gather x2, local copies, waits for them, and re-layouts, shards(): positions[:, rows]  3 us
    pallas_call x3, Pallas kernels, tree_call(): pl.pallas_call(kernel, in_specs=[SMEM] + [VMEM] * len(arrays), out_specs=...  2.59 us
    unnamed x18, local copies, waits for them, and re-layouts  1.85 us
    pallas_call x1, Pallas kernels, early_beams(): pl.pallas_call(kernel, in_specs=[VMEM] * (1 + len(chunks)), out_specs=VME...  1.78 us
    pallas_call x1, Pallas kernels, last_levels(): pl.pallas_call(kernel, in_specs=[VMEM] * (2 + len(chunks)), out_specs=[VM...  1.46 us
  transfers between devices with their start and end apart: 9, of which 7 were waited for; matrix products, arithmetic and copies ran while one was open for 9% of the time, Pallas kernels for 20%

profile of v1, /device:TPU:0, one launch (start us, length us, event | category | flops | bytes accessed | tf_op | source)
XLA Modules:
  0.0 50.8 jit_solution(8700588659976651681)
XLA Ops:
  0.0 0.5 %collective-permute-start = (f32[3,512]{1,0:T(4,128)}, f32[3,512]{1,0:T(4,128)S(1)}, u32[]{:S(2)}, u32[]{:S(2)}) collective-permute-start(f32[3,512]{1,0:T(4,128)} %param.11), channel_id=1, source_target_pairs={{0,1},{1,0},{2,3},{3,2},{4,5},{5,4},{6,7},{7,6},{8,9},{9,8},{10,11... | collective-permute-start | bytes 18440 | tf_op jit(solution)/shard_map/ppermute | solution.py:22
  0.5 1.6 %copy-done.1 = bf16[2,256,1,8,256]{4,3,2,1,0:T(8,128)(2,1)S(1)} copy-done((bf16[2,256,1,8,256]{4,3,2,1,0:T(8,128)(2,1)S(1)}, bf16[2,256,1,8,256]{4,3,2,1,0:T(8,128)(2,1)}, u32[]{:S(2)}) %copy-start.1) | copy-done | bytes 2097176
  2.1 0.8 %split_channels.1 = (bf16[2,256,256]{2,1,0:T(8,128)(2,1)S(1)}, bf16[2,256,256]{2,1,0:T(8,128)(2,1)S(1)}, bf16[2,256,256]{2,1,0:T(8,128)(2,1)S(1)}, bf16[2,256,256]{2,1,0:T(8,128)(2,1)S(1)}) custom-call(bf16[2,2048,256]{2,1,0:T(8,128)(2,1)S(1)} %bitcast.12), custom_call_target="tpu_custom_call" | custom-call | tf_op jit(solution)/shard_map/split_channels/pallas_call | solution.py:40
  2.9 2.6 %collective-permute-start.1 = (bf16[2,256,256]{2,1,0:T(8,128)(2,1)S(1)}, bf16[2,256,256]{2,1,0:T(8,128)(2,1)S(1)}, u32[]{:S(2)}, u32[]{:S(2)}) collective-permute-start(bf16[2,256,256]{2,1,0:T(8,128)(2,1)S(1)} %get-tuple-element.16), channel_id=1, source_target_pairs={{0,4},{4,0},{8,12},{12,8},{1,5},{5,1},{9,13},{13,9},{2,6},{6,2},{1... | collective-permute-start | bytes 786440 | tf_op jit(solution)/shard_map/ppermute | solution.py:22
  5.6 2.5 %collective-permute-start.2 = (bf16[2,256,256]{2,1,0:T(8,128)(2,1)S(1)}, bf16[2,256,256]{2,1,0:T(8,128)(2,1)S(1)}, u32[]{:S(2)}, u32[]{:S(2)}) collective-permute-start(bf16[2,256,256]{2,1,0:T(8,128)(2,1)S(1)} %get-tuple-element.17), channel_id=1, source_target_pairs={{0,12},{4,8},{8,4},{12,0},{1,13},{5,9},{9,5},{13,1},{2,14},{6,10},... | collective-permute-start | bytes 786440 | tf_op jit(solution)/shard_map/ppermute | solution.py:22
  8.2 0.6 %gather_fusion = s32[4,256]{1,0:T(4,128)S(1)} fusion(s32[4,256]{1,0:T(4,128)S(1)} %reshape.53, s32[1024]{0:T(1024)S(1)} %pad_clamp_fusion), kind=kCustom, calls=%fused_computation | custom fusion | bytes 8208 | tf_op jit(solution)/shard_map/gather | solution.py:293
  8.9 0.6 %gather_fusion.2 = f32[4,2,256]{2,1,0:T(2,128)S(1)} fusion(f32[2,4,256]{2,0,1:T(2,128)S(1)} %bitcast.15, s32[1024]{0:T(1024)S(1)} %pad_clamp_fusion), kind=kCustom, calls=%fused_computation.2 | custom fusion | bytes 16400 | tf_op jit(solution)/shard_map/gather | solution.py:295
  9.7 2.8 %gather_fusion.1 = f32[1024,3]{1,0:T(8,128)S(1)} fusion(f32[3,1024]{0,1:T(8,128)S(1)} %copy.11, s32[1024]{0:T(1024)S(1)} %broadcast_clamp_fusion), kind=kCustom, calls=%fused_computation.1 | custom fusion | bytes 28672 | tf_op jit(solution)/shard_map/gather | solution.py:297
  12.7 7.4 %make_weights.1.w_ref = bf16[2,1024,1024]{2,1,0:T(8,128)(2,1)S(1)} custom-call(s32[16]{0:T(128)S(1)} %copy-done.2, f32[3,1024]{1,0:T(4,128)S(1)} %bitcast.13, f32[2,1024]{1,0:T(2,128)S(1)} %bitcast.14, f32[3,1024]{1,0:T(4,128)S(1)} %pad_maximum_fusion.dir_ref), custom_call_target="tpu_custom_call" | custom-call | tf_op jit(solution)/shard_map/make_weights/pallas_call | solution.py:119
  20.1 0.7 %collective-permute-done.2.refs_2_ = bf16[2,256,256]{2,1,0:T(8,128)(2,1)S(1)} collective-permute-done((bf16[2,256,256]{2,1,0:T(8,128)(2,1)S(1)}, bf16[2,256,256]{2,1,0:T(8,128)(2,1)S(1)}, u32[]{:S(2)}, u32[]{:S(2)}) %collective-permute-start.2) | collective-permute-done | bytes 262176 | tf_op jit(solution)/shard_map/ppermute | solution.py:22
  20.9 1.8 %early_beams.1.part_ref = f32[1024,512]{1,0:T(8,128)S(1)} custom-call(bf16[2,1024,1024]{2,1,0:T(8,128)(2,1)S(1)} %make_weights.1.w_ref, bf16[2,256,256]{2,1,0:T(8,128)(2,1)S(1)} %get-tuple-element.15.refs_0_, bf16[2,256,256]{2,1,0:T(8,128)(2,1)S(1)} %collective-permute-done.1.refs_1_, bf16[2,256,256]{2,1,0:T(8,128)(2,1)S(1)} %collective-permute-done.2.refs_2_), custom_call_target="tpu_custom_call" | custom-call | tf_op jit(solution)/shard_map/early_beams/pallas_call | solution.py:161
  22.7 9.1 %collective-permute-done.3.refs_0_ = bf16[2,256,256]{2,1,0:T(8,128)(2,1)S(1)} collective-permute-done((bf16[2,256,256]{2,1,0:T(8,128)(2,1)S(1)}, bf16[2,256,256]{2,1,0:T(8,128)(2,1)S(1)}, u32[]{:S(2)}, u32[]{:S(2)}) %collective-permute-start.3) | collective-permute-done | bytes 262176 | tf_op jit(solution)/shard_map/ppermute | solution.py:22
  31.7 1.5 %last_levels.1 = (f32[32,512]{1,0:T(8,128)S(1)}, f32[32,512]{1,0:T(8,128)S(1)}) custom-call(bf16[2,1024,1024]{2,1,0:T(8,128)(2,1)S(1)} %make_weights.1.w_ref, f32[1024,512]{1,0:T(8,128)S(1)} %early_beams.1.part_ref, bf16[2,256,256]{2,1,0:T(8,128)(2,1)S(1)} %collective-permute-done.3.refs_0_), custom_call_target="tpu_custom_call" | custom-call | tf_op jit(solution)/shard_map/last_levels/pallas_call | solution.py:197
  33.3 1.1 %collective-permute-done.4.other_ref = f32[32,512]{1,0:T(8,128)S(1)} collective-permute-done((f32[32,512]{1,0:T(8,128)S(1)}, f32[32,512]{1,0:T(8,128)S(1)}, u32[]{:S(2)}, u32[]{:S(2)}) %collective-permute-start.4) | collective-permute-done | bytes 65568 | tf_op jit(solution)/shard_map/ppermute | solution.py:22
  34.5 0.6 %core_round.1 = (f32[2,32,512]{2,1,0:T(8,128)S(1)}, bf16[2,32,512]{2,1,0:T(8,128)(2,1)S(1)}) custom-call(s32[4,16]{1,0:T(4,128)S(1)} %reshape.52.delay_ref, f32[32,512]{1,0:T(8,128)S(1)} %get-tuple-element.19.own_ref, f32[32,512]{1,0:T(8,128)S(1)} %collective-permute-done.4.other_ref), custom_call_target="tpu_custom_call" | custom-call | tf_op jit(solution)/shard_map/core_round/pallas_call | solution.py:215
  35.2 3.2 %collective-permute-start.6 = (bf16[2,32,512]{2,1,0:T(8,128)(2,1)S(1)}, bf16[2,32,512]{2,1,0:T(8,128)(2,1)S(1)}, u32[]{:S(2)}, u32[]{:S(2)}) collective-permute-start(bf16[2,32,512]{2,1,0:T(8,128)(2,1)S(1)} %get-tuple-element.22), channel_id=1, source_target_pairs={{0,8},{4,12},{8,0},{12,4},{1,9},{5,13},{9,1},{13,5},{2,10},{6,14},... | collective-permute-start | bytes 196616 | tf_op jit(solution)/shard_map/ppermute | solution.py:22
  38.4 1.2 %collective-permute-start.7 = (bf16[2,32,512]{2,1,0:T(8,128)(2,1)S(1)}, bf16[2,32,512]{2,1,0:T(8,128)(2,1)S(1)}, u32[]{:S(2)}, u32[]{:S(2)}) collective-permute-start(bf16[2,32,512]{2,1,0:T(8,128)(2,1)S(1)} %get-tuple-element.22), channel_id=1, source_target_pairs={{0,12},{4,8},{8,4},{12,0},{1,13},{5,9},{9,5},{13,1},{2,14},{6,10},... | collective-permute-start | bytes 196616 | tf_op jit(solution)/shard_map/ppermute | solution.py:22
  39.6 0.8 %collective-permute-done.5.refs_1_ = bf16[2,32,512]{2,1,0:T(8,128)(2,1)S(1)} collective-permute-done((bf16[2,32,512]{2,1,0:T(8,128)(2,1)S(1)}, bf16[2,32,512]{2,1,0:T(8,128)(2,1)S(1)}, u32[]{:S(2)}, u32[]{:S(2)}) %collective-permute-start.5) | collective-permute-done | bytes 65568 | tf_op jit(solution)/shard_map/ppermute | solution.py:22
  40.4 2.8 %collective-permute-done.6.refs_2_ = bf16[2,32,512]{2,1,0:T(8,128)(2,1)S(1)} collective-permute-done((bf16[2,32,512]{2,1,0:T(8,128)(2,1)S(1)}, bf16[2,32,512]{2,1,0:T(8,128)(2,1)S(1)}, u32[]{:S(2)}, u32[]{:S(2)}) %collective-permute-start.6) | collective-permute-done | bytes 65568 | tf_op jit(solution)/shard_map/ppermute | solution.py:22
  43.2 1.4 %collective-permute-done.7.refs_3_ = bf16[2,32,512]{2,1,0:T(8,128)(2,1)S(1)} collective-permute-done((bf16[2,32,512]{2,1,0:T(8,128)(2,1)S(1)}, bf16[2,32,512]{2,1,0:T(8,128)(2,1)S(1)}, u32[]{:S(2)}, u32[]{:S(2)}) %collective-permute-start.7) | collective-permute-done | bytes 65568 | tf_op jit(solution)/shard_map/ppermute | solution.py:22
  44.5 0.7 %rounds_chan.1 = (f32[2,32,512]{2,1,0:T(8,128)S(1)}, bf16[2,32,512]{2,1,0:T(8,128)(2,1)S(1)}) custom-call(s32[4,16]{1,0:T(4,128)S(1)} %reshape.52.delay_ref, f32[2,32,512]{2,1,0:T(8,128)S(1)} %get-tuple-element.21.refs_0_, bf16[2,32,512]{2,1,0:T(8,128)(2,1)S(1)} %collective-permute-done.5.refs_1_, bf16[2,32,512]{2,1,0:T(8,128)(2,1)S(1)} %collective-permute-done.6.refs_2_, ...), custom_call_target="tpu_custom_call" | custom-call | tf_op jit(solution)/shard_map/rounds_chan/pallas_call | solution.py:215
  45.2 1.6 %collective-permute-start.8 = (bf16[2,32,512]{2,1,0:T(8,128)(2,1)S(1)}, bf16[2,32,512]{2,1,0:T(8,128)(2,1)S(1)}, u32[]{:S(2)}, u32[]{:S(2)}) collective-permute-start(bf16[2,32,512]{2,1,0:T(8,128)(2,1)S(1)} %get-tuple-element.24), channel_id=1, source_target_pairs={{0,2},{2,0},{1,3},{3,1},{4,6},{6,4},{5,7},{7,5},{8,10},{10,8},{9,1... | collective-permute-start | bytes 196616 | tf_op jit(solution)/shard_map/ppermute | solution.py:22
  46.8 2.8 %collective-permute-done.8.refs_1_ = bf16[2,32,512]{2,1,0:T(8,128)(2,1)S(1)} collective-permute-done((bf16[2,32,512]{2,1,0:T(8,128)(2,1)S(1)}, bf16[2,32,512]{2,1,0:T(8,128)(2,1)S(1)}, u32[]{:S(2)}, u32[]{:S(2)}) %collective-permute-start.8) | collective-permute-done | bytes 65568 | tf_op jit(solution)/shard_map/ppermute | solution.py:22
  49.6 1.3 %rounds_band.1 = f32[2,32,512]{2,1,0:T(8,128)} custom-call(s32[4,16]{1,0:T(4,128)S(1)} %reshape.52.delay_ref, f32[2,32,512]{2,1,0:T(8,128)S(1)} %get-tuple-element.23.refs_0_, bf16[2,32,512]{2,1,0:T(8,128)(2,1)S(1)} %collective-permute-done.8.refs_1_), custom_call_target="tpu_custom_call" | custom-call | tf_op jit(solution)/shard_map/rounds_band/pallas_call | solution.py:215
  (31 shorter events, 0.9 us)
Async XLA Ops:
  0.0 8.8 %copy-start = (f32[2,1,2,1024]{3,2,1,0:T(2,128)S(1)}, f32[2,1,2,1024]{3,2,1,0:T(2,128)}, u32[]{:S(2)}) copy-start(f32[2,1,2,1024]{3,2,1,0:T(2,128)} %param.9) | copy-start | bytes 49156
  0.0 8.2 %copy-start.7 = (s32[4]{0:T(128)S(1)}, s32[4]{0:T(128)}, u32[]{:S(2)}) copy-start(s32[4]{0:T(128)} %constant.24.clone) | copy-start | bytes 52
  0.0 12.7 %copy-start.2 = (s32[16]{0:T(128)S(1)}, s32[16]{0:T(128)}, u32[]{:S(2)}) copy-start(s32[16]{0:T(128)} %order_ref.1) | copy-start | bytes 196
  0.0 12.7 %collective-permute-start = (f32[3,512]{1,0:T(4,128)}, f32[3,512]{1,0:T(4,128)S(1)}, u32[]{:S(2)}, u32[]{:S(2)}) collective-permute-start(f32[3,512]{1,0:T(4,128)} %param.11), channel_id=1, source_target_pairs={{0,1},{1,0},{2,3},{3,2},{4,5},{5,4},{6,7},{7,6},{8,9},{9,8},{10,11... | collective-permute-start | bytes 18440 | tf_op jit(solution)/shard_map/ppermute | solution.py:22
  0.5 1.6 %copy-start.1 = (bf16[2,256,1,8,256]{4,3,2,1,0:T(8,128)(2,1)S(1)}, bf16[2,256,1,8,256]{4,3,2,1,0:T(8,128)(2,1)}, u32[]{:S(2)}) copy-start(bf16[2,256,1,8,256]{4,3,2,1,0:T(8,128)(2,1)} %param.8) | copy-start | bytes 6291460
  2.1 6.1 %copy-start.6 = (s32[1024]{0:T(1024)S(1)}, s32[1024]{0:T(1024)}, u32[]{:S(2)}) copy-start(s32[1024]{0:T(1024)} %param.12) | copy-start | bytes 12292
  2.1 7.3 %copy-start.3 = (f32[3,1024]{1,0:T(4,128)S(1)}, f32[3,1024]{1,0:T(4,128)}, u32[]{:S(2)}) copy-start(f32[3,1024]{1,0:T(4,128)} %param.10) | copy-start | bytes 36868
  2.1 10.6 %copy-start.4 = (f32[3,512]{1,0:T(4,128)S(1)}, f32[3,512]{1,0:T(4,128)}, u32[]{:S(2)}) copy-start(f32[3,512]{1,0:T(4,128)} %param.11) | copy-start | bytes 18436
  2.9 17.2 %collective-permute-start.1 = (bf16[2,256,256]{2,1,0:T(8,128)(2,1)S(1)}, bf16[2,256,256]{2,1,0:T(8,128)(2,1)S(1)}, u32[]{:S(2)}, u32[]{:S(2)}) collective-permute-start(bf16[2,256,256]{2,1,0:T(8,128)(2,1)S(1)} %get-tuple-element.16), channel_id=1, source_target_pairs={{0,4},{4,0},{8,12},{12,8},{1,5},{5,1},{9,13},{13,9},{2,6},{6,2},{1... | collective-permute-start | bytes 786440 | tf_op jit(solution)/shard_map/ppermute | solution.py:22
  5.6 15.3 %collective-permute-start.2 = (bf16[2,256,256]{2,1,0:T(8,128)(2,1)S(1)}, bf16[2,256,256]{2,1,0:T(8,128)(2,1)S(1)}, u32[]{:S(2)}, u32[]{:S(2)}) collective-permute-start(bf16[2,256,256]{2,1,0:T(8,128)(2,1)S(1)} %get-tuple-element.17), channel_id=1, source_target_pairs={{0,12},{4,8},{8,4},{12,0},{1,13},{5,9},{9,5},{13,1},{2,14},{6,10},... | collective-permute-start | bytes 786440 | tf_op jit(solution)/shard_map/ppermute | solution.py:22
  8.1 23.7 %collective-permute-start.3 = (bf16[2,256,256]{2,1,0:T(8,128)(2,1)S(1)}, bf16[2,256,256]{2,1,0:T(8,128)(2,1)S(1)}, u32[]{:S(2)}, u32[]{:S(2)}) collective-permute-start(bf16[2,256,256]{2,1,0:T(8,128)(2,1)S(1)} %get-tuple-element.18), channel_id=1, source_target_pairs={{0,8},{4,12},{8,0},{12,4},{1,9},{5,13},{9,1},{13,5},{2,10},{6,14},... | collective-permute-start | bytes 786440 | tf_op jit(solution)/shard_map/ppermute | solution.py:22
  22.6 10.6 %copy-start.5 = (s32[4,2,8]{2,1,0:T(2,128)S(1)}, s32[4,2,8]{2,1,0:T(2,128)}, u32[]{:S(2)}) copy-start(s32[4,2,8]{2,1,0:T(2,128)} %param.14) | copy-start | bytes 772
  33.2 1.3 %collective-permute-start.4 = (f32[32,512]{1,0:T(8,128)S(1)}, f32[32,512]{1,0:T(8,128)S(1)}, u32[]{:S(2)}, u32[]{:S(2)}) collective-permute-start(f32[32,512]{1,0:T(8,128)S(1)} %get-tuple-element.20), channel_id=1, source_target_pairs={{0,1},{1,0},{2,3},{3,2},{4,5},{5,4},{6,7},{7,6},{8,9},{9,8},{10,11... | collective-permute-start | bytes 196616 | tf_op jit(solution)/shard_map/ppermute | solution.py:22
  35.1 5.3 %collective-permute-start.5 = (bf16[2,32,512]{2,1,0:T(8,128)(2,1)S(1)}, bf16[2,32,512]{2,1,0:T(8,128)(2,1)S(1)}, u32[]{:S(2)}, u32[]{:S(2)}) collective-permute-start(bf16[2,32,512]{2,1,0:T(8,128)(2,1)S(1)} %get-tuple-element.22), channel_id=1, source_target_pairs={{0,4},{4,0},{8,12},{12,8},{1,5},{5,1},{9,13},{13,9},{2,6},{6,2},{1... | collective-permute-start | bytes 196616 | tf_op jit(solution)/shard_map/ppermute | solution.py:22
  35.2 8.0 %collective-permute-start.6 = (bf16[2,32,512]{2,1,0:T(8,128)(2,1)S(1)}, bf16[2,32,512]{2,1,0:T(8,128)(2,1)S(1)}, u32[]{:S(2)}, u32[]{:S(2)}) collective-permute-start(bf16[2,32,512]{2,1,0:T(8,128)(2,1)S(1)} %get-tuple-element.22), channel_id=1, source_target_pairs={{0,8},{4,12},{8,0},{12,4},{1,9},{5,13},{9,1},{13,5},{2,10},{6,14},... | collective-permute-start | bytes 196616 | tf_op jit(solution)/shard_map/ppermute | solution.py:22
  38.4 6.2 %collective-permute-start.7 = (bf16[2,32,512]{2,1,0:T(8,128)(2,1)S(1)}, bf16[2,32,512]{2,1,0:T(8,128)(2,1)S(1)}, u32[]{:S(2)}, u32[]{:S(2)}) collective-permute-start(bf16[2,32,512]{2,1,0:T(8,128)(2,1)S(1)} %get-tuple-element.22), channel_id=1, source_target_pairs={{0,12},{4,8},{8,4},{12,0},{1,13},{5,9},{9,5},{13,1},{2,14},{6,10},... | collective-permute-start | bytes 196616 | tf_op jit(solution)/shard_map/ppermute | solution.py:22
  45.2 4.3 %collective-permute-start.8 = (bf16[2,32,512]{2,1,0:T(8,128)(2,1)S(1)}, bf16[2,32,512]{2,1,0:T(8,128)(2,1)S(1)}, u32[]{:S(2)}, u32[]{:S(2)}) collective-permute-start(bf16[2,32,512]{2,1,0:T(8,128)(2,1)S(1)} %get-tuple-element.24), channel_id=1, source_target_pairs={{0,2},{2,0},{1,3},{3,1},{4,6},{6,4},{5,7},{7,5},{8,10},{10,8},{9,1... | collective-permute-start | bytes 196616 | tf_op jit(solution)/shard_map/ppermute | solution.py:22

commit v2 on v1

--- a/solution.py
+++ b/solution.py
@@ -22,31 +22,59 @@
     return lax.ppermute(value, axis, pairs)
 
 
-def split_channels(voltages, masks):
+def split_channels(voltages, pieces, token=None):
     parts, ants, _, chans, samples = voltages.shape
     per_dev = lax.axis_size("beam")
-
-    def kernel(v_ref, *refs):
-        outs, wide = refs[: len(masks)], refs[len(masks) :]
-        for lane, half in enumerate(wide):
-            half[...] = v_ref[0, :, pl.ds(lane * 128, 128)].astype(jnp.float32)
+    start = min(first for _, first, _ in pieces)
+    stop = max(last for _, _, last in pieces)
+    group = max(16, (stop - start) // 4)
+    jobs = [(p, first) for first in range(start, stop, group) for p in range(parts)]
+
+    def kernel(v_hbm, *refs):
+        outs = refs[-len(pieces) - 4 : -4]
+        raw, low, high, sems = refs[-4:]
         z = lax.axis_index("chan")
         e = lax.axis_index("beam")
-        for mask, out in zip(masks, outs):
-            chan = (z ^ mask) * per_dev + e
-            for lane, half in enumerate(wide):
-                out[0, :, pl.ds(lane * 128, 128)] = half[pl.ds(chan, ants, stride=chans), :].astype(jnp.bfloat16)
-
-    return pl.pallas_call(
-        kernel,
-        grid=(parts,),
-        in_specs=[pl.BlockSpec((1, ants * chans, samples), lambda p: (p, 0, 0))],
-        out_specs=[pl.BlockSpec((1, ants, samples), lambda p: (p, 0, 0))] * len(masks),
-        out_shape=[jax.ShapeDtypeStruct((parts, ants, samples), jnp.bfloat16)] * len(masks),
-        scratch_shapes=[pltpu.VMEM((ants * chans, 128), jnp.float32)] * (samples // 128),
+
+        def fetch(number):
+            p, first = jobs[number]
+            rows = v_hbm.at[p, pl.ds(first * chans, group * chans), :]
+            return pltpu.make_async_copy(rows, raw.at[number], sems.at[number])
+
+        for number in range(len(jobs)):
+            fetch(number).start()
+        for number, (p, first) in enumerate(jobs):
+            fetch(number).wait()
+            slot = number % 2
+            for lane, wide in enumerate((low, high)):
+                wide[slot] = raw[number, :, pl.ds(lane * 128, 128)].astype(jnp.float32)
+            for (mask, piece_first, piece_last), out in zip(pieces, outs):
+                if piece_first <= first < piece_last:
+                    chan = (z ^ mask) * per_dev + e
+                    at = pl.ds(first - piece_first, group)
+                    for lane, wide in enumerate((low, high)):
+                        rows = wide[slot, pl.ds(chan, group, stride=chans), :]
+                        out[p, at, pl.ds(lane * 128, 128)] = rows.astype(jnp.bfloat16)
+
+    assert samples == 256
+    tokens = [] if token is None else [token]
+    in_hbm = pltpu.with_memory_space_constraint(voltages.reshape(parts, ants * chans, samples), pltpu.HBM)
+    return pl.pallas_call(
+        kernel,
+        in_specs=[pl.BlockSpec(memory_space=pltpu.HBM)] + [pl.BlockSpec(memory_space=pl.ANY)] * len(tokens),
+        out_specs=[VMEM] * len(pieces),
+        out_shape=[
+            jax.ShapeDtypeStruct((parts, last - first, samples), jnp.bfloat16) for _, first, last in pieces
+        ],
+        scratch_shapes=[
+            pltpu.VMEM((len(jobs), group * chans, samples), jnp.bfloat16),
+            pltpu.VMEM((2, group * chans, 128), jnp.float32),
+            pltpu.VMEM((2, group * chans, 128), jnp.float32),
+            pltpu.SemaphoreType.DMA((len(jobs),)),
+        ],
         compiler_params=PARAMS,
         name="split_channels",
-    )(voltages.reshape(parts, ants * chans, samples))
+    )(in_hbm, *tokens)
 
 
 def horner(coefs, u):
@@ -135,7 +163,7 @@
         ],
         compiler_params=PARAMS,
         name="make_weights",
-    )(chan_order, pos, gain, dirs)
+    )(pltpu.with_memory_space_constraint(chan_order, pltpu.SMEM), pos, gain, dirs)
 
 
 def chunk_product(w_ref, chunks, first, beam_rows):
@@ -219,7 +247,7 @@
         out_shape=outs,
         compiler_params=PARAMS,
         name=name,
-    )(delays, *arrays)
+    )(pltpu.with_memory_space_constraint(delays, pltpu.SMEM), *arrays)
 
 
 def store(outs, slot, value):
@@ -284,20 +312,28 @@
     chan_index = lax.axis_index("chan")
     beam_index = lax.axis_index("beam")
 
-    masks = [0] + [m for m in range(1, chan_count) if m != chan_count // 2] + [chan_count // 2]
-    blocks = split_channels(voltages, masks)
-    far = {m: partner(blocks[masks.index(m)], "chan", m) for m in reversed(masks[1:])}
-    chunks = [blocks[0]] + [far[m] for m in masks[1:]]
+    middle = chan_count // 2
+    near = list(range(middle))
+    distant = list(range(chan_count - 1, middle, -1))
+    masks = near + distant + [middle]
+    first = split_channels(voltages, [(middle, 0, ants // 2)])
+    across = split_channels(voltages, [(m, 0, ants) for m in distant] + [(middle, ants // 2, ants)], first[0])
+    beside = split_channels(voltages, [(m, 0, ants) for m in near], across[0])
+    first = [partner(first[0], "chan", middle)]
+    across = [partner(v, "chan", m) for v, m in zip(across, distant + [middle])]
+    beside = [beside[0]] + [partner(v, "chan", m) for v, m in zip(beside[1:], near[1:])]
+    chunks = beside + across[:-1] + first + across[-1:]
 
     order = chan_index ^ jnp.array(masks, jnp.int32)
     rows = antenna_row_lookup.reshape(chan_count, ants)[order].reshape(-1)
     gain = lax.dynamic_index_in_dim(gains[:, 0], beam_index, 1, keepdims=False)
     gain = gain.reshape(2, chan_count, ants)[:, order].reshape(2, -1)
-    dirs = jnp.concatenate([directions, partner(directions, "beam", 1)], axis=1)
+    held, _ = lax.optimization_barrier((directions, chunks[0]))
+    dirs = jnp.concatenate([directions, partner(held, "beam", 1)], axis=1)
     weights = make_weights(positions[:, rows], gain, dirs, chan_order, total, in_band)
 
     partial = early_beams(weights, chunks[:-1])
-    ours, theirs = last_levels(weights, chunks[-1:], ants * (chan_count - 1), partial, total)
+    ours, theirs = last_levels(weights, chunks[-1:], ants * chan_count - ants // 2, partial, total)
 
     flat_delays = delays.reshape(delays.shape[0], total)
     state, sent = core_round(ours, partner(theirs, "beam", 1), flat_delays, in_band)

time: 51 us -> 48.9 us (0.959)
  waiting for transfers between devices: 18.7 us -> 10.8 us
  Pallas kernels: 14 us -> 18.3 us
  starting transfers between devices: 11.8 us -> 14.8 us
  local copies, waits for them, and re-layouts: 6.11 us -> 4.53 us
    ppermute x9 -> x10, waiting for transfers between devices: 18.7 us -> 10.8 us  [partner(): return lax.ppermute(value, axis, pairs)]
    pallas_call x1 -> x3, Pallas kernels: 0.8 us -> 4.65 us  [split_channels(): pl.pallas_call(kernel, in_specs=[pl.BlockSpec(memory_space=pltpu.HBM)] +...]
    ppermute x9 -> x10, starting transfers between devices: 11.8 us -> 14.8 us  [partner(): return lax.ppermute(value, axis, pairs)]
    unnamed x18 -> x16, local copies, waits for them, and re-layouts: 1.85 us -> 0.27 us
    pallas_call x1, Pallas kernels: 1.78 us -> 2.32 us  [early_beams(): pl.pallas_call(kernel, in_specs=[VMEM] * (1 + len(chunks)), out_specs=VME...]
  transfers between devices with their start and end apart: 9 -> 10, of which waited for: 7 -> 5; matrix products, arithmetic and copies ran while one was open for 9% -> 9% of each run, Pallas kernels for 20% -> 27%
where the time goes in v2:
time: 48.9 us; the launch traced here: 48.7 us
  Pallas kernels  18.3 us (37%)
  starting transfers between devices  14.8 us (30%)
  waiting for transfers between devices  10.8 us (22%)
  local copies, waits for them, and re-layouts  4.53 us (9%)
    ppermute x10, starting transfers between devices, partner(): return lax.ppermute(value, axis, pairs)  14.8 us
    ppermute x10, waiting for transfers between devices, partner(): return lax.ppermute(value, axis, pairs)  10.8 us
    pallas_call x1, Pallas kernels, make_weights(): pl.pallas_call(kernel, grid=(beams // block,), in_specs=[SMEM, pl.BlockSp...  7.38 us
    pallas_call x3, Pallas kernels, split_channels(): pl.pallas_call(kernel, in_specs=[pl.BlockSpec(memory_space=pltpu.HBM)] +...  4.65 us
    gather x2, local copies, waits for them, and re-layouts, shards(): positions[:, rows]  3 us
    pallas_call x3, Pallas kernels, tree_call(): pl.pallas_call(kernel, in_specs=[SMEM] + [VMEM] * len(arrays), out_specs=...  2.59 us
    pallas_call x1, Pallas kernels, early_beams(): pl.pallas_call(kernel, in_specs=[VMEM] * (1 + len(chunks)), out_specs=VME...  2.32 us
    pallas_call x1, Pallas kernels, last_levels(): pl.pallas_call(kernel, in_specs=[VMEM] * (2 + len(chunks)), out_specs=[VM...  1.4 us
  transfers between devices with their start and end apart: 10, of which 5 were waited for; matrix products, arithmetic and copies ran while one was open for 9% of the time, Pallas kernels for 27%

profile of v2, /device:TPU:0, one launch (start us, length us, event | category | flops | bytes accessed | tf_op | source)
XLA Modules:
  0.0 48.7 jit_solution(9259642783787890922)
XLA Ops:
  0.0 1.4 %split_channels.3.refs_0_ = bf16[2,128,256]{2,1,0:T(8,128)(2,1)S(1)} custom-call(bf16[2,2048,256]{2,1,0:T(8,128)(2,1)} %bitcast.14), custom_call_target="tpu_custom_call" | custom-call | tf_op jit(solution)/shard_map/split_channels/pallas_call | solution.py:62
  1.4 4.1 %collective-permute-start.3 = (bf16[2,128,256]{2,1,0:T(8,128)(2,1)S(1)}, bf16[2,128,256]{2,1,0:T(8,128)(2,1)S(1)}, u32[]{:S(2)}, u32[]{:S(2)}) collective-permute-start(bf16[2,128,256]{2,1,0:T(8,128)(2,1)S(1)} %split_channels.3.refs_0_), channel_id=1, source_target_pairs={{0,8},{4,12},{8,0},{12,4},{1,9},{5,13},{9,1},{13,5},{2,10},{6,14},... | collective-permute-start | bytes 393224 | tf_op jit(solution)/shard_map/ppermute | solution.py:22
  5.5 1.6 %split_channels.4 = (bf16[2,256,256]{2,1,0:T(8,128)(2,1)S(1)}, bf16[2,128,256]{2,1,0:T(8,128)(2,1)S(1)}) custom-call(bf16[2,2048,256]{2,1,0:T(8,128)(2,1)} %bitcast.15, bf16[2,128,256]{2,1,0:T(8,128)(2,1)S(1)} %split_channels.3.refs_0_), custom_call_target="tpu_custom_call" | custom-call | tf_op jit(solution)/shard_map/split_channels/pallas_call | solution.py:62
  7.2 1.4 %collective-permute-start.2 = (bf16[2,256,256]{2,1,0:T(8,128)(2,1)S(1)}, bf16[2,256,256]{2,1,0:T(8,128)(2,1)S(1)}, u32[]{:S(2)}, u32[]{:S(2)}) collective-permute-start(bf16[2,256,256]{2,1,0:T(8,128)(2,1)S(1)} %get-tuple-element.16.refs_0_), channel_id=1, source_target_pairs={{0,12},{4,8},{8,4},{12,0},{1,13},{5,9},{9,5},{13,1},{2,14},{6,10},... | collective-permute-start | bytes 786440 | tf_op jit(solution)/shard_map/ppermute | solution.py:22
  8.6 1.6 %split_channels.5 = (bf16[2,256,256]{2,1,0:T(8,128)(2,1)S(1)}, bf16[2,256,256]{2,1,0:T(8,128)(2,1)S(1)}) custom-call(bf16[2,2048,256]{2,1,0:T(8,128)(2,1)} %bitcast.16, bf16[2,256,256]{2,1,0:T(8,128)(2,1)S(1)} %get-tuple-element.16.refs_0_), custom_call_target="tpu_custom_call" | custom-call | tf_op jit(solution)/shard_map/split_channels/pallas_call | solution.py:62
  10.3 0.3 collective-permute-start.1
  10.7 2.8 %collective-permute-start.4 = (bf16[2,128,256]{2,1,0:T(8,128)(2,1)S(1)}, bf16[2,128,256]{2,1,0:T(8,128)(2,1)S(1)}, u32[]{:S(2)}, u32[]{:S(2)}) collective-permute-start(bf16[2,128,256]{2,1,0:T(8,128)(2,1)S(1)} %get-tuple-element.20), channel_id=1, source_target_pairs={{0,8},{4,12},{8,0},{12,4},{1,9},{5,13},{9,1},{13,5},{2,10},{6,14},... | collective-permute-start | bytes 393224 | tf_op jit(solution)/shard_map/ppermute | solution.py:22
  13.5 0.6 %gather_fusion = s32[4,256]{1,0:T(4,128)S(1)} fusion(s32[4,256]{1,0:T(4,128)S(1)} %reshape.55, s32[1024]{0:T(1024)S(1)} %pad_clamp_fusion), kind=kCustom, calls=%fused_computation | custom fusion | bytes 8208 | tf_op jit(solution)/shard_map/gather | solution.py:328
  14.1 0.6 %gather_fusion.2 = f32[4,2,256]{2,1,0:T(2,128)S(1)} fusion(f32[2,4,256]{2,0,1:T(2,128)S(1)} %bitcast.17, s32[1024]{0:T(1024)S(1)} %pad_clamp_fusion), kind=kCustom, calls=%fused_computation.2 | custom fusion | bytes 16400 | tf_op jit(solution)/shard_map/gather | solution.py:330
  15.0 2.8 %gather_fusion.1 = f32[1024,3]{1,0:T(8,128)S(1)} fusion(f32[3,1024]{0,1:T(8,128)S(1)} %copy.11, s32[1024]{0:T(1024)S(1)} %broadcast_clamp_fusion), kind=kCustom, calls=%fused_computation.1 | custom fusion | bytes 28672 | tf_op jit(solution)/shard_map/gather | solution.py:333
  18.0 7.4 %make_weights.1.w_ref = bf16[2,1024,1024]{2,1,0:T(8,128)(2,1)S(1)} custom-call(s32[16]{0:T(128)S(1)} %copy-done.1, f32[3,1024]{1,0:T(4,128)S(1)} %bitcast.12, f32[2,1024]{1,0:T(2,128)S(1)} %bitcast.13, f32[3,1024]{1,0:T(4,128)S(1)} %pad_maximum_fusion.dir_ref), custom_call_target="tpu_custom_call" | custom-call | tf_op jit(solution)/shard_map/make_weights/pallas_call | solution.py:147
  25.4 2.3 %early_beams.1.part_ref = f32[1024,512]{1,0:T(8,128)S(1)} custom-call(bf16[2,1024,1024]{2,1,0:T(8,128)(2,1)S(1)} %make_weights.1.w_ref, bf16[2,256,256]{2,1,0:T(8,128)(2,1)S(1)} %get-tuple-element.17.refs_0_, bf16[2,256,256]{2,1,0:T(8,128)(2,1)S(1)} %collective-permute-done.1.refs_1_, bf16[2,256,256]{2,1,0:T(8,128)(2,1)S(1)} %collective-permute-done.2.refs_2_, ...), custom_call_target="tpu_custom_call" | custom-call | tf_op jit(solution)/shard_map/early_beams/pallas_call | solution.py:189
  27.8 1.0 %collective-permute-done.4.refs_0_ = bf16[2,128,256]{2,1,0:T(8,128)(2,1)S(1)} collective-permute-done((bf16[2,128,256]{2,1,0:T(8,128)(2,1)S(1)}, bf16[2,128,256]{2,1,0:T(8,128)(2,1)S(1)}, u32[]{:S(2)}, u32[]{:S(2)}) %collective-permute-start.4) | collective-permute-done | bytes 131104 | tf_op jit(solution)/shard_map/ppermute | solution.py:22
  28.7 1.4 %last_levels.1 = (f32[32,512]{1,0:T(8,128)S(1)}, f32[32,512]{1,0:T(8,128)S(1)}) custom-call(bf16[2,1024,1024]{2,1,0:T(8,128)(2,1)S(1)} %make_weights.1.w_ref, f32[1024,512]{1,0:T(8,128)S(1)} %early_beams.1.part_ref, bf16[2,128,256]{2,1,0:T(8,128)(2,1)S(1)} %collective-permute-done.4.refs_0_), custom_call_target="tpu_custom_call" | custom-call | tf_op jit(solution)/shard_map/last_levels/pallas_call | solution.py:225
  30.3 1.1 %collective-permute-done.5.other_ref = f32[32,512]{1,0:T(8,128)S(1)} collective-permute-done((f32[32,512]{1,0:T(8,128)S(1)}, f32[32,512]{1,0:T(8,128)S(1)}, u32[]{:S(2)}, u32[]{:S(2)}) %collective-permute-start.5) | collective-permute-done | bytes 65568 | tf_op jit(solution)/shard_map/ppermute | solution.py:22
  31.5 0.6 %core_round.1 = (f32[2,32,512]{2,1,0:T(8,128)S(1)}, bf16[2,32,512]{2,1,0:T(8,128)(2,1)S(1)}) custom-call(s32[4,16]{1,0:T(4,128)S(1)} %reshape.54.delay_ref, f32[32,512]{1,0:T(8,128)S(1)} %get-tuple-element.21.own_ref, f32[32,512]{1,0:T(8,128)S(1)} %collective-permute-done.5.other_ref), custom_call_target="tpu_custom_call" | custom-call | tf_op jit(solution)/shard_map/core_round/pallas_call | solution.py:243
  32.1 1.0 %collective-permute-start.6 = (bf16[2,32,512]{2,1,0:T(8,128)(2,1)S(1)}, bf16[2,32,512]{2,1,0:T(8,128)(2,1)S(1)}, u32[]{:S(2)}, u32[]{:S(2)}) collective-permute-start(bf16[2,32,512]{2,1,0:T(8,128)(2,1)S(1)} %get-tuple-element.24), channel_id=1, source_target_pairs={{0,4},{4,0},{8,12},{12,8},{1,5},{5,1},{9,13},{13,9},{2,6},{6,2},{1... | collective-permute-start | bytes 196616 | tf_op jit(solution)/shard_map/ppermute | solution.py:22
  33.1 3.2 %collective-permute-start.7 = (bf16[2,32,512]{2,1,0:T(8,128)(2,1)S(1)}, bf16[2,32,512]{2,1,0:T(8,128)(2,1)S(1)}, u32[]{:S(2)}, u32[]{:S(2)}) collective-permute-start(bf16[2,32,512]{2,1,0:T(8,128)(2,1)S(1)} %get-tuple-element.24), channel_id=1, source_target_pairs={{0,8},{4,12},{8,0},{12,4},{1,9},{5,13},{9,1},{13,5},{2,10},{6,14},... | collective-permute-start | bytes 196616 | tf_op jit(solution)/shard_map/ppermute | solution.py:22
  36.6 3.8 %collective-permute-done.7.refs_2_ = bf16[2,32,512]{2,1,0:T(8,128)(2,1)S(1)} collective-permute-done((bf16[2,32,512]{2,1,0:T(8,128)(2,1)S(1)}, bf16[2,32,512]{2,1,0:T(8,128)(2,1)S(1)}, u32[]{:S(2)}, u32[]{:S(2)}) %collective-permute-start.7) | collective-permute-done | bytes 65568 | tf_op jit(solution)/shard_map/ppermute | solution.py:22
  40.4 2.1 %collective-permute-done.8.refs_3_ = bf16[2,32,512]{2,1,0:T(8,128)(2,1)S(1)} collective-permute-done((bf16[2,32,512]{2,1,0:T(8,128)(2,1)S(1)}, bf16[2,32,512]{2,1,0:T(8,128)(2,1)S(1)}, u32[]{:S(2)}, u32[]{:S(2)}) %collective-permute-start.8) | collective-permute-done | bytes 65568 | tf_op jit(solution)/shard_map/ppermute | solution.py:22
  42.4 0.7 %rounds_chan.1 = (f32[2,32,512]{2,1,0:T(8,128)S(1)}, bf16[2,32,512]{2,1,0:T(8,128)(2,1)S(1)}) custom-call(s32[4,16]{1,0:T(4,128)S(1)} %reshape.54.delay_ref, f32[2,32,512]{2,1,0:T(8,128)S(1)} %get-tuple-element.23.refs_0_, bf16[2,32,512]{2,1,0:T(8,128)(2,1)S(1)} %collective-permute-done.6.refs_1_, bf16[2,32,512]{2,1,0:T(8,128)(2,1)S(1)} %collective-permute-done.7.refs_2_, ...), custom_call_target="tpu_custom_call" | custom-call | tf_op jit(solution)/shard_map/rounds_chan/pallas_call | solution.py:243
  43.1 1.6 %collective-permute-start.9 = (bf16[2,32,512]{2,1,0:T(8,128)(2,1)S(1)}, bf16[2,32,512]{2,1,0:T(8,128)(2,1)S(1)}, u32[]{:S(2)}, u32[]{:S(2)}) collective-permute-start(bf16[2,32,512]{2,1,0:T(8,128)(2,1)S(1)} %get-tuple-element.26), channel_id=1, source_target_pairs={{0,2},{2,0},{1,3},{3,1},{4,6},{6,4},{5,7},{7,5},{8,10},{10,8},{9,1... | collective-permute-start | bytes 196616 | tf_op jit(solution)/shard_map/ppermute | solution.py:22
  44.7 2.8 %collective-permute-done.9.refs_1_ = bf16[2,32,512]{2,1,0:T(8,128)(2,1)S(1)} collective-permute-done((bf16[2,32,512]{2,1,0:T(8,128)(2,1)S(1)}, bf16[2,32,512]{2,1,0:T(8,128)(2,1)S(1)}, u32[]{:S(2)}, u32[]{:S(2)}) %collective-permute-start.9) | collective-permute-done | bytes 65568 | tf_op jit(solution)/shard_map/ppermute | solution.py:22
  47.5 1.3 %rounds_band.1 = f32[2,32,512]{2,1,0:T(8,128)} custom-call(s32[4,16]{1,0:T(4,128)S(1)} %reshape.54.delay_ref, f32[2,32,512]{2,1,0:T(8,128)S(1)} %get-tuple-element.25.refs_0_, bf16[2,32,512]{2,1,0:T(8,128)(2,1)S(1)} %collective-permute-done.9.refs_1_), custom_call_target="tpu_custom_call" | custom-call | tf_op jit(solution)/shard_map/rounds_band/pallas_call | solution.py:243
  (33 shorter events, 1.1 us)
Async XLA Ops:
  0.0 14.1 %copy-start = (f32[2,1,2,1024]{3,2,1,0:T(2,128)S(1)}, f32[2,1,2,1024]{3,2,1,0:T(2,128)}, u32[]{:S(2)}) copy-start(f32[2,1,2,1024]{3,2,1,0:T(2,128)} %param.9) | copy-start | bytes 49156
  1.4 8.9 %copy-start.3 = (f32[3,512]{1,0:T(4,128)S(1)}, f32[3,512]{1,0:T(4,128)}, u32[]{:S(2)}) copy-start(f32[3,512]{1,0:T(4,128)} %param.11) | copy-start | bytes 18436
  1.4 12.0 %copy-start.6 = (s32[4]{0:T(128)S(1)}, s32[4]{0:T(128)}, u32[]{:S(2)}) copy-start(s32[4]{0:T(128)} %constant.24.clone) | copy-start | bytes 52
  1.4 12.0 %copy-start.5 = (s32[1024]{0:T(1024)S(1)}, s32[1024]{0:T(1024)}, u32[]{:S(2)}) copy-start(s32[1024]{0:T(1024)} %param.12) | copy-start | bytes 12292
  1.4 13.3 %copy-start.2 = (f32[3,1024]{1,0:T(4,128)S(1)}, f32[3,1024]{1,0:T(4,128)}, u32[]{:S(2)}) copy-start(f32[3,1024]{1,0:T(4,128)} %param.10) | copy-start | bytes 36868
  1.4 23.9 %collective-permute-start.3 = (bf16[2,128,256]{2,1,0:T(8,128)(2,1)S(1)}, bf16[2,128,256]{2,1,0:T(8,128)(2,1)S(1)}, u32[]{:S(2)}, u32[]{:S(2)}) collective-permute-start(bf16[2,128,256]{2,1,0:T(8,128)(2,1)S(1)} %split_channels.3.refs_0_), channel_id=1, source_target_pairs={{0,8},{4,12},{8,0},{12,4},{1,9},{5,13},{9,1},{13,5},{2,10},{6,14},... | collective-permute-start | bytes 393224 | tf_op jit(solution)/shard_map/ppermute | solution.py:22
  7.2 10.8 %copy-start.1 = (s32[16]{0:T(128)S(1)}, s32[16]{0:T(128)}, u32[]{:S(2)}) copy-start(s32[16]{0:T(128)} %order_ref.1) | copy-start | bytes 196
  7.2 18.2 %collective-permute-start.2 = (bf16[2,256,256]{2,1,0:T(8,128)(2,1)S(1)}, bf16[2,256,256]{2,1,0:T(8,128)(2,1)S(1)}, u32[]{:S(2)}, u32[]{:S(2)}) collective-permute-start(bf16[2,256,256]{2,1,0:T(8,128)(2,1)S(1)} %get-tuple-element.16.refs_0_), channel_id=1, source_target_pairs={{0,12},{4,8},{8,4},{12,0},{1,13},{5,9},{9,5},{13,1},{2,14},{6,10},... | collective-permute-start | bytes 786440 | tf_op jit(solution)/shard_map/ppermute | solution.py:22
  10.3 7.7 %collective-permute-start = (f32[3,512]{1,0:T(4,128)S(1)}, f32[3,512]{1,0:T(4,128)S(1)}, u32[]{:S(2)}, u32[]{:S(2)}) collective-permute-start(f32[3,512]{1,0:T(4,128)S(1)} %copy-done.3), channel_id=1, source_target_pairs={{0,1},{1,0},{2,3},{3,2},{4,5},{5,4},{6,7},{7,6},{8,9},{9,8},{10,11... | collective-permute-start | bytes 18440 | tf_op jit(solution)/shard_map/ppermute | solution.py:22
  10.3 15.1 %collective-permute-start.1 = (bf16[2,256,256]{2,1,0:T(8,128)(2,1)S(1)}, bf16[2,256,256]{2,1,0:T(8,128)(2,1)S(1)}, u32[]{:S(2)}, u32[]{:S(2)}) collective-permute-start(bf16[2,256,256]{2,1,0:T(8,128)(2,1)S(1)} %get-tuple-element.19), channel_id=1, source_target_pairs={{0,4},{4,0},{8,12},{12,8},{1,5},{5,1},{9,13},{13,9},{2,6},{6,2},{1... | collective-permute-start | bytes 786440 | tf_op jit(solution)/shard_map/ppermute | solution.py:22
  10.7 18.1 %collective-permute-start.4 = (bf16[2,128,256]{2,1,0:T(8,128)(2,1)S(1)}, bf16[2,128,256]{2,1,0:T(8,128)(2,1)S(1)}, u32[]{:S(2)}, u32[]{:S(2)}) collective-permute-start(bf16[2,128,256]{2,1,0:T(8,128)(2,1)S(1)} %get-tuple-element.20), channel_id=1, source_target_pairs={{0,8},{4,12},{8,0},{12,4},{1,9},{5,13},{9,1},{13,5},{2,10},{6,14},... | collective-permute-start | bytes 393224 | tf_op jit(solution)/shard_map/ppermute | solution.py:22
  27.7 2.5 %copy-start.4 = (s32[4,2,8]{2,1,0:T(2,128)S(1)}, s32[4,2,8]{2,1,0:T(2,128)}, u32[]{:S(2)}) copy-start(s32[4,2,8]{2,1,0:T(2,128)} %param.14) | copy-start | bytes 772
  30.2 1.3 %collective-permute-start.5 = (f32[32,512]{1,0:T(8,128)S(1)}, f32[32,512]{1,0:T(8,128)S(1)}, u32[]{:S(2)}, u32[]{:S(2)}) collective-permute-start(f32[32,512]{1,0:T(8,128)S(1)} %get-tuple-element.22), channel_id=1, source_target_pairs={{0,1},{1,0},{2,3},{3,2},{4,5},{5,4},{6,7},{7,6},{8,9},{9,8},{10,11... | collective-permute-start | bytes 196616 | tf_op jit(solution)/shard_map/ppermute | solution.py:22
  32.1 4.5 %collective-permute-start.6 = (bf16[2,32,512]{2,1,0:T(8,128)(2,1)S(1)}, bf16[2,32,512]{2,1,0:T(8,128)(2,1)S(1)}, u32[]{:S(2)}, u32[]{:S(2)}) collective-permute-start(bf16[2,32,512]{2,1,0:T(8,128)(2,1)S(1)} %get-tuple-element.24), channel_id=1, source_target_pairs={{0,4},{4,0},{8,12},{12,8},{1,5},{5,1},{9,13},{13,9},{2,6},{6,2},{1... | collective-permute-start | bytes 196616 | tf_op jit(solution)/shard_map/ppermute | solution.py:22
  33.1 7.3 %collective-permute-start.7 = (bf16[2,32,512]{2,1,0:T(8,128)(2,1)S(1)}, bf16[2,32,512]{2,1,0:T(8,128)(2,1)S(1)}, u32[]{:S(2)}, u32[]{:S(2)}) collective-permute-start(bf16[2,32,512]{2,1,0:T(8,128)(2,1)S(1)} %get-tuple-element.24), channel_id=1, source_target_pairs={{0,8},{4,12},{8,0},{12,4},{1,9},{5,13},{9,1},{13,5},{2,10},{6,14},... | collective-permute-start | bytes 196616 | tf_op jit(solution)/shard_map/ppermute | solution.py:22
  36.3 6.2 %collective-permute-start.8 = (bf16[2,32,512]{2,1,0:T(8,128)(2,1)S(1)}, bf16[2,32,512]{2,1,0:T(8,128)(2,1)S(1)}, u32[]{:S(2)}, u32[]{:S(2)}) collective-permute-start(bf16[2,32,512]{2,1,0:T(8,128)(2,1)S(1)} %get-tuple-element.24), channel_id=1, source_target_pairs={{0,12},{4,8},{8,4},{12,0},{1,13},{5,9},{9,5},{13,1},{2,14},{6,10},... | collective-permute-start | bytes 196616 | tf_op jit(solution)/shard_map/ppermute | solution.py:22
  43.1 4.3 %collective-permute-start.9 = (bf16[2,32,512]{2,1,0:T(8,128)(2,1)S(1)}, bf16[2,32,512]{2,1,0:T(8,128)(2,1)S(1)}, u32[]{:S(2)}, u32[]{:S(2)}) collective-permute-start(bf16[2,32,512]{2,1,0:T(8,128)(2,1)S(1)} %get-tuple-element.26), channel_id=1, source_target_pairs={{0,2},{2,0},{1,3},{3,1},{4,6},{6,4},{5,7},{7,5},{8,10},{10,8},{9,1... | collective-permute-start | bytes 196616 | tf_op jit(solution)/shard_map/ppermute | solution.py:22

commit v3 on v0

v3 whole, which is shorter than its diff:
```python
import math

import jax
import jax.numpy as jnp
from jax import lax
from jax.experimental import pallas as pl
from jax.experimental.pallas import tpu as pltpu
from jax.sharding import PartitionSpec as P

INTEG = 8
VMEM = pl.BlockSpec(memory_space=pltpu.VMEM)
SMEM = pl.BlockSpec(memory_space=pltpu.SMEM)
PARAMS = pltpu.CompilerParams(vmem_limit_bytes=40 * 1024 * 1024)
SIN = (6.283184915580925, -41.34158901325128, 81.59993513909575, -76.61436771142901, 41.342343389037076, -12.470285565721209)
COS = (0.9999992089426497, -19.738979914331107, 64.92864094416844, -85.27141067260794, 58.789407905427666, -21.069178520245686)
ROUNDER = 1.5 * 2.0**23
PHASE_ROWS = 32
LONG = pl.CostEstimate(flops=10**10, bytes_accessed=10**8, transcendentals=10**8)
SHORT = pl.CostEstimate(flops=0, bytes_accessed=0, transcendentals=0)


def partner(value, flips):
    axes = tuple(axis for axis in ("chan", "band", "beam") if axis in dict(flips))
    sizes = [lax.axis_size(axis) for axis in axes]
    flip = 0
    for axis, bit in flips:
        flip ^= (1 << bit) * math.prod(sizes[axes.index(axis) + 1 :])
    pairs = [(source, source ^ flip) for source in range(math.prod(sizes))]
    return lax.ppermute(value, axes, pairs)


def chan_partner(value, mask):
    return partner(value, [("chan", bit) for bit in range(mask.bit_length()) if mask >> bit & 1])


def split_channels(voltages, pieces, from_hbm, token=None):
    parts, ants, _, chans, samples = voltages.shape
    per_dev = lax.axis_size("beam")
    start = min(first for _, first, _ in pieces)
    stop = max(last for _, _, last in pieces)
    group = max(16, (stop - start) // 4)
    jobs = [(p, first) for first in range(start, stop, group) for p in range(parts)]
    lanes = range(0, samples, 128)
    tokens = [] if token is None else [token]

    def kernel(v_ref, *refs):
        refs = refs[len(tokens) :]
        outs, wide, (raw, sems) = refs[: len(pieces)], refs[len(pieces) : -2], refs[-2:]
        z = lax.axis_index("chan")
        e = lax.axis_index("beam")

        def rows(number):
            p, first = jobs[number]
            return v_ref.at[p, pl.ds(first * chans, group * chans), :]

        def fetch(number):
            return pltpu.make_async_copy(rows(number), raw.at[number], sems.at[number])

        if from_hbm:
            for number in range(len(jobs)):
                fetch(number).start()
        for number, (p, first) in enumerate(jobs):
            if from_hbm:
                fetch(number).wait()
            block = raw.at[number] if from_hbm else rows(number)
            slot = number % 2
            for lane, half in zip(lanes, wide):
                half[slot] = block[:, pl.ds(lane, 128)].astype(jnp.float32)
            for (mask, piece_first, piece_last), out in zip(pieces, outs):
                if piece_first <= first < piece_last:
                    chan = (z ^ mask) * per_dev + e
                    at = pl.ds(first - piece_first, group)
                    for lane, half in zip(lanes, wide):
                        out[p, at, pl.ds(lane, 128)] = half[slot, pl.ds(chan, group, stride=chans), :].astype(jnp.bfloat16)

    place = pltpu.HBM if from_hbm else pltpu.VMEM
    raw_slots = len(jobs) if from_hbm else 1
    return pl.pallas_call(
        kernel,
        in_specs=[pl.BlockSpec(memory_space=place)] + [pl.BlockSpec(memory_space=pl.ANY)] * len(tokens),
        out_specs=[VMEM] * len(pieces),
        out_shape=[
            jax.ShapeDtypeStruct((parts, last - first, samples), jnp.bfloat16) for _, first, last in pieces
        ],
        scratch_shapes=[pltpu.VMEM((2, group * chans, 128), jnp.float32)] * len(lanes)
        + [
            pltpu.VMEM((raw_slots, group * chans, samples), jnp.bfloat16),
            pltpu.SemaphoreType.DMA((raw_slots,)),
        ],
        compiler_params=PARAMS,
        name="split_channels",
    )(pltpu.with_memory_space_constraint(voltages.reshape(parts, ants * chans, samples), place), *tokens)


def horner(coefs, u):
    total = coefs[-1] * u + coefs[-2]
    for coef in coefs[-3::-1]:
        total = total * u + coef
    return total


def bf16_parts(x):
    first = x.astype(jnp.bfloat16).astype(jnp.float32)
    rest = x - first
    second = rest.astype(jnp.bfloat16).astype(jnp.float32)
    return first, second, rest - second


def xor_blocks(x, index, count):
    size = x.shape[-1] // count
    for bit in range(count.bit_length() - 1):
        swapped = [x[..., (i ^ (1 << bit)) * size : (i ^ (1 << bit)) * size + size] for i in range(count)]
        x = jnp.where((index >> bit) & 1 == 1, jnp.concatenate(swapped, axis=-1), x)
    return x


def phase_rows(dirs):
    parts = jnp.concatenate(bf16_parts(dirs), axis=0)
    rows = [parts, parts, parts, jnp.ones((3, dirs.shape[1]), jnp.float32)]
    rows.append(jnp.zeros((PHASE_ROWS - 30, dirs.shape[1]), jnp.float32))
    return jnp.concatenate(rows, axis=0).astype(jnp.bfloat16)


def fill_weights(left_ref, right_ref, length_ref, turns, out):
    _, beams, ants = out.shape
    block = turns.shape[0]
    lanes = min(ants, 512)

    def block_of_beams(number, carry):
        start = pl.multiple_of(number * block, block)
        turns[...] = lax.dot_general(
            left_ref[:, pl.ds(start, block)],
            right_ref[...],
            (((0,), (0,)), ((), ())),
            preferred_element_type=jnp.float32,
        )

        def rows(step, carry):
            at = pl.ds(pl.multiple_of(step * 16, 16), 16)
            to = pl.ds(pl.multiple_of(start + step * 16, 16), 16)
            for lane in range(0, ants, lanes):
                cols = pl.ds(lane, lanes)
                x = turns[at, cols]
                t = x - ((x + ROUNDER) - ROUNDER)
                u = t * t
                scale = length_ref[:, cols]
                out[0, to, cols] = (horner(COS, u) * scale).astype(jnp.bfloat16)
                out[1, to, cols] = (horner(SIN, u) * (t * scale)).astype(jnp.bfloat16)
            return carry

        return lax.fori_loop(0, block // 16, rows, carry)

    lax.fori_loop(0, beams // block, block_of_beams, 0)


def our_weights(positions, lookup, gains, dirs, chan_order, masks, total, in_band):
    ants, beams = positions.shape[1], dirs.shape[1]
    per_dev = lax.axis_size("beam")
    size = ants // len(masks)
    lanes = min(ants, 512)

    def in_order(x, z):
        x = xor_blocks(x, z, len(masks))
        return jnp.concatenate([x[..., m * size : m * size + size] for m in masks], axis=-1)

    def kernel(order_ref, pos_ref, look_ref, gain_ref, dir_ref, out, right_ref, length_ref, left, turns):
        z = lax.axis_index("chan")
        e = lax.axis_index("beam")
        slot = lax.axis_index("band") * in_band + z * per_dev + e
        freq = 1.0 + order_ref[slot].astype(jnp.float32) * (1.0 / total)

        g_re = in_order(jnp.where(e == 0, gain_ref[0, 0:1, :], gain_ref[0, 1:2, :]), z)
        g_im = in_order(jnp.where(e == 0, gain_ref[1, 0:1, :], gain_ref[1, 1:2, :]), z)
        top = jnp.maximum(jnp.abs(g_re), jnp.abs(g_im))
        low = jnp.minimum(jnp.abs(g_re), jnp.abs(g_im))
        ratio = low / jnp.where(top > 0.0, top, 1.0)
        length_ref[...] = top * jnp.sqrt(1.0 + ratio * ratio) * (1.0 / math.sqrt(ants))

        parts = [jnp.concatenate([part] * 3, axis=0) for part in bf16_parts(pos_ref[...] * -freq)]
        parts.append(jnp.zeros((PHASE_ROWS - 27, ants), jnp.float32))
        table = jnp.concatenate(parts, axis=0).astype(jnp.bfloat16)
        look = in_order(look_ref[...], z)
        antenna = lax.broadcasted_iota(jnp.int32, (ants, lanes), 0)
        turn_parts = jnp.concatenate(
            [jnp.zeros((27, ants), jnp.float32)]
            + list(bf16_parts(jnp.arctan2(g_im, g_re) * (0.5 / math.pi)))
            + [jnp.zeros((PHASE_ROWS - 30, ants), jnp.float32)],
            axis=0,
        )
        for lane in range(0, ants, lanes):
            chosen = jnp.where(antenna == look[:, lane : lane + lanes], 1.0, 0.0).astype(jnp.bfloat16)
            rows = jnp.dot(table, chosen, preferred_element_type=jnp.float32)
            right_ref[:, pl.ds(lane, lanes)] = (rows + turn_parts[:, lane : lane + lanes]).astype(jnp.bfloat16)
        left[...] = phase_rows(dir_ref[...])
        fill_weights(left, right_ref, length_ref, turns, out)

    return pl.pallas_call(
        kernel,
        in_specs=[SMEM] + [VMEM] * 4,
        out_specs=[VMEM] * 3,
        out_shape=[
            jax.ShapeDtypeStruct((2, beams, ants), jnp.bfloat16),
            jax.ShapeDtypeStruct((PHASE_ROWS, ants), jnp.bfloat16),
            jax.ShapeDtypeStruct((1, ants), jnp.float32),
        ],
        scratch_shapes=[
            pltpu.VMEM((PHASE_ROWS, beams), jnp.bfloat16),
            pltpu.VMEM((min(beams, 128), ants), jnp.float32),
        ],
        compiler_params=PARAMS,
        cost_estimate=LONG,
        name="our_weights",
    )(chan_order, positions, lookup, gains, dirs)


def their_weights(right, length, dirs):
    ants, beams = right.shape[1], dirs.shape[1]

    def kernel(right_ref, length_ref, dir_ref, out, left, turns):
        left[...] = phase_rows(dir_ref[...])
        fill_weights(left, right_ref, length_ref, turns, out)

    return pl.pallas_call(
        kernel,
        in_specs=[VMEM] * 3,
        out_specs=VMEM,
        out_shape=jax.ShapeDtypeStruct((2, beams, ants), jnp.bfloat16),
        scratch_shapes=[
            pltpu.VMEM((PHASE_ROWS, beams), jnp.bfloat16),
            pltpu.VMEM((min(beams, 128), ants), jnp.float32),
        ],
        compiler_params=PARAMS,
        cost_estimate=SHORT,
        name="their_weights",
    )(right, length, dirs)


def chunk_product(w_ref, blocks, first, beam_rows):
    re = jnp.concatenate([re for re, _ in blocks], axis=0)
    im = jnp.concatenate([im for _, im in blocks], axis=0)
    straight = jnp.concatenate([re, im], axis=1)
    turned = jnp.concatenate([-im, re], axis=1)
    cols = pl.ds(first, re.shape[0])
    dot = lambda a, b: jnp.dot(a, b, preferred_element_type=jnp.float32)
    return dot(w_ref[0, beam_rows, cols], straight) + dot(w_ref[1, beam_rows, cols], turned)


def filled(ref, before, after):
    zeros = lambda count: [jnp.zeros((count, ref.shape[2]), ref.dtype)] if count else []
    return [jnp.concatenate(zeros(before) + [ref[p]] + zeros(after), axis=0) for p in range(2)]


def early_beams(weights, chunks, rest):
    half = weights[0].shape[1]
    samples = chunks[0].shape[2]
    step = min(half, 256)

    def kernel(ours_ref, theirs_ref, *refs):
        blocks = [filled(ref, 0, 0) for ref in refs[:-2]] + [filled(refs[-2], 0, rest)]
        for number, w_ref in enumerate((ours_ref, theirs_ref)):
            for row in range(0, half, step):
                product = chunk_product(w_ref, blocks, 0, pl.ds(row, step))
                refs[-1][pl.ds(number * half + row, step), :] = product

    return pl.pallas_call(
        kernel,
        in_specs=[VMEM] * (2 + len(chunks)),
        out_specs=VMEM,
        out_shape=jax.ShapeDtypeStruct((2 * half, 2 * samples), jnp.float32),
        compiler_params=PARAMS,
        cost_estimate=SHORT,
        name="early_beams",
    )(*weights, *chunks)


def two_parts(x):
    high = x.astype(jnp.bfloat16)
    return high, (x - high.astype(jnp.float32)).astype(jnp.bfloat16)


def last_levels(weights, chunk, done, partial, total):
    _, half, ants = weights[0].shape
    samples = chunk.shape[2]
    bins = samples // INTEG
    step = min(half, 256)
    first = ants - chunk.shape[1] - done

    def kernel(ours_ref, theirs_ref, part_ref, chunk_ref, high_ref, low_ref, sent_ref):
        blocks = [filled(chunk_ref, done, 0)]
        bin_no = lax.broadcasted_iota(jnp.int32, (bins, samples), 0)
        time = lax.broadcasted_iota(jnp.int32, (bins, samples), 1)
        centre = jnp.where(time // INTEG == bin_no, 1.0 / INTEG, 0.0) - 1.0 / samples
        centre = centre.astype(jnp.bfloat16)
        for number, w_ref in enumerate((ours_ref, theirs_ref)):
            for row in range(0, half, step):
                rows = pl.ds(row, step)
                beam = part_ref[pl.ds(number * half + row, step), :] + chunk_product(w_ref, blocks, first, rows)
                re, im = beam[:, :samples], beam[:, samples:]
                high, low = two_parts(re * re + im * im)
                dot = lambda b: lax.dot_general(centre, b, (((1,), (1,)), ((), ())), preferred_element_type=jnp.float32)
                high, low = two_parts((dot(high) + dot(low)) * (1.0 / math.sqrt(total)))
                if number == 0:
                    high_ref[:, rows] = high
                    low_ref[:, rows] = low
                else:
                    sent_ref[:, rows] = high

    return pl.pallas_call(
        kernel,
        in_specs=[VMEM] * 4,
        out_specs=[VMEM] * 3,
        out_shape=[jax.ShapeDtypeStruct((bins, half), jnp.bfloat16)] * 3,
        compiler_params=PARAMS,
        name="last_levels",
    )(*weights, partial, chunk)


def tree_maps(delays, steps, bins, in_band):
    per_dev = lax.axis_size("beam")
    sources = [[0] + list(range(1 << len(bits))) for bits in steps]

    def kernel(delay_ref, *outs):
        def place(flips):
            at = {axis: lax.axis_index(axis) for axis in ("band", "chan", "beam")}
            for axis, bit in flips:
                at[axis] = at[axis] ^ (1 << bit)
            return at

        round_no = 0
        for bits, srcs, out in zip(steps, sources, outs):
            row = lax.broadcasted_iota(jnp.int32, out.shape[1:], 0)
            col = lax.broadcasted_iota(jnp.int32, out.shape[1:], 1)
            for slot in range(per_dev):
                shift = jnp.zeros_like(col)
                for number, source in enumerate(srcs):
                    moved = 0
                    for k, (axis, bit) in enumerate(bits):
                        later = [bits[j] for j in range(k + 1, len(bits)) if source >> j & 1]
                        end = place(later)
                        start = place(later + ([bits[k]] if source >> k & 1 else []))
                        delay = delay_ref[round_no + k, end["band"] * in_band + end["chan"] * per_dev + slot]
                        moved = moved + ((start[axis] >> bit) & 1) * delay
                    shift = jnp.where(col // bins == number, moved, shift)
                hit = lax.rem(row - col + len(bits) * bins + out.shape[2] - shift, bins) == 0
                out[slot] = jnp.where(hit, 1.0, 0.0).astype(jnp.bfloat16)
            round_no += len(bits)

    return pl.pallas_call(
        kernel,
        in_specs=[SMEM],
        out_specs=[VMEM] * len(steps),
        out_shape=[jax.ShapeDtypeStruct((per_dev, bins, len(srcs) * bins), jnp.bfloat16) for srcs in sources],
        compiler_params=PARAMS,
        name="tree_maps",
    )(delays)


def tree_step(matrix, states, final):
    slots, bins, _ = matrix.shape
    width = states[0].shape[-1]

    def kernel(map_ref, *refs):
        ins, outs = refs[: len(states)], refs[len(states) :]
        for slot in range(slots):
            column = [ref[...] if len(ref.shape) == 2 else ref[slot] for ref in ins]
            value = jnp.dot(map_ref[slot], jnp.concatenate(column, axis=0), preferred_element_type=jnp.float32)
            for out, part in zip(outs, [value] if final else two_parts(value)):
                out[slot] = part

    dtypes = [jnp.float32] if final else [jnp.bfloat16] * 2
    return pl.pallas_call(
        kernel,
        in_specs=[VMEM] * (1 + len(states)),
        out_specs=[VMEM] * len(dtypes),
        out_shape=[jax.ShapeDtypeStruct((slots, bins, width), dtype) for dtype in dtypes],
        compiler_params=PARAMS,
        name="tree_step",
    )(matrix, *states)


def shards(voltages, gains, positions, directions, antenna_row_lookup, chan_order, delays):
    chan_count = lax.axis_size("chan")
    band_count = lax.axis_size("band")
    per_dev = gains.shape[2]
    assert per_dev == lax.axis_size("beam") == 2
    in_band = per_dev * chan_count
    total = in_band * band_count
    ants, samples = voltages.shape[1], voltages.shape[4]
    bins = samples // INTEG

    middle = chan_count // 2
    near = list(range(middle))
    distant = list(range(chan_count - 1, middle, -1))
    masks = near + distant + [middle]
    cut = ants // 4
    first = split_channels(voltages, [(middle, 0, cut)], True)
    across = split_channels(voltages, [(m, 0, ants) for m in distant] + [(middle, cut, ants)], False, first[0])
    beside = split_channels(voltages, [(m, 0, ants) for m in near], False, across[0])
    first = [chan_partner(first[0], middle)]
    across = [chan_partner(v, m) for v, m in zip(across, distant + [middle])]
    chunks = [beside[0]] + [chan_partner(v, m) for v, m in zip(beside[1:], near[1:])]
    chunks += across[:-1] + first

    lookup = antenna_row_lookup.reshape(1, -1)
    placed, _ = lax.optimization_barrier((positions, beside[0]))
    ours, right, length = our_weights(placed, lookup, gains[:, 0], directions, chan_order, masks, total, in_band)
    held, _ = lax.optimization_barrier((directions, length))
    weights = [ours, their_weights(right, length, partner(held, [("beam", 0)]))]
    partial = early_beams(weights, chunks, ants - cut)

    bits = [("beam", 0)]
    for axis, count in (("chan", chan_count), ("band", band_count)):
        bits += [(axis, bit) for bit in range(count.bit_length() - 1)]
    steps = [bits[i : i + 2] for i in range(0, len(bits), 2)]
    maps = tree_maps(delays.reshape(delays.shape[0], total), steps, bins, in_band)
    partial, *maps = lax.optimization_barrier((partial, *maps))

    high, low, other = last_levels(weights, across[-1], cut, partial, total)
    for number, (step, matrix) in enumerate(zip(steps, maps)):
        states = [high, low]
        for source in range(1, 1 << len(step)):
            flips = [place for k, place in enumerate(step) if source >> k & 1]
            states.append(partner(other if ("beam", 0) in flips else high, flips))
        if number == len(steps) - 1:
            (state,) = tree_step(matrix, states, True)
        else:
            high, low = tree_step(matrix, states, False)
    return state.reshape(1, per_dev, bins, state.shape[2])


def solution(mesh):
    placed = (
        P(None, "chan", "band", None, "group"),
        P(None, "band", "chan", None),
        P(),
        P(None, ("group", "beam")),
        P(),
        P(),
        P(),
    )
    return jax.shard_map(
        shards,
        mesh=mesh,
        in_specs=placed,
        out_specs=P("band", "chan", None, ("group", "beam")),
        check_vma=False,
    )
```

time: 94.5 us -> 46.7 us (0.49)
  other arithmetic: 38.1 us -> 0 us
  local copies, waits for them, and re-layouts: 20 us -> 0.8 us
  Pallas kernels: 0 us -> 16.8 us
  waiting for transfers between devices: 22.3 us -> 13.7 us
  starting transfers between devices: 8.15 us -> 15 us
  matrix products: 5.44 us -> 0 us
    pallas_call x0 -> x10, Pallas kernels: none -> 16.8 us  [the longest x1 4.55 us: our_weights(): pl.pallas_call(kernel, in_specs=[SMEM] + [VMEM] * 4, out_specs=[VMEM] * 3...]
    neg x1 -> x0, other arithmetic: 16.1 us -> none  [beam_weights(): lower_rows = jnp.concatenate([-w_im, w_re], axis=2)]
    convert_element_type x1 -> x0, other arithmetic: 15.9 us -> none  [beam_weights(): w_re = ((g_re * cosine + g_im * sine) * factor).astype(jnp.bfloat16)]
    ppermute x3 -> x11, starting transfers between devices: 1.7 us -> 15 us  [partner(): return lax.ppermute(value, axes, pairs)]
    all_to_all x1 -> x0, waiting for transfers between devices: 7.65 us -> none  [shards(): lax.all_to_all(voltages, 'chan', split_axis=3, concat_axis=1, tiled=True)]
    gather x5 -> x0, local copies, waits for them, and re-layouts: 7.11 us -> none  [the longest x4 4.3 us: one_row(): return lax.dynamic_slice_in_dim(row, length - shift, length, 0)]
    all_to_all x1 -> x0, starting transfers between devices: 6.45 us -> none  [shards(): lax.all_to_all(voltages, 'chan', split_axis=3, concat_axis=1, tiled=True)]
    dot_general x1 -> x0, matrix products: 5.44 us -> none  [shards(): jnp.einsum('pacn,cpaq->cnq', flat, weights, preferred_element_type=jnp.fl...]
  transfers between devices with their start and end apart: 4 -> 11, of which waited for: 4 -> 5; matrix products, arithmetic and copies ran while one was open for 43% -> 2% of each run, Pallas kernels for 0% -> 28%
where the time goes in v3:
time: 46.7 us; the launch traced here: 46.4 us
  Pallas kernels  16.8 us (36%)
  starting transfers between devices  15 us (32%)
  waiting for transfers between devices  13.7 us (29%)
  local copies, waits for them, and re-layouts  0.8 us (2%)
    ppermute x11, starting transfers between devices, partner(): return lax.ppermute(value, axes, pairs)  15 us
    ppermute x11, waiting for transfers between devices, partner(): return lax.ppermute(value, axes, pairs)  13.7 us
    pallas_call x1, Pallas kernels, our_weights(): pl.pallas_call(kernel, in_specs=[SMEM] + [VMEM] * 4, out_specs=[VMEM] * 3...  4.55 us
    pallas_call x3, Pallas kernels, split_channels(): pl.pallas_call(kernel, in_specs=[pl.BlockSpec(memory_space=place)] + [pl....  3.6 us
    pallas_call x1, Pallas kernels, their_weights(): pl.pallas_call(kernel, in_specs=[VMEM] * 3, out_specs=VMEM, out_shape=jax...  3.2 us
    pallas_call x1, Pallas kernels, early_beams(): pl.pallas_call(kernel, in_specs=[VMEM] * (2 + len(chunks)), out_specs=VME...  2.32 us
    pallas_call x1, Pallas kernels, last_levels(): pl.pallas_call(kernel, in_specs=[VMEM] * 4, out_specs=[VMEM] * 3, out_sha...  1.46 us
    pallas_call x2, Pallas kernels, tree_step(): pl.pallas_call(kernel, in_specs=[VMEM] * (1 + len(states)), out_specs=[VM...  1 us
  transfers between devices with their start and end apart: 11, of which 5 were waited for; matrix products, arithmetic and copies ran while one was open for 2% of the time, Pallas kernels for 28%

profile of v3, /device:TPU:0, one launch (start us, length us, event | category | flops | bytes accessed | tf_op | source)
XLA Modules:
  0.0 46.4 jit_solution(9651297449179263265)
XLA Ops:
  0.0 1.3 %split_channels.3.refs_0_ = bf16[2,64,256]{2,1,0:T(8,128)(2,1)S(1)} custom-call(bf16[2,2048,256]{2,1,0:T(8,128)(2,1)} %bitcast.4), custom_call_target="tpu_custom_call" | custom-call | tf_op jit(solution)/shard_map/split_channels/pallas_call | solution.py:78
  1.4 4.1 %collective-permute-start.3 = (bf16[2,64,256]{2,1,0:T(8,128)(2,1)S(1)}, bf16[2,64,256]{2,1,0:T(8,128)(2,1)S(1)}, u32[]{:S(2)}, u32[]{:S(2)}) collective-permute-start(bf16[2,64,256]{2,1,0:T(8,128)(2,1)S(1)} %split_channels.3.refs_0_), channel_id=1, source_target_pairs={{0,8},{4,12},{8,0},{12,4},{1,9},{5,13},{9,1},{13,5},{2,10},{6,14},... | collective-permute-start | bytes 196616 | tf_op jit(solution)/shard_map/ppermute | solution.py:29
  5.5 1.1 %split_channels.4 = (bf16[2,256,256]{2,1,0:T(8,128)(2,1)S(1)}, bf16[2,192,256]{2,1,0:T(8,128)(2,1)}) custom-call(bf16[2,2048,256]{2,1,0:T(8,128)(2,1)S(1)} %bitcast.5, bf16[2,64,256]{2,1,0:T(8,128)(2,1)S(1)} %split_channels.3.refs_0_), custom_call_target="tpu_custom_call" | custom-call | tf_op jit(solution)/shard_map/split_channels/pallas_call | solution.py:78
  6.6 1.5 %collective-permute-start.2 = (bf16[2,256,256]{2,1,0:T(8,128)(2,1)S(1)}, bf16[2,256,256]{2,1,0:T(8,128)(2,1)S(1)}, u32[]{:S(2)}, u32[]{:S(2)}) collective-permute-start(bf16[2,256,256]{2,1,0:T(8,128)(2,1)S(1)} %get-tuple-element.24.refs_0_), channel_id=1, source_target_pairs={{0,12},{4,8},{8,4},{12,0},{1,13},{5,9},{9,5},{13,1},{2,14},{6,10},... | collective-permute-start | bytes 786440 | tf_op jit(solution)/shard_map/ppermute | solution.py:29
  8.1 1.2 %split_channels.5 = (bf16[2,256,256]{2,1,0:T(8,128)(2,1)S(1)}, bf16[2,256,256]{2,1,0:T(8,128)(2,1)}) custom-call(bf16[2,2048,256]{2,1,0:T(8,128)(2,1)S(1)} %bitcast.6, bf16[2,256,256]{2,1,0:T(8,128)(2,1)S(1)} %get-tuple-element.24.refs_0_), custom_call_target="tpu_custom_call" | custom-call | tf_op jit(solution)/shard_map/split_channels/pallas_call | solution.py:78
  9.3 0.2 collective-permute-start.1
  9.5 2.8 %collective-permute-start.4 = (bf16[2,192,256]{2,1,0:T(8,128)(2,1)}, bf16[2,192,256]{2,1,0:T(8,128)(2,1)S(1)}, u32[]{:S(2)}, u32[]{:S(2)}) collective-permute-start(bf16[2,192,256]{2,1,0:T(8,128)(2,1)} %get-tuple-element.37), channel_id=1, source_target_pairs={{0,8},{4,12},{8,0},{12,4},{1,9},{5,13},{9,1},{13,5},{2,10},{6,14},... | collective-permute-start | bytes 589832 | tf_op jit(solution)/shard_map/ppermute | solution.py:29
  12.3 4.5 %our_weights.1 = (bf16[2,512,1024]{2,1,0:T(8,128)(2,1)S(1)}, bf16[32,1024]{1,0:T(8,128)(2,1)S(1)}, f32[1,1024]{1,0:T(1,128)S(1)}) custom-call(s32[16]{0:T(128)S(1)} %copy-done.4, f32[3,1024]{1,0:T(4,128)S(1)} %copy-done.1, s32[1,1024]{1,0:T(1,128)S(1)} %bitcast.8, f32[2,2,1024]{2,1,0:T(2,128)S(1)} %bitcast.7, f32[3,512]{1,0:T(4,128)} %dir_ref.1), custom_call_target="tpu_custom_call" | custom-call | flops 10000000000 | bytes 100000000 | tf_op jit(solution)/shard_map/our_weights/pallas_call | solution.py:197
  17.0 0.8 %reshape.16.delay_ref = s32[4,16]{1,0:T(4,128)S(1)} reshape(s32[4,2,8]{2,1,0:T(2,128)} %param.13) | data formatting | bytes 512 | tf_op jit(solution)/shard_map/reshape | solution.py:415
  17.7 0.6 %tree_maps.1 = (bf16[2,32,160]{2,1,0:T(8,128)(2,1)S(1)}, bf16[2,32,160]{2,1,0:T(8,128)(2,1)S(1)}) custom-call(s32[4,16]{1,0:T(4,128)S(1)} %reshape.16.delay_ref), custom_call_target="tpu_custom_call" | custom-call | tf_op jit(solution)/shard_map/tree_maps/pallas_call | solution.py:348
  18.4 3.2 %their_weights.1.theirs_ref = bf16[2,512,1024]{2,1,0:T(8,128)(2,1)S(1)} custom-call(bf16[32,1024]{1,0:T(8,128)(2,1)S(1)} %get-tuple-element.28.right_ref, f32[1,1024]{1,0:T(1,128)S(1)} %get-tuple-element.29.length_ref, f32[3,512]{1,0:T(4,128)S(1)} %collective-permute-done.dir_ref), custom_call_target="tpu_custom_call" | custom-call | tf_op jit(solution)/shard_map/their_weights/pallas_call | solution.py:223
  21.6 1.1 %collective-permute-done.1.refs_1_ = bf16[2,256,256]{2,1,0:T(8,128)(2,1)S(1)} collective-permute-done((bf16[2,256,256]{2,1,0:T(8,128)(2,1)}, bf16[2,256,256]{2,1,0:T(8,128)(2,1)S(1)}, u32[]{:S(2)}, u32[]{:S(2)}) %collective-permute-start.1) | collective-permute-done | bytes 262176 | tf_op jit(solution)/shard_map/ppermute | solution.py:29
  22.7 2.3 %early_beams.1.part_ref = f32[1024,512]{1,0:T(8,128)S(1)} custom-call(bf16[2,512,1024]{2,1,0:T(8,128)(2,1)S(1)} %get-tuple-element.27.ours_ref, bf16[2,512,1024]{2,1,0:T(8,128)(2,1)S(1)} %their_weights.1.theirs_ref, bf16[2,256,256]{2,1,0:T(8,128)(2,1)S(1)} %get-tuple-element.25.refs_0_, bf16[2,256,256]{2,1,0:T(8,128)(2,1)S(1)} %collective-permute-done.1.refs_1_, ...), custom_call_target="tpu_custom_call" | custom-call | tf_op jit(solution)/shard_map/early_beams/pallas_call | solution.py:265
  25.0 4.5 %collective-permute-done.4.chunk_ref = bf16[2,192,256]{2,1,0:T(8,128)(2,1)S(1)} collective-permute-done((bf16[2,192,256]{2,1,0:T(8,128)(2,1)}, bf16[2,192,256]{2,1,0:T(8,128)(2,1)S(1)}, u32[]{:S(2)}, u32[]{:S(2)}) %collective-permute-start.4) | collective-permute-done | bytes 196640 | tf_op jit(solution)/shard_map/ppermute | solution.py:29
  29.5 1.5 %last_levels.1 = (bf16[32,512]{1,0:T(8,128)(2,1)S(1)}, bf16[32,512]{1,0:T(8,128)(2,1)S(1)}, bf16[32,512]{1,0:T(8,128)(2,1)S(1)}) custom-call(bf16[2,512,1024]{2,1,0:T(8,128)(2,1)S(1)} %get-tuple-element.27.ours_ref, bf16[2,512,1024]{2,1,0:T(8,128)(2,1)S(1)} %their_weights.1.theirs_ref, f32[1024,512]{1,0:T(8,128)S(1)} %early_beams.1.part_ref, ...), custom_call_target="tpu_custom_call" | custom-call | tf_op jit(solution)/shard_map/last_levels/pallas_call | solution.py:308
  31.1 1.8 %collective-permute-start.7 = (bf16[32,512]{1,0:T(8,128)(2,1)S(1)}, bf16[32,512]{1,0:T(8,128)(2,1)S(1)}, u32[]{:S(2)}, u32[]{:S(2)}) collective-permute-start(bf16[32,512]{1,0:T(8,128)(2,1)S(1)} %get-tuple-element.40), channel_id=1, source_target_pairs={{0,5},{1,4},{4,1},{5,0},{8,13},{9,12},{12,9},{13,8},{2,7},{3,6},{6... | collective-permute-start | bytes 98312 | tf_op jit(solution)/shard_map/ppermute | solution.py:29
  32.9 2.3 %collective-permute-done.6.refs_3_ = bf16[32,512]{1,0:T(8,128)(2,1)S(1)} collective-permute-done((bf16[32,512]{1,0:T(8,128)(2,1)S(1)}, bf16[32,512]{1,0:T(8,128)(2,1)S(1)}, u32[]{:S(2)}, u32[]{:S(2)}) %collective-permute-start.6) | collective-permute-done | bytes 32800 | tf_op jit(solution)/shard_map/ppermute | solution.py:29
  35.1 0.2 tree_step.2
  35.3 3.5 %collective-permute-start.10 = (bf16[2,32,512]{2,1,0:T(8,128)(2,1)S(1)}, bf16[2,32,512]{2,1,0:T(8,128)(2,1)S(1)}, u32[]{:S(2)}, u32[]{:S(2)}) collective-permute-start(bf16[2,32,512]{2,1,0:T(8,128)(2,1)S(1)} %get-tuple-element.41.refs_0_), channel_id=1, source_target_pairs={{0,10},{2,8},{4,14},{6,12},{8,2},{10,0},{12,6},{14,4},{1,11},{3,9}... | collective-permute-start | bytes 196616 | tf_op jit(solution)/shard_map/ppermute | solution.py:29
  38.9 0.4 collective-permute-start.8
  39.2 0.5 %collective-permute-start.9 = (bf16[2,32,512]{2,1,0:T(8,128)(2,1)S(1)}, bf16[2,32,512]{2,1,0:T(8,128)(2,1)S(1)}, u32[]{:S(2)}, u32[]{:S(2)}) collective-permute-start(bf16[2,32,512]{2,1,0:T(8,128)(2,1)S(1)} %get-tuple-element.41.refs_0_), channel_id=1, source_target_pairs={{0,2},{2,0},{1,3},{3,1},{4,6},{6,4},{5,7},{7,5},{8,10},{10,8},{9,1... | collective-permute-start | bytes 196616 | tf_op jit(solution)/shard_map/ppermute | solution.py:29
  39.8 5.0 %collective-permute-done.10.refs_4_ = bf16[2,32,512]{2,1,0:T(8,128)(2,1)S(1)} collective-permute-done((bf16[2,32,512]{2,1,0:T(8,128)(2,1)S(1)}, bf16[2,32,512]{2,1,0:T(8,128)(2,1)S(1)}, u32[]{:S(2)}, u32[]{:S(2)}) %collective-permute-start.10) | collective-permute-done | bytes 65568 | tf_op jit(solution)/shard_map/ppermute | solution.py:29
  44.7 0.9 %collective-permute-done.8.refs_2_ = bf16[2,32,512]{2,1,0:T(8,128)(2,1)S(1)} collective-permute-done((bf16[2,32,512]{2,1,0:T(8,128)(2,1)S(1)}, bf16[2,32,512]{2,1,0:T(8,128)(2,1)S(1)}, u32[]{:S(2)}, u32[]{:S(2)}) %collective-permute-start.8) | collective-permute-done | bytes 65568 | tf_op jit(solution)/shard_map/ppermute | solution.py:29
  45.6 0.8 %tree_step.3 = f32[2,32,512]{2,1,0:T(8,128)} custom-call(bf16[2,32,160]{2,1,0:T(8,128)(2,1)S(1)} %get-tuple-element.34.map_ref, bf16[2,32,512]{2,1,0:T(8,128)(2,1)S(1)} %get-tuple-element.41.refs_0_, bf16[2,32,512]{2,1,0:T(8,128)(2,1)S(1)} %get-tuple-element.42.refs_1_, bf16[2,32,512]{2,1,0:T(8,128)(2,1)S(1)} %collective-permute-done.8.refs_2_, ...), custom_call_target="tpu_custom_call" | custom-call | tf_op jit(solution)/shard_map/tree_step/pallas_call | solution.py:371
  (19 shorter events, 0.2 us)
Async XLA Ops:
  0.0 5.5 %copy-start = (bf16[2,256,1,8,256]{4,3,2,1,0:T(8,128)(2,1)S(1)}, bf16[2,256,1,8,256]{4,3,2,1,0:T(8,128)(2,1)}, u32[]{:S(2)}) copy-start(bf16[2,256,1,8,256]{4,3,2,1,0:T(8,128)(2,1)} %param.7) | copy-start | bytes 6291460
  1.3 11.0 %copy-start.1 = (f32[3,1024]{1,0:T(4,128)S(1)}, f32[3,1024]{1,0:T(4,128)}, u32[]{:S(2)}) copy-start(f32[3,1024]{1,0:T(4,128)} %pos_ref) | copy-start | bytes 36868
  1.3 11.0 %copy-start.2 = (f32[2,1,2,1024]{3,2,1,0:T(2,128)S(1)}, f32[2,1,2,1024]{3,2,1,0:T(2,128)}, u32[]{:S(2)}) copy-start(f32[2,1,2,1024]{3,2,1,0:T(2,128)} %param.8) | copy-start | bytes 49156
  1.3 11.0 %copy-start.3 = (s32[1024]{0:T(1024)S(1)}, s32[1024]{0:T(1024)}, u32[]{:S(2)}) copy-start(s32[1024]{0:T(1024)} %param.11) | copy-start | bytes 12292
  1.3 11.0 %copy-start.4 = (s32[16]{0:T(128)S(1)}, s32[16]{0:T(128)}, u32[]{:S(2)}) copy-start(s32[16]{0:T(128)} %order_ref.1) | copy-start | bytes 196
  1.4 20.2 %collective-permute-start.3 = (bf16[2,64,256]{2,1,0:T(8,128)(2,1)S(1)}, bf16[2,64,256]{2,1,0:T(8,128)(2,1)S(1)}, u32[]{:S(2)}, u32[]{:S(2)}) collective-permute-start(bf16[2,64,256]{2,1,0:T(8,128)(2,1)S(1)} %split_channels.3.refs_0_), channel_id=1, source_target_pairs={{0,8},{4,12},{8,0},{12,4},{1,9},{5,13},{9,1},{13,5},{2,10},{6,14},... | collective-permute-start | bytes 196616 | tf_op jit(solution)/shard_map/ppermute | solution.py:29
  6.6 16.1 %collective-permute-start.2 = (bf16[2,256,256]{2,1,0:T(8,128)(2,1)S(1)}, bf16[2,256,256]{2,1,0:T(8,128)(2,1)S(1)}, u32[]{:S(2)}, u32[]{:S(2)}) collective-permute-start(bf16[2,256,256]{2,1,0:T(8,128)(2,1)S(1)} %get-tuple-element.24.refs_0_), channel_id=1, source_target_pairs={{0,12},{4,8},{8,4},{12,0},{1,13},{5,9},{9,5},{13,1},{2,14},{6,10},... | collective-permute-start | bytes 786440 | tf_op jit(solution)/shard_map/ppermute | solution.py:29
  9.3 13.4 %collective-permute-start.1 = (bf16[2,256,256]{2,1,0:T(8,128)(2,1)}, bf16[2,256,256]{2,1,0:T(8,128)(2,1)S(1)}, u32[]{:S(2)}, u32[]{:S(2)}) collective-permute-start(bf16[2,256,256]{2,1,0:T(8,128)(2,1)} %get-tuple-element.31), channel_id=1, source_target_pairs={{0,4},{4,0},{8,12},{12,8},{1,5},{5,1},{9,13},{13,9},{2,6},{6,2},{1... | collective-permute-start | bytes 786440 | tf_op jit(solution)/shard_map/ppermute | solution.py:29
  9.5 20.0 %collective-permute-start.4 = (bf16[2,192,256]{2,1,0:T(8,128)(2,1)}, bf16[2,192,256]{2,1,0:T(8,128)(2,1)S(1)}, u32[]{:S(2)}, u32[]{:S(2)}) collective-permute-start(bf16[2,192,256]{2,1,0:T(8,128)(2,1)} %get-tuple-element.37), channel_id=1, source_target_pairs={{0,8},{4,12},{8,0},{12,4},{1,9},{5,13},{9,1},{13,5},{2,10},{6,14},... | collective-permute-start | bytes 589832 | tf_op jit(solution)/shard_map/ppermute | solution.py:29
  16.9 1.5 %collective-permute-start = (f32[3,512]{1,0:T(4,128)}, f32[3,512]{1,0:T(4,128)S(1)}, u32[]{:S(2)}, u32[]{:S(2)}) collective-permute-start(f32[3,512]{1,0:T(4,128)} %dir_ref.1), channel_id=1, source_target_pairs={{0,1},{1,0},{2,3},{3,2},{4,5},{5,4},{6,7},{7,6},{8,9},{9,8},{10,11... | collective-permute-start | bytes 18440 | tf_op jit(solution)/shard_map/ppermute | solution.py:29
  30.9 1.9 %collective-permute-start.5 = (bf16[32,512]{1,0:T(8,128)(2,1)S(1)}, bf16[32,512]{1,0:T(8,128)(2,1)S(1)}, u32[]{:S(2)}, u32[]{:S(2)}) collective-permute-start(bf16[32,512]{1,0:T(8,128)(2,1)S(1)} %get-tuple-element.40), channel_id=1, source_target_pairs={{0,1},{1,0},{2,3},{3,2},{4,5},{5,4},{6,7},{7,6},{8,9},{9,8},{10,11... | collective-permute-start | bytes 98312 | tf_op jit(solution)/shard_map/ppermute | solution.py:29
  31.0 4.2 %collective-permute-start.6 = (bf16[32,512]{1,0:T(8,128)(2,1)S(1)}, bf16[32,512]{1,0:T(8,128)(2,1)S(1)}, u32[]{:S(2)}, u32[]{:S(2)}) collective-permute-start(bf16[32,512]{1,0:T(8,128)(2,1)S(1)} %get-tuple-element.38.refs_0_), channel_id=1, source_target_pairs={{0,4},{4,0},{8,12},{12,8},{1,5},{5,1},{9,13},{13,9},{2,6},{6,2},{1... | collective-permute-start | bytes 98312 | tf_op jit(solution)/shard_map/ppermute | solution.py:29
  31.1 4.1 %collective-permute-start.7 = (bf16[32,512]{1,0:T(8,128)(2,1)S(1)}, bf16[32,512]{1,0:T(8,128)(2,1)S(1)}, u32[]{:S(2)}, u32[]{:S(2)}) collective-permute-start(bf16[32,512]{1,0:T(8,128)(2,1)S(1)} %get-tuple-element.40), channel_id=1, source_target_pairs={{0,5},{1,4},{4,1},{5,0},{8,13},{9,12},{12,9},{13,8},{2,7},{3,6},{6... | collective-permute-start | bytes 98312 | tf_op jit(solution)/shard_map/ppermute | solution.py:29
  35.3 9.4 %collective-permute-start.10 = (bf16[2,32,512]{2,1,0:T(8,128)(2,1)S(1)}, bf16[2,32,512]{2,1,0:T(8,128)(2,1)S(1)}, u32[]{:S(2)}, u32[]{:S(2)}) collective-permute-start(bf16[2,32,512]{2,1,0:T(8,128)(2,1)S(1)} %get-tuple-element.41.refs_0_), channel_id=1, source_target_pairs={{0,10},{2,8},{4,14},{6,12},{8,2},{10,0},{12,6},{14,4},{1,11},{3,9}... | collective-permute-start | bytes 196616 | tf_op jit(solution)/shard_map/ppermute | solution.py:29
  38.9 6.8 %collective-permute-start.8 = (bf16[2,32,512]{2,1,0:T(8,128)(2,1)S(1)}, bf16[2,32,512]{2,1,0:T(8,128)(2,1)S(1)}, u32[]{:S(2)}, u32[]{:S(2)}) collective-permute-start(bf16[2,32,512]{2,1,0:T(8,128)(2,1)S(1)} %get-tuple-element.41.refs_0_), channel_id=1, source_target_pairs={{0,8},{4,12},{8,0},{12,4},{1,9},{5,13},{9,1},{13,5},{2,10},{6,14},... | collective-permute-start | bytes 196616 | tf_op jit(solution)/shard_map/ppermute | solution.py:29
  39.2 6.4 %collective-permute-start.9 = (bf16[2,32,512]{2,1,0:T(8,128)(2,1)S(1)}, bf16[2,32,512]{2,1,0:T(8,128)(2,1)S(1)}, u32[]{:S(2)}, u32[]{:S(2)}) collective-permute-start(bf16[2,32,512]{2,1,0:T(8,128)(2,1)S(1)} %get-tuple-element.41.refs_0_), channel_id=1, source_target_pairs={{0,2},{2,0},{1,3},{3,1},{4,6},{6,4},{5,7},{7,5},{8,10},{10,8},{9,1... | collective-permute-start | bytes 196616 | tf_op jit(solution)/shard_map/ppermute | solution.py:29

commit v4 on v3

--- a/solution.py
+++ b/solution.py
@@ -253,7 +253,7 @@
 def early_beams(weights, chunks, rest):
     half = weights[0].shape[1]
     samples = chunks[0].shape[2]
-    step = min(half, 256)
+    step = min(half, 512)
 
     def kernel(ours_ref, theirs_ref, *refs):
         blocks = [filled(ref, 0, 0) for ref in refs[:-2]] + [filled(refs[-2], 0, rest)]
@@ -282,7 +282,7 @@
     _, half, ants = weights[0].shape
     samples = chunk.shape[2]
     bins = samples // INTEG
-    step = min(half, 256)
+    step = min(half, 512)
     first = ants - chunk.shape[1] - done
 
     def kernel(ours_ref, theirs_ref, part_ref, chunk_ref, high_ref, low_ref, sent_ref):
@@ -315,9 +315,13 @@
     )(*weights, partial, chunk)
 
 
-def tree_maps(delays, steps, bins, in_band):
+def subsets(bits):
+    return [[bit for k, bit in enumerate(bits) if pick >> k & 1] for pick in range(1 << len(bits))]
+
+
+def tree_maps(delays, stages, bins, in_band):
     per_dev = lax.axis_size("beam")
-    sources = [[0] + list(range(1 << len(bits))) for bits in steps]
+    shapes = [(per_dev, bins << len(sent), bins * (1 + (1 << len(got)))) for _, got, sent in stages]
 
     def kernel(delay_ref, *outs):
         def place(flips):
@@ -326,56 +330,82 @@
                 at[axis] = at[axis] ^ (1 << bit)
             return at
 
-        round_no = 0
-        for bits, srcs, out in zip(steps, sources, outs):
-            row = lax.broadcasted_iota(jnp.int32, out.shape[1:], 0)
-            col = lax.broadcasted_iota(jnp.int32, out.shape[1:], 1)
+        def total_delay(bits, first_round, target, source, slot):
+            moved = 0
+            for k, (axis, bit) in enumerate(bits):
+                later = [b for b in bits[k + 1 :] if b in target or b in source]
+                end = place(target + later)
+                start = place(target + later + [b for b in bits[k : k + 1] if b in target or b in source])
+                delay = delay_ref[first_round + k, end["band"] * in_band + end["chan"] * per_dev + slot]
+                moved = moved + ((start[axis] >> bit) & 1) * delay
+            return moved
+
+        first_round = 0
+        for (bits, got, sent), out in zip(stages, outs):
+            sources = [[]] + subsets(got)
+            shape = (bins, out.shape[2])
+            row = lax.broadcasted_iota(jnp.int32, shape, 0)
+            col = lax.broadcasted_iota(jnp.int32, shape, 1)
             for slot in range(per_dev):
-                shift = jnp.zeros_like(col)
-                for number, source in enumerate(srcs):
-                    moved = 0
-                    for k, (axis, bit) in enumerate(bits):
-                        later = [bits[j] for j in range(k + 1, len(bits)) if source >> j & 1]
-                        end = place(later)
-                        start = place(later + ([bits[k]] if source >> k & 1 else []))
-                        delay = delay_ref[round_no + k, end["band"] * in_band + end["chan"] * per_dev + slot]
-                        moved = moved + ((start[axis] >> bit) & 1) * delay
-                    shift = jnp.where(col // bins == number, moved, shift)
-                hit = lax.rem(row - col + len(bits) * bins + out.shape[2] - shift, bins) == 0
-                out[slot] = jnp.where(hit, 1.0, 0.0).astype(jnp.bfloat16)
-            round_no += len(bits)
+                for number, target in enumerate(subsets(sent)):
+                    shift = jnp.zeros_like(col)
+                    for place_no, source in enumerate(sources):
+                        moved = total_delay(bits, first_round, target, source, slot)
+                        shift = jnp.where(col // bins == place_no, moved, shift)
+                    hit = lax.rem(row - col + len(bits) * bins + shape[1] - shift, bins) == 0
+                    out[slot, pl.ds(number * bins, bins), :] = jnp.where(hit, 1.0, 0.0).astype(jnp.bfloat16)
+            first_round += len(bits)
 
     return pl.pallas_call(
         kernel,
         in_specs=[SMEM],
-        out_specs=[VMEM] * len(steps),
-        out_shape=[jax.ShapeDtypeStruct((per_dev, bins, len(srcs) * bins), jnp.bfloat16) for srcs in sources],
+        out_specs=[VMEM] * len(stages),
+        out_shape=[jax.ShapeDtypeStruct(shape, jnp.bfloat16) for shape in shapes],
         compiler_params=PARAMS,
         name="tree_maps",
     )(delays)
 
 
-def tree_step(matrix, states, final):
-    slots, bins, _ = matrix.shape
+def tree_stage(matrix, states, bins, final):
+    slots, rows, _ = matrix.shape
     width = states[0].shape[-1]
+    targets = rows // bins
+    dtypes = [jnp.float32] + [jnp.bfloat16] * (targets - 1) if final else [jnp.bfloat16] * 2
 
     def kernel(map_ref, *refs):
         ins, outs = refs[: len(states)], refs[len(states) :]
         for slot in range(slots):
             column = [ref[...] if len(ref.shape) == 2 else ref[slot] for ref in ins]
             value = jnp.dot(map_ref[slot], jnp.concatenate(column, axis=0), preferred_element_type=jnp.float32)
-            for out, part in zip(outs, [value] if final else two_parts(value)):
-                out[slot] = part
-
-    dtypes = [jnp.float32] if final else [jnp.bfloat16] * 2
+            parts = [value[t * bins : t * bins + bins] for t in range(targets)] if final else two_parts(value)
+            for out, part in zip(outs, parts):
+                out[slot] = part.astype(out.dtype)
+
     return pl.pallas_call(
         kernel,
         in_specs=[VMEM] * (1 + len(states)),
         out_specs=[VMEM] * len(dtypes),
         out_shape=[jax.ShapeDtypeStruct((slots, bins, width), dtype) for dtype in dtypes],
         compiler_params=PARAMS,
-        name="tree_step",
+        name="tree_stage",
     )(matrix, *states)
+
+
+def tree_sum(values):
+    def kernel(*refs):
+        total = refs[0][...]
+        for ref in refs[1:-1]:
+            total = total + ref[...].astype(jnp.float32)
+        refs[-1][...] = total
+
+    return pl.pallas_call(
+        kernel,
+        in_specs=[VMEM] * len(values),
+        out_specs=VMEM,
+        out_shape=jax.ShapeDtypeStruct(values[0].shape, jnp.float32),
+        compiler_params=PARAMS,
+        name="tree_sum",
+    )(*values)
 
 
 def shards(voltages, gains, positions, directions, antenna_row_lookup, chan_order, delays):
@@ -392,10 +422,11 @@
     near = list(range(middle))
     distant = list(range(chan_count - 1, middle, -1))
     masks = near + distant + [middle]
-    cut = ants // 4
-    first = split_channels(voltages, [(middle, 0, cut)], True)
-    across = split_channels(voltages, [(m, 0, ants) for m in distant] + [(middle, cut, ants)], False, first[0])
-    beside = split_channels(voltages, [(m, 0, ants) for m in near], False, across[0])
+    cut = ants // 2
+    first = list(split_channels(voltages, [(middle, 0, cut)], True))
+    copied, first[0] = lax.optimization_barrier((voltages, first[0]))
+    across = split_channels(copied, [(m, 0, ants) for m in distant] + [(middle, cut, ants)], False, first[0])
+    beside = split_channels(copied, [(m, 0, ants) for m in near], False, across[0])
     first = [chan_partner(first[0], middle)]
     across = [chan_partner(v, m) for v, m in zip(across, distant + [middle])]
     chunks = [beside[0]] + [chan_partner(v, m) for v, m in zip(beside[1:], near[1:])]
@@ -411,21 +442,24 @@
     bits = [("beam", 0)]
     for axis, count in (("chan", chan_count), ("band", band_count)):
         bits += [(axis, bit) for bit in range(count.bit_length() - 1)]
-    steps = [bits[i : i + 2] for i in range(0, len(bits), 2)]
-    maps = tree_maps(delays.reshape(delays.shape[0], total), steps, bins, in_band)
+    last = bits[-4:]
+    got = [bit for bit in last if bit in (("beam", 0), ("chan", chan_count.bit_length() - 2))]
+    got += [bit for bit in last[::-1] if bit not in got][: 2 - len(got)]
+    stages = [(pair, pair, []) for pair in (bits[i : i + 2] for i in range(0, len(bits) - 4, 2))]
+    stages.append((last, got, [bit for bit in last if bit not in got]))
+    maps = tree_maps(delays.reshape(delays.shape[0], total), stages, bins, in_band)
     partial, *maps = lax.optimization_barrier((partial, *maps))
 
     high, low, other = last_levels(weights, across[-1], cut, partial, total)
-    for number, (step, matrix) in enumerate(zip(steps, maps)):
+    for (_, got, sent), matrix in zip(stages, maps):
         states = [high, low]
-        for source in range(1, 1 << len(step)):
-            flips = [place for k, place in enumerate(step) if source >> k & 1]
+        for flips in subsets(got)[1:]:
             states.append(partner(other if ("beam", 0) in flips else high, flips))
-        if number == len(steps) - 1:
-            (state,) = tree_step(matrix, states, True)
-        else:
-            high, low = tree_step(matrix, states, False)
-    return state.reshape(1, per_dev, bins, state.shape[2])
+        result = tree_stage(matrix, states, bins, bool(sent))
+        if not sent:
+            high, low = result
+    sums = [result[0]] + [partner(value, flips) for value, flips in zip(result[1:], subsets(sent)[1:])]
+    return tree_sum(sums).reshape(1, per_dev, bins, high.shape[-1])
 
 
 def solution(mesh):

time: 46.7 us -> 45 us (0.964)
  waiting for transfers between devices: 13.7 us -> 10.8 us
  local copies, waits for them, and re-layouts: 0.8 us -> 2.24 us
    ppermute x11, waiting for transfers between devices: 13.7 us -> 10.8 us  [partner(): return lax.ppermute(value, axes, pairs)]
    unnamed x10 -> x14, local copies, waits for them, and re-layouts: 0.03 us -> 1.47 us
  transfers between devices with their start and end apart: 11 -> 11, of which waited for: 5 -> 6; matrix products, arithmetic and copies ran while one was open for 2% -> 2% of each run, Pallas kernels for 28% -> 29%
where the time goes in v4:
time: 45 us; the launch traced here: 44.8 us
  Pallas kernels  16.6 us (37%)
  starting transfers between devices  15 us (33%)
  waiting for transfers between devices  10.8 us (24%)
  local copies, waits for them, and re-layouts  2.24 us (5%)
    ppermute x11, starting transfers between devices, partner(): return lax.ppermute(value, axes, pairs)  15 us
    ppermute x11, waiting for transfers between devices, partner(): return lax.ppermute(value, axes, pairs)  10.8 us
    pallas_call x1, Pallas kernels, our_weights(): pl.pallas_call(kernel, in_specs=[SMEM] + [VMEM] * 4, out_specs=[VMEM] * 3...  4.55 us
    pallas_call x3, Pallas kernels, split_channels(): pl.pallas_call(kernel, in_specs=[pl.BlockSpec(memory_space=place)] + [pl....  3.78 us
    pallas_call x1, Pallas kernels, their_weights(): pl.pallas_call(kernel, in_specs=[VMEM] * 3, out_specs=VMEM, out_shape=jax...  3.2 us
    pallas_call x1, Pallas kernels, early_beams(): pl.pallas_call(kernel, in_specs=[VMEM] * (2 + len(chunks)), out_specs=VME...  2.33 us
    unnamed x14, local copies, waits for them, and re-layouts  1.47 us
    pallas_call x1, Pallas kernels, last_levels(): pl.pallas_call(kernel, in_specs=[VMEM] * 4, out_specs=[VMEM] * 3, out_sha...  1.12 us
  transfers between devices with their start and end apart: 11, of which 6 were waited for; matrix products, arithmetic and copies ran while one was open for 2% of the time, Pallas kernels for 29%

profile of v4, /device:TPU:0, one launch (start us, length us, event | category | flops | bytes accessed | tf_op | source)
XLA Modules:
  0.0 44.8 jit_solution(5108844025341696383)
XLA Ops:
  0.0 1.5 %split_channels.3.refs_0_ = bf16[2,128,256]{2,1,0:T(8,128)(2,1)S(1)} custom-call(bf16[2,2048,256]{2,1,0:T(8,128)(2,1)} %bitcast.5), custom_call_target="tpu_custom_call" | custom-call | tf_op jit(solution)/shard_map/split_channels/pallas_call | solution.py:78
  1.5 4.1 %collective-permute-start.3 = (bf16[2,128,256]{2,1,0:T(8,128)(2,1)S(1)}, bf16[2,128,256]{2,1,0:T(8,128)(2,1)S(1)}, u32[]{:S(2)}, u32[]{:S(2)}) collective-permute-start(bf16[2,128,256]{2,1,0:T(8,128)(2,1)S(1)} %split_channels.3.refs_0_), channel_id=1, source_target_pairs={{0,8},{4,12},{8,0},{12,4},{1,9},{5,13},{9,1},{13,5},{2,10},{6,14},... | collective-permute-start | bytes 393224 | tf_op jit(solution)/shard_map/ppermute | solution.py:29
  5.7 1.1 %split_channels.4 = (bf16[2,256,256]{2,1,0:T(8,128)(2,1)S(1)}, bf16[2,128,256]{2,1,0:T(8,128)(2,1)}) custom-call(bf16[2,2048,256]{2,1,0:T(8,128)(2,1)S(1)} %bitcast.6, bf16[2,128,256]{2,1,0:T(8,128)(2,1)S(1)} %split_channels.3.refs_0_), custom_call_target="tpu_custom_call" | custom-call | tf_op jit(solution)/shard_map/split_channels/pallas_call | solution.py:78
  6.7 1.5 %collective-permute-start.2 = (bf16[2,256,256]{2,1,0:T(8,128)(2,1)S(1)}, bf16[2,256,256]{2,1,0:T(8,128)(2,1)S(1)}, u32[]{:S(2)}, u32[]{:S(2)}) collective-permute-start(bf16[2,256,256]{2,1,0:T(8,128)(2,1)S(1)} %get-tuple-element.27.refs_0_), channel_id=1, source_target_pairs={{0,12},{4,8},{8,4},{12,0},{1,13},{5,9},{9,5},{13,1},{2,14},{6,10},... | collective-permute-start | bytes 786440 | tf_op jit(solution)/shard_map/ppermute | solution.py:29
  8.2 1.2 %split_channels.5 = (bf16[2,256,256]{2,1,0:T(8,128)(2,1)S(1)}, bf16[2,256,256]{2,1,0:T(8,128)(2,1)}) custom-call(bf16[2,2048,256]{2,1,0:T(8,128)(2,1)S(1)} %bitcast.7, bf16[2,256,256]{2,1,0:T(8,128)(2,1)S(1)} %get-tuple-element.27.refs_0_), custom_call_target="tpu_custom_call" | custom-call | tf_op jit(solution)/shard_map/split_channels/pallas_call | solution.py:78
  9.7 2.8 %collective-permute-start.4 = (bf16[2,128,256]{2,1,0:T(8,128)(2,1)}, bf16[2,128,256]{2,1,0:T(8,128)(2,1)S(1)}, u32[]{:S(2)}, u32[]{:S(2)}) collective-permute-start(bf16[2,128,256]{2,1,0:T(8,128)(2,1)} %get-tuple-element.37), channel_id=1, source_target_pairs={{0,8},{4,12},{8,0},{12,4},{1,9},{5,13},{9,1},{13,5},{2,10},{6,14},... | collective-permute-start | bytes 393224 | tf_op jit(solution)/shard_map/ppermute | solution.py:29
  12.5 4.5 %our_weights.1 = (bf16[2,512,1024]{2,1,0:T(8,128)(2,1)S(1)}, bf16[32,1024]{1,0:T(8,128)(2,1)S(1)}, f32[1,1024]{1,0:T(1,128)S(1)}) custom-call(s32[16]{0:T(128)S(1)} %copy-done.6, f32[3,1024]{1,0:T(4,128)S(1)} %copy-done.3, s32[1,1024]{1,0:T(1,128)S(1)} %bitcast.9, f32[2,2,1024]{2,1,0:T(2,128)S(1)} %bitcast.8, f32[3,512]{1,0:T(4,128)} %dir_ref.1), custom_call_target="tpu_custom_call" | custom-call | flops 10000000000 | bytes 100000000 | tf_op jit(solution)/shard_map/our_weights/pallas_call | solution.py:197
  17.0 0.6 %copy-done.1 = bf16[32,1024]{1,0:T(8,128)(2,1)} copy-done((bf16[32,1024]{1,0:T(8,128)(2,1)}, bf16[32,1024]{1,0:T(8,128)(2,1)S(1)}, u32[]{:S(2)}) %copy-start.1) | copy-done | bytes 65560
  17.7 0.8 %reshape.19.delay_ref = s32[4,16]{1,0:T(4,128)S(1)} reshape(s32[4,2,8]{2,1,0:T(2,128)} %param.13) | data formatting | bytes 512 | tf_op jit(solution)/shard_map/reshape | solution.py:450
  18.4 0.7 %tree_maps.1.map_ref = bf16[2,128,160]{2,1,0:T(8,128)(2,1)S(1)} custom-call(s32[4,16]{1,0:T(4,128)S(1)} %reshape.19.delay_ref), custom_call_target="tpu_custom_call" | custom-call | tf_op jit(solution)/shard_map/tree_maps/pallas_call | solution.py:359
  19.1 0.8 %copy-done.2 = bf16[32,1024]{1,0:T(8,128)(2,1)S(1)} copy-done((bf16[32,1024]{1,0:T(8,128)(2,1)S(1)}, bf16[32,1024]{1,0:T(8,128)(2,1)}, u32[]{:S(2)}) %copy-start.2) | copy-done | bytes 65560
  20.0 3.2 %their_weights.1.theirs_ref = bf16[2,512,1024]{2,1,0:T(8,128)(2,1)S(1)} custom-call(bf16[32,1024]{1,0:T(8,128)(2,1)S(1)} %copy-done.2, f32[1,1024]{1,0:T(1,128)S(1)} %get-tuple-element.32.length_ref, f32[3,512]{1,0:T(4,128)S(1)} %collective-permute-done.dir_ref), custom_call_target="tpu_custom_call" | custom-call | tf_op jit(solution)/shard_map/their_weights/pallas_call | solution.py:223
  23.2 2.3 %early_beams.1.part_ref = f32[1024,512]{1,0:T(8,128)S(1)} custom-call(bf16[2,512,1024]{2,1,0:T(8,128)(2,1)S(1)} %get-tuple-element.30.ours_ref, bf16[2,512,1024]{2,1,0:T(8,128)(2,1)S(1)} %their_weights.1.theirs_ref, bf16[2,256,256]{2,1,0:T(8,128)(2,1)S(1)} %get-tuple-element.28.refs_0_, bf16[2,256,256]{2,1,0:T(8,128)(2,1)S(1)} %collective-permute-done.1.refs_1_, ...), custom_call_target="tpu_custom_call" | custom-call | tf_op jit(solution)/shard_map/early_beams/pallas_call | solution.py:265
  25.5 3.3 %collective-permute-done.4.chunk_ref = bf16[2,128,256]{2,1,0:T(8,128)(2,1)S(1)} collective-permute-done((bf16[2,128,256]{2,1,0:T(8,128)(2,1)}, bf16[2,128,256]{2,1,0:T(8,128)(2,1)S(1)}, u32[]{:S(2)}, u32[]{:S(2)}) %collective-permute-start.4) | collective-permute-done | bytes 131104 | tf_op jit(solution)/shard_map/ppermute | solution.py:29
  28.8 1.1 %last_levels.1 = (bf16[32,512]{1,0:T(8,128)(2,1)S(1)}, bf16[32,512]{1,0:T(8,128)(2,1)S(1)}, bf16[32,512]{1,0:T(8,128)(2,1)S(1)}) custom-call(bf16[2,512,1024]{2,1,0:T(8,128)(2,1)S(1)} %get-tuple-element.30.ours_ref, bf16[2,512,1024]{2,1,0:T(8,128)(2,1)S(1)} %their_weights.1.theirs_ref, f32[1024,512]{1,0:T(8,128)S(1)} %early_beams.1.part_ref, ...), custom_call_target="tpu_custom_call" | custom-call | tf_op jit(solution)/shard_map/last_levels/pallas_call | solution.py:308
  30.0 2.3 %collective-permute-start.6 = (bf16[32,512]{1,0:T(8,128)(2,1)S(1)}, bf16[32,512]{1,0:T(8,128)(2,1)S(1)}, u32[]{:S(2)}, u32[]{:S(2)}) collective-permute-start(bf16[32,512]{1,0:T(8,128)(2,1)S(1)} %get-tuple-element.38.refs_0_), channel_id=1, source_target_pairs={{0,8},{4,12},{8,0},{12,4},{1,9},{5,13},{9,1},{13,5},{2,10},{6,14},... | collective-permute-start | bytes 98312 | tf_op jit(solution)/shard_map/ppermute | solution.py:29
  32.3 0.4 collective-permute-start.7
  32.8 2.1 %collective-permute-done.6.refs_3_ = bf16[32,512]{1,0:T(8,128)(2,1)S(1)} collective-permute-done((bf16[32,512]{1,0:T(8,128)(2,1)S(1)}, bf16[32,512]{1,0:T(8,128)(2,1)S(1)}, u32[]{:S(2)}, u32[]{:S(2)}) %collective-permute-start.6) | collective-permute-done | bytes 32800 | tf_op jit(solution)/shard_map/ppermute | solution.py:29
  34.9 1.7 %collective-permute-done.7.refs_4_ = bf16[32,512]{1,0:T(8,128)(2,1)S(1)} collective-permute-done((bf16[32,512]{1,0:T(8,128)(2,1)S(1)}, bf16[32,512]{1,0:T(8,128)(2,1)S(1)}, u32[]{:S(2)}, u32[]{:S(2)}) %collective-permute-start.7) | collective-permute-done | bytes 32800 | tf_op jit(solution)/shard_map/ppermute | solution.py:29
  36.8 2.8 %collective-permute-start.10 = (bf16[2,32,512]{2,1,0:T(8,128)(2,1)S(1)}, bf16[2,32,512]{2,1,0:T(8,128)(2,1)S(1)}, u32[]{:S(2)}, u32[]{:S(2)}) collective-permute-start(bf16[2,32,512]{2,1,0:T(8,128)(2,1)S(1)} %get-tuple-element.44), channel_id=1, source_target_pairs={{0,6},{2,4},{4,2},{6,0},{8,14},{10,12},{12,10},{14,8},{1,7},{3,5},... | collective-permute-start | bytes 196616 | tf_op jit(solution)/shard_map/ppermute | solution.py:29
  39.8 0.5 %collective-permute-start.9 = (bf16[2,32,512]{2,1,0:T(8,128)(2,1)S(1)}, bf16[2,32,512]{2,1,0:T(8,128)(2,1)S(1)}, u32[]{:S(2)}, u32[]{:S(2)}) collective-permute-start(bf16[2,32,512]{2,1,0:T(8,128)(2,1)S(1)} %get-tuple-element.43), channel_id=1, source_target_pairs={{0,2},{2,0},{1,3},{3,1},{4,6},{6,4},{5,7},{7,5},{8,10},{10,8},{9,1... | collective-permute-start | bytes 196616 | tf_op jit(solution)/shard_map/ppermute | solution.py:29
  40.4 1.7 %collective-permute-done.10.refs_3_ = bf16[2,32,512]{2,1,0:T(8,128)(2,1)S(1)} collective-permute-done((bf16[2,32,512]{2,1,0:T(8,128)(2,1)S(1)}, bf16[2,32,512]{2,1,0:T(8,128)(2,1)S(1)}, u32[]{:S(2)}, u32[]{:S(2)}) %collective-permute-start.10) | collective-permute-done | bytes 65568 | tf_op jit(solution)/shard_map/ppermute | solution.py:29
  42.1 1.8 %collective-permute-done.8.refs_1_ = bf16[2,32,512]{2,1,0:T(8,128)(2,1)S(1)} collective-permute-done((bf16[2,32,512]{2,1,0:T(8,128)(2,1)S(1)}, bf16[2,32,512]{2,1,0:T(8,128)(2,1)S(1)}, u32[]{:S(2)}, u32[]{:S(2)}) %collective-permute-start.8) | collective-permute-done | bytes 65568 | tf_op jit(solution)/shard_map/ppermute | solution.py:29
  44.1 0.7 %tree_sum.1 = f32[2,32,512]{2,1,0:T(8,128)} custom-call(f32[2,32,512]{2,1,0:T(8,128)S(1)} %get-tuple-element.41.refs_0_, bf16[2,32,512]{2,1,0:T(8,128)(2,1)S(1)} %collective-permute-done.8.refs_1_, bf16[2,32,512]{2,1,0:T(8,128)(2,1)S(1)} %collective-permute-done.9.refs_2_, bf16[2,32,512]{2,1,0:T(8,128)(2,1)S(1)} %collective-permute-done.10.refs_3_), custom_call_target="tpu_custom_call" | custom-call | tf_op jit(solution)/shard_map/tree_sum/pallas_call | solution.py:401
  (23 shorter events, 0.9 us)
Async XLA Ops:
  0.0 5.6 %copy-start = (bf16[2,256,1,8,256]{4,3,2,1,0:T(8,128)(2,1)S(1)}, bf16[2,256,1,8,256]{4,3,2,1,0:T(8,128)(2,1)}, u32[]{:S(2)}) copy-start(bf16[2,256,1,8,256]{4,3,2,1,0:T(8,128)(2,1)} %param.7) | copy-start | bytes 6291460
  1.5 21.7 %collective-permute-start.3 = (bf16[2,128,256]{2,1,0:T(8,128)(2,1)S(1)}, bf16[2,128,256]{2,1,0:T(8,128)(2,1)S(1)}, u32[]{:S(2)}, u32[]{:S(2)}) collective-permute-start(bf16[2,128,256]{2,1,0:T(8,128)(2,1)S(1)} %split_channels.3.refs_0_), channel_id=1, source_target_pairs={{0,8},{4,12},{8,0},{12,4},{1,9},{5,13},{9,1},{13,5},{2,10},{6,14},... | collective-permute-start | bytes 393224 | tf_op jit(solution)/shard_map/ppermute | solution.py:29
  5.6 6.8 %copy-start.3 = (f32[3,1024]{1,0:T(4,128)S(1)}, f32[3,1024]{1,0:T(4,128)}, u32[]{:S(2)}) copy-start(f32[3,1024]{1,0:T(4,128)} %pos_ref) | copy-start | bytes 36868
  5.6 6.8 %copy-start.4 = (f32[2,1,2,1024]{3,2,1,0:T(2,128)S(1)}, f32[2,1,2,1024]{3,2,1,0:T(2,128)}, u32[]{:S(2)}) copy-start(f32[2,1,2,1024]{3,2,1,0:T(2,128)} %param.8) | copy-start | bytes 49156
  5.6 6.8 %copy-start.5 = (s32[1024]{0:T(1024)S(1)}, s32[1024]{0:T(1024)}, u32[]{:S(2)}) copy-start(s32[1024]{0:T(1024)} %param.11) | copy-start | bytes 12292
  5.6 6.8 %copy-start.6 = (s32[16]{0:T(128)S(1)}, s32[16]{0:T(128)}, u32[]{:S(2)}) copy-start(s32[16]{0:T(128)} %order_ref.1) | copy-start | bytes 196
  6.7 16.5 %collective-permute-start.2 = (bf16[2,256,256]{2,1,0:T(8,128)(2,1)S(1)}, bf16[2,256,256]{2,1,0:T(8,128)(2,1)S(1)}, u32[]{:S(2)}, u32[]{:S(2)}) collective-permute-start(bf16[2,256,256]{2,1,0:T(8,128)(2,1)S(1)} %get-tuple-element.27.refs_0_), channel_id=1, source_target_pairs={{0,12},{4,8},{8,4},{12,0},{1,13},{5,9},{9,5},{13,1},{2,14},{6,10},... | collective-permute-start | bytes 786440 | tf_op jit(solution)/shard_map/ppermute | solution.py:29
  9.4 13.8 %collective-permute-start.1 = (bf16[2,256,256]{2,1,0:T(8,128)(2,1)}, bf16[2,256,256]{2,1,0:T(8,128)(2,1)S(1)}, u32[]{:S(2)}, u32[]{:S(2)}) collective-permute-start(bf16[2,256,256]{2,1,0:T(8,128)(2,1)} %get-tuple-element.34), channel_id=1, source_target_pairs={{0,4},{4,0},{8,12},{12,8},{1,5},{5,1},{9,13},{13,9},{2,6},{6,2},{1... | collective-permute-start | bytes 786440 | tf_op jit(solution)/shard_map/ppermute | solution.py:29
  9.7 19.2 %collective-permute-start.4 = (bf16[2,128,256]{2,1,0:T(8,128)(2,1)}, bf16[2,128,256]{2,1,0:T(8,128)(2,1)S(1)}, u32[]{:S(2)}, u32[]{:S(2)}) collective-permute-start(bf16[2,128,256]{2,1,0:T(8,128)(2,1)} %get-tuple-element.37), channel_id=1, source_target_pairs={{0,8},{4,12},{8,0},{12,4},{1,9},{5,13},{9,1},{13,5},{2,10},{6,14},... | collective-permute-start | bytes 393224 | tf_op jit(solution)/shard_map/ppermute | solution.py:29
  17.0 0.6 %copy-start.1 = (bf16[32,1024]{1,0:T(8,128)(2,1)}, bf16[32,1024]{1,0:T(8,128)(2,1)S(1)}, u32[]{:S(2)}) copy-start(bf16[32,1024]{1,0:T(8,128)(2,1)S(1)} %get-tuple-element.31.right_ref) | copy-start | bytes 196612
  17.6 1.5 %collective-permute-start = (f32[3,512]{1,0:T(4,128)}, f32[3,512]{1,0:T(4,128)S(1)}, u32[]{:S(2)}, u32[]{:S(2)}) collective-permute-start(f32[3,512]{1,0:T(4,128)} %dir_ref.1), channel_id=1, source_target_pairs={{0,1},{1,0},{2,3},{3,2},{4,5},{5,4},{6,7},{7,6},{8,9},{9,8},{10,11... | collective-permute-start | bytes 18440 | tf_op jit(solution)/shard_map/ppermute | solution.py:29
  19.1 0.8 %copy-start.2 = (bf16[32,1024]{1,0:T(8,128)(2,1)S(1)}, bf16[32,1024]{1,0:T(8,128)(2,1)}, u32[]{:S(2)}) copy-start(bf16[32,1024]{1,0:T(8,128)(2,1)} %copy-done.1) | copy-start | bytes 196612
  30.0 2.8 %collective-permute-start.5 = (bf16[32,512]{1,0:T(8,128)(2,1)S(1)}, bf16[32,512]{1,0:T(8,128)(2,1)S(1)}, u32[]{:S(2)}, u32[]{:S(2)}) collective-permute-start(bf16[32,512]{1,0:T(8,128)(2,1)S(1)} %get-tuple-element.40), channel_id=1, source_target_pairs={{0,1},{1,0},{2,3},{3,2},{4,5},{5,4},{6,7},{7,6},{8,9},{9,8},{10,11... | collective-permute-start | bytes 98312 | tf_op jit(solution)/shard_map/ppermute | solution.py:29
  30.0 4.9 %collective-permute-start.6 = (bf16[32,512]{1,0:T(8,128)(2,1)S(1)}, bf16[32,512]{1,0:T(8,128)(2,1)S(1)}, u32[]{:S(2)}, u32[]{:S(2)}) collective-permute-start(bf16[32,512]{1,0:T(8,128)(2,1)S(1)} %get-tuple-element.38.refs_0_), channel_id=1, source_target_pairs={{0,8},{4,12},{8,0},{12,4},{1,9},{5,13},{9,1},{13,5},{2,10},{6,14},... | collective-permute-start | bytes 98312 | tf_op jit(solution)/shard_map/ppermute | solution.py:29
  32.3 4.2 %collective-permute-start.7 = (bf16[32,512]{1,0:T(8,128)(2,1)S(1)}, bf16[32,512]{1,0:T(8,128)(2,1)S(1)}, u32[]{:S(2)}, u32[]{:S(2)}) collective-permute-start(bf16[32,512]{1,0:T(8,128)(2,1)S(1)} %get-tuple-element.40), channel_id=1, source_target_pairs={{0,9},{1,8},{4,13},{5,12},{8,1},{9,0},{12,5},{13,4},{2,11},{3,10},... | collective-permute-start | bytes 98312 | tf_op jit(solution)/shard_map/ppermute | solution.py:29
  36.8 5.3 %collective-permute-start.10 = (bf16[2,32,512]{2,1,0:T(8,128)(2,1)S(1)}, bf16[2,32,512]{2,1,0:T(8,128)(2,1)S(1)}, u32[]{:S(2)}, u32[]{:S(2)}) collective-permute-start(bf16[2,32,512]{2,1,0:T(8,128)(2,1)S(1)} %get-tuple-element.44), channel_id=1, source_target_pairs={{0,6},{2,4},{4,2},{6,0},{8,14},{10,12},{12,10},{14,8},{1,7},{3,5},... | collective-permute-start | bytes 196616 | tf_op jit(solution)/shard_map/ppermute | solution.py:29
  39.6 4.3 %collective-permute-start.8 = (bf16[2,32,512]{2,1,0:T(8,128)(2,1)S(1)}, bf16[2,32,512]{2,1,0:T(8,128)(2,1)S(1)}, u32[]{:S(2)}, u32[]{:S(2)}) collective-permute-start(bf16[2,32,512]{2,1,0:T(8,128)(2,1)S(1)} %get-tuple-element.42), channel_id=1, source_target_pairs={{0,4},{4,0},{8,12},{12,8},{1,5},{5,1},{9,13},{13,9},{2,6},{6,2},{1... | collective-permute-start | bytes 196616 | tf_op jit(solution)/shard_map/ppermute | solution.py:29
  39.8 4.3 %collective-permute-start.9 = (bf16[2,32,512]{2,1,0:T(8,128)(2,1)S(1)}, bf16[2,32,512]{2,1,0:T(8,128)(2,1)S(1)}, u32[]{:S(2)}, u32[]{:S(2)}) collective-permute-start(bf16[2,32,512]{2,1,0:T(8,128)(2,1)S(1)} %get-tuple-element.43), channel_id=1, source_target_pairs={{0,2},{2,0},{1,3},{3,1},{4,6},{6,4},{5,7},{7,5},{8,10},{10,8},{9,1... | collective-permute-start | bytes 196616 | tf_op jit(solution)/shard_map/ppermute | solution.py:29

commit v5 on v4

--- a/solution.py
+++ b/solution.py
@@ -245,32 +245,39 @@
     return dot(w_ref[0, beam_rows, cols], straight) + dot(w_ref[1, beam_rows, cols], turned)
 
 
+HIGH_EXTRA, OTHER_EXTRA = 1, 0
+SUM_EXTRA = (1, 0, 2)
+
+
 def filled(ref, before, after):
     zeros = lambda count: [jnp.zeros((count, ref.shape[2]), ref.dtype)] if count else []
     return [jnp.concatenate(zeros(before) + [ref[p]] + zeros(after), axis=0) for p in range(2)]
 
 
-def early_beams(weights, chunks, rest):
+def early_beams(weights, chunks, first, rest, partial=None):
     half = weights[0].shape[1]
     samples = chunks[0].shape[2]
-    step = min(half, 512)
+    step = min(half, 256)
+    before = [] if partial is None else [partial]
 
     def kernel(ours_ref, theirs_ref, *refs):
-        blocks = [filled(ref, 0, 0) for ref in refs[:-2]] + [filled(refs[-2], 0, rest)]
+        refs, out = refs[:-1], refs[-1]
+        blocks = [filled(ref, 0, 0) for ref in refs[len(before) : -1]] + [filled(refs[-1], 0, rest)]
         for number, w_ref in enumerate((ours_ref, theirs_ref)):
             for row in range(0, half, step):
-                product = chunk_product(w_ref, blocks, 0, pl.ds(row, step))
-                refs[-1][pl.ds(number * half + row, step), :] = product
-
-    return pl.pallas_call(
-        kernel,
-        in_specs=[VMEM] * (2 + len(chunks)),
+                product = chunk_product(w_ref, blocks, first, pl.ds(row, step))
+                at = pl.ds(number * half + row, step)
+                out[at, :] = product + refs[0][at, :] if before else product
+
+    return pl.pallas_call(
+        kernel,
+        in_specs=[VMEM] * (2 + len(before) + len(chunks)),
         out_specs=VMEM,
         out_shape=jax.ShapeDtypeStruct((2 * half, 2 * samples), jnp.float32),
         compiler_params=PARAMS,
         cost_estimate=SHORT,
         name="early_beams",
-    )(*weights, *chunks)
+    )(*weights, *before, *chunks)
 
 
 def two_parts(x):
@@ -278,38 +285,64 @@
     return high, (x - high.astype(jnp.float32)).astype(jnp.bfloat16)
 
 
-def last_levels(weights, chunk, done, partial, total):
+def message(blocks, width, extra):
+    return jax.ShapeDtypeStruct((blocks * width // 128 + 16 * extra, 128), jnp.bfloat16)
+
+
+def put(ref, first, value):
+    bins, width = value.shape
+    for lane in range(0, width, 128):
+        ref[pl.ds(first, bins), :] = value[:, lane : lane + 128].astype(ref.dtype)
+        first += bins
+    return first
+
+
+def take(ref, number, bins, width):
+    first = number * bins * width // 128
+    pieces = [ref[pl.ds(first + lane // 128 * bins, bins), :] for lane in range(0, width, 128)]
+    return jnp.concatenate(pieces, axis=1)
+
+
+def pad(ref, first):
+    if first < ref.shape[0]:
+        ref[pl.ds(first, ref.shape[0] - first), :] = jnp.zeros((ref.shape[0] - first, 128), ref.dtype)
+
+
+def last_levels(weights, chunk, partial, total):
     _, half, ants = weights[0].shape
     samples = chunk.shape[2]
     bins = samples // INTEG
-    step = min(half, 512)
-    first = ants - chunk.shape[1] - done
+    count = chunk.shape[1]
+    first = ants - count
 
     def kernel(ours_ref, theirs_ref, part_ref, chunk_ref, high_ref, low_ref, sent_ref):
-        blocks = [filled(chunk_ref, done, 0)]
+        re, im = chunk_ref[0], chunk_ref[1]
+        antennas = jnp.concatenate(
+            [jnp.concatenate([re, im], axis=1), jnp.concatenate([-im, re], axis=1)], axis=0
+        )
         bin_no = lax.broadcasted_iota(jnp.int32, (bins, samples), 0)
         time = lax.broadcasted_iota(jnp.int32, (bins, samples), 1)
         centre = jnp.where(time // INTEG == bin_no, 1.0 / INTEG, 0.0) - 1.0 / samples
-        centre = centre.astype(jnp.bfloat16)
+        centre = jnp.concatenate([centre, centre], axis=1).astype(jnp.bfloat16)
         for number, w_ref in enumerate((ours_ref, theirs_ref)):
-            for row in range(0, half, step):
-                rows = pl.ds(row, step)
-                beam = part_ref[pl.ds(number * half + row, step), :] + chunk_product(w_ref, blocks, first, rows)
-                re, im = beam[:, :samples], beam[:, samples:]
-                high, low = two_parts(re * re + im * im)
-                dot = lambda b: lax.dot_general(centre, b, (((1,), (1,)), ((), ())), preferred_element_type=jnp.float32)
-                high, low = two_parts((dot(high) + dot(low)) * (1.0 / math.sqrt(total)))
-                if number == 0:
-                    high_ref[:, rows] = high
-                    low_ref[:, rows] = low
-                else:
-                    sent_ref[:, rows] = high
+            both = jnp.concatenate([w_ref[0, :, pl.ds(first, count)], w_ref[1, :, pl.ds(first, count)]], axis=1)
+            beam = part_ref[pl.ds(number * half, half), :] + jnp.dot(both, antennas, preferred_element_type=jnp.float32)
+            re, im = beam[:, :samples], beam[:, samples:]
+            high, low = two_parts(re * re + im * im)
+            parts = jnp.concatenate([high, low], axis=1)
+            level = lax.dot_general(centre, parts, (((1,), (1,)), ((), ())), preferred_element_type=jnp.float32)
+            high, low = two_parts(level * (1.0 / math.sqrt(total)))
+            if number == 0:
+                pad(high_ref, put(high_ref, 0, high))
+                put(low_ref, 0, low)
+            else:
+                pad(sent_ref, put(sent_ref, 0, high))
 
     return pl.pallas_call(
         kernel,
         in_specs=[VMEM] * 4,
         out_specs=[VMEM] * 3,
-        out_shape=[jax.ShapeDtypeStruct((bins, half), jnp.bfloat16)] * 3,
+        out_shape=[message(bins, half, HIGH_EXTRA), message(bins, half, 0), message(bins, half, OTHER_EXTRA)],
         compiler_params=PARAMS,
         name="last_levels",
     )(*weights, partial, chunk)
@@ -366,46 +399,61 @@
     )(delays)
 
 
-def tree_stage(matrix, states, bins, final):
+def tree_stage(matrix, states, bins, width, final):
     slots, rows, _ = matrix.shape
-    width = states[0].shape[-1]
     targets = rows // bins
-    dtypes = [jnp.float32] + [jnp.bfloat16] * (targets - 1) if final else [jnp.bfloat16] * 2
+    blocks = bins * slots
+    if final:
+        shapes = [jax.ShapeDtypeStruct((slots, bins, width), jnp.float32)]
+        shapes += [message(blocks, width, extra) for extra in SUM_EXTRA[: targets - 1]]
+    else:
+        shapes = [message(blocks, width, 0)] * 2
 
     def kernel(map_ref, *refs):
         ins, outs = refs[: len(states)], refs[len(states) :]
+        row = 0
         for slot in range(slots):
-            column = [ref[...] if len(ref.shape) == 2 else ref[slot] for ref in ins]
+            column = [take(ref, slot if ref.shape[0] >= blocks * width // 128 else 0, bins, width) for ref in ins]
             value = jnp.dot(map_ref[slot], jnp.concatenate(column, axis=0), preferred_element_type=jnp.float32)
-            parts = [value[t * bins : t * bins + bins] for t in range(targets)] if final else two_parts(value)
-            for out, part in zip(outs, parts):
-                out[slot] = part.astype(out.dtype)
+            if final:
+                outs[0][slot] = value[:bins]
+                parts = [value[t * bins : t * bins + bins] for t in range(1, targets)]
+            else:
+                parts = two_parts(value)
+            for out, part in zip(outs[-len(parts) :], parts):
+                after = put(out, row, part)
+            row = after
+        for out in outs[-len(parts) :]:
+            pad(out, row)
 
     return pl.pallas_call(
         kernel,
         in_specs=[VMEM] * (1 + len(states)),
-        out_specs=[VMEM] * len(dtypes),
-        out_shape=[jax.ShapeDtypeStruct((slots, bins, width), dtype) for dtype in dtypes],
+        out_specs=[VMEM] * len(shapes),
+        out_shape=shapes,
         compiler_params=PARAMS,
         name="tree_stage",
     )(matrix, *states)
 
 
-def tree_sum(values):
-    def kernel(*refs):
-        total = refs[0][...]
-        for ref in refs[1:-1]:
-            total = total + ref[...].astype(jnp.float32)
-        refs[-1][...] = total
-
-    return pl.pallas_call(
-        kernel,
-        in_specs=[VMEM] * len(values),
+def tree_sum(own, received):
+    slots, bins, width = own.shape
+
+    def kernel(own_ref, *refs):
+        for slot in range(slots):
+            total = own_ref[slot]
+            for ref in refs[:-1]:
+                total = total + take(ref, slot, bins, width).astype(jnp.float32)
+            refs[-1][slot] = total
+
+    return pl.pallas_call(
+        kernel,
+        in_specs=[VMEM] * (1 + len(received)),
         out_specs=VMEM,
-        out_shape=jax.ShapeDtypeStruct(values[0].shape, jnp.float32),
+        out_shape=jax.ShapeDtypeStruct(own.shape, jnp.float32),
         compiler_params=PARAMS,
         name="tree_sum",
-    )(*values)
+    )(own, *received)
 
 
 def shards(voltages, gains, positions, directions, antenna_row_lookup, chan_order, delays):
@@ -421,23 +469,23 @@
     middle = chan_count // 2
     near = list(range(middle))
     distant = list(range(chan_count - 1, middle, -1))
-    masks = near + distant + [middle]
+    masks = distant + near + [middle]
     cut = ants // 2
     first = list(split_channels(voltages, [(middle, 0, cut)], True))
-    copied, first[0] = lax.optimization_barrier((voltages, first[0]))
-    across = split_channels(copied, [(m, 0, ants) for m in distant] + [(middle, cut, ants)], False, first[0])
-    beside = split_channels(copied, [(m, 0, ants) for m in near], False, across[0])
+    across = split_channels(voltages, [(m, 0, ants) for m in distant] + [(middle, cut, ants)], True, first[0])
+    beside = split_channels(voltages, [(m, 0, ants) for m in near], True, across[0])
     first = [chan_partner(first[0], middle)]
     across = [chan_partner(v, m) for v, m in zip(across, distant + [middle])]
     chunks = [beside[0]] + [chan_partner(v, m) for v, m in zip(beside[1:], near[1:])]
-    chunks += across[:-1] + first
+    chunks += first
 
     lookup = antenna_row_lookup.reshape(1, -1)
     placed, _ = lax.optimization_barrier((positions, beside[0]))
     ours, right, length = our_weights(placed, lookup, gains[:, 0], directions, chan_order, masks, total, in_band)
     held, _ = lax.optimization_barrier((directions, length))
     weights = [ours, their_weights(right, length, partner(held, [("beam", 0)]))]
-    partial = early_beams(weights, chunks, ants - cut)
+    partial = early_beams(weights, chunks, ants * len(distant), ants - cut)
+    partial = early_beams(weights, across[:-1], 0, 0, partial) if distant else partial
 
     bits = [("beam", 0)]
     for axis, count in (("chan", chan_count), ("band", band_count)):
@@ -450,16 +498,16 @@
     maps = tree_maps(delays.reshape(delays.shape[0], total), stages, bins, in_band)
     partial, *maps = lax.optimization_barrier((partial, *maps))
 
-    high, low, other = last_levels(weights, across[-1], cut, partial, total)
+    high, low, other = last_levels(weights, across[-1], partial, total)
     for (_, got, sent), matrix in zip(stages, maps):
         states = [high, low]
         for flips in subsets(got)[1:]:
             states.append(partner(other if ("beam", 0) in flips else high, flips))
-        result = tree_stage(matrix, states, bins, bool(sent))
+        result = tree_stage(matrix, states, bins, directions.shape[1], bool(sent))
         if not sent:
             high, low = result
-    sums = [result[0]] + [partner(value, flips) for value, flips in zip(result[1:], subsets(sent)[1:])]
-    return tree_sum(sums).reshape(1, per_dev, bins, high.shape[-1])
+    received = [partner(value, flips) for value, flips in zip(result[1:], subsets(sent)[1:])]
+    return tree_sum(result[0], received).reshape(1, per_dev, bins, directions.shape[1])
 
 
 def solution(mesh):

time: 45 us -> 44.6 us (level)
  waiting for transfers between devices: 10.8 us -> 7.4 us
  Pallas kernels: 16.6 us -> 18.7 us
  starting transfers between devices: 15 us -> 15.8 us
    ppermute x11, waiting for transfers between devices: 10.8 us -> 7.4 us  [partner(): return lax.ppermute(value, axes, pairs)]
    pallas_call x3, Pallas kernels: 3.78 us -> 5.99 us  [split_channels(): pl.pallas_call(kernel, in_specs=[pl.BlockSpec(memory_space=place)] + [pl....]
    ppermute x11, starting transfers between devices: 15 us -> 15.8 us  [partner(): return lax.ppermute(value, axes, pairs)]
    pallas_call x2 -> x3, Pallas kernels: 3.01 us -> 3.18 us  [the longest x2 2.49 us: early_beams(): pl.pallas_call(kernel, in_specs=[VMEM] * (2 + len(before) + len(chunks)),...]
    unnamed x14 -> x12, local copies, waits for them, and re-layouts: 1.47 us -> 1.47 us
  transfers between devices with their start and end apart: 11 -> 11, of which waited for: 6 -> 3; matrix products, arithmetic and copies ran while one was open for 2% -> 2% of each run, Pallas kernels for 29% -> 35%
where the time goes in v5:
time: 44.6 us; the launch traced here: 44.3 us
  Pallas kernels  18.7 us (42%)
  starting transfers between devices  15.8 us (35%)
  waiting for transfers between devices  7.4 us (17%)
  local copies, waits for them, and re-layouts  2.23 us (5%)
    ppermute x11, starting transfers between devices, partner(): return lax.ppermute(value, axes, pairs)  15.8 us
    ppermute x11, waiting for transfers between devices, partner(): return lax.ppermute(value, axes, pairs)  7.4 us
    pallas_call x3, Pallas kernels, split_channels(): pl.pallas_call(kernel, in_specs=[pl.BlockSpec(memory_space=place)] + [pl....  5.99 us
    pallas_call x1, Pallas kernels, our_weights(): pl.pallas_call(kernel, in_specs=[SMEM] + [VMEM] * 4, out_specs=[VMEM] * 3...  4.55 us
    pallas_call x1, Pallas kernels, their_weights(): pl.pallas_call(kernel, in_specs=[VMEM] * 3, out_specs=VMEM, out_shape=jax...  3.2 us
    pallas_call x2, Pallas kernels, early_beams(): pl.pallas_call(kernel, in_specs=[VMEM] * (2 + len(before) + len(chunks)),...  2.49 us
    unnamed x12, local copies, waits for them, and re-layouts  1.47 us
  transfers between devices with their start and end apart: 11, of which 3 were waited for; matrix products, arithmetic and copies ran while one was open for 2% of the time, Pallas kernels for 35%

profile of v5, /device:TPU:0, one launch (start us, length us, event | category | flops | bytes accessed | tf_op | source)
XLA Modules:
  0.0 44.3 jit_solution(9552168569113568981)
XLA Ops:
  0.0 1.4 %split_channels.3.refs_0_ = bf16[2,128,256]{2,1,0:T(8,128)(2,1)S(1)} custom-call(bf16[2,2048,256]{2,1,0:T(8,128)(2,1)} %bitcast.6), custom_call_target="tpu_custom_call" | custom-call | tf_op jit(solution)/shard_map/split_channels/pallas_call | solution.py:78
  1.4 4.1 %collective-permute-start.2 = (bf16[2,128,256]{2,1,0:T(8,128)(2,1)S(1)}, bf16[2,128,256]{2,1,0:T(8,128)(2,1)S(1)}, u32[]{:S(2)}, u32[]{:S(2)}) collective-permute-start(bf16[2,128,256]{2,1,0:T(8,128)(2,1)S(1)} %split_channels.3.refs_0_), channel_id=1, source_target_pairs={{0,8},{4,12},{8,0},{12,4},{1,9},{5,13},{9,1},{13,5},{2,10},{6,14},... | collective-permute-start | bytes 393224 | tf_op jit(solution)/shard_map/ppermute | solution.py:29
  5.5 2.3 %split_channels.4 = (bf16[2,256,256]{2,1,0:T(8,128)(2,1)S(1)}, bf16[2,128,256]{2,1,0:T(8,128)(2,1)}) custom-call(bf16[2,2048,256]{2,1,0:T(8,128)(2,1)} %bitcast.7, bf16[2,128,256]{2,1,0:T(8,128)(2,1)S(1)} %split_channels.3.refs_0_), custom_call_target="tpu_custom_call" | custom-call | tf_op jit(solution)/shard_map/split_channels/pallas_call | solution.py:78
  7.8 1.4 %collective-permute-start.3 = (bf16[2,256,256]{2,1,0:T(8,128)(2,1)S(1)}, bf16[2,256,256]{2,1,0:T(8,128)(2,1)S(1)}, u32[]{:S(2)}, u32[]{:S(2)}) collective-permute-start(bf16[2,256,256]{2,1,0:T(8,128)(2,1)S(1)} %get-tuple-element.23.refs_0_), channel_id=1, source_target_pairs={{0,12},{4,8},{8,4},{12,0},{1,13},{5,9},{9,5},{13,1},{2,14},{6,10},... | collective-permute-start | bytes 786440 | tf_op jit(solution)/shard_map/ppermute | solution.py:29
  9.2 2.3 %split_channels.5 = (bf16[2,256,256]{2,1,0:T(8,128)(2,1)S(1)}, bf16[2,256,256]{2,1,0:T(8,128)(2,1)}) custom-call(bf16[2,2048,256]{2,1,0:T(8,128)(2,1)} %bitcast.8, bf16[2,256,256]{2,1,0:T(8,128)(2,1)S(1)} %get-tuple-element.23.refs_0_), custom_call_target="tpu_custom_call" | custom-call | tf_op jit(solution)/shard_map/split_channels/pallas_call | solution.py:78
  11.6 0.3 collective-permute-start.1
  11.9 2.8 %collective-permute-start.4 = (bf16[2,128,256]{2,1,0:T(8,128)(2,1)}, bf16[2,128,256]{2,1,0:T(8,128)(2,1)S(1)}, u32[]{:S(2)}, u32[]{:S(2)}) collective-permute-start(bf16[2,128,256]{2,1,0:T(8,128)(2,1)} %get-tuple-element.33), channel_id=1, source_target_pairs={{0,8},{4,12},{8,0},{12,4},{1,9},{5,13},{9,1},{13,5},{2,10},{6,14},... | collective-permute-start | bytes 393224 | tf_op jit(solution)/shard_map/ppermute | solution.py:29
  14.7 4.5 %our_weights.1 = (bf16[2,512,1024]{2,1,0:T(8,128)(2,1)S(1)}, bf16[32,1024]{1,0:T(8,128)(2,1)S(1)}, f32[1,1024]{1,0:T(1,128)S(1)}) custom-call(s32[16]{0:T(128)S(1)} %copy-done.5, f32[3,1024]{1,0:T(4,128)S(1)} %copy-done.2, s32[1,1024]{1,0:T(1,128)S(1)} %bitcast.5, f32[2,2,1024]{2,1,0:T(2,128)S(1)} %bitcast.4, f32[3,512]{1,0:T(4,128)} %dir_ref.1), custom_call_target="tpu_custom_call" | custom-call | flops 10000000000 | bytes 100000000 | tf_op jit(solution)/shard_map/our_weights/pallas_call | solution.py:197
  19.3 0.6 %copy-done = bf16[32,1024]{1,0:T(8,128)(2,1)} copy-done((bf16[32,1024]{1,0:T(8,128)(2,1)}, bf16[32,1024]{1,0:T(8,128)(2,1)S(1)}, u32[]{:S(2)}) %copy-start) | copy-done | bytes 65560
  19.9 0.8 %reshape.16.delay_ref = s32[4,16]{1,0:T(4,128)S(1)} reshape(s32[4,2,8]{2,1,0:T(2,128)} %param.13) | data formatting | bytes 512 | tf_op jit(solution)/shard_map/reshape | solution.py:498
  20.6 0.7 %tree_maps.1.map_ref = bf16[2,128,160]{2,1,0:T(8,128)(2,1)S(1)} custom-call(s32[4,16]{1,0:T(4,128)S(1)} %reshape.16.delay_ref), custom_call_target="tpu_custom_call" | custom-call | tf_op jit(solution)/shard_map/tree_maps/pallas_call | solution.py:392
  21.4 0.8 %copy-done.1 = bf16[32,1024]{1,0:T(8,128)(2,1)S(1)} copy-done((bf16[32,1024]{1,0:T(8,128)(2,1)S(1)}, bf16[32,1024]{1,0:T(8,128)(2,1)}, u32[]{:S(2)}) %copy-start.1) | copy-done | bytes 65560
  22.2 3.2 %their_weights.1.theirs_ref = bf16[2,512,1024]{2,1,0:T(8,128)(2,1)S(1)} custom-call(bf16[32,1024]{1,0:T(8,128)(2,1)S(1)} %copy-done.1, f32[1,1024]{1,0:T(1,128)S(1)} %get-tuple-element.28.length_ref, f32[3,512]{1,0:T(4,128)S(1)} %collective-permute-done.dir_ref), custom_call_target="tpu_custom_call" | custom-call | tf_op jit(solution)/shard_map/their_weights/pallas_call | solution.py:223
  25.4 1.8 %early_beams.2.refs_0_ = f32[1024,512]{1,0:T(8,128)S(1)} custom-call(bf16[2,512,1024]{2,1,0:T(8,128)(2,1)S(1)} %get-tuple-element.26.ours_ref, bf16[2,512,1024]{2,1,0:T(8,128)(2,1)S(1)} %their_weights.1.theirs_ref, bf16[2,256,256]{2,1,0:T(8,128)(2,1)S(1)} %get-tuple-element.24.refs_0_, bf16[2,256,256]{2,1,0:T(8,128)(2,1)S(1)} %collective-permute-done.1.refs_1_, ...), custom_call_target="tpu_custom_call" | custom-call | tf_op jit(solution)/shard_map/early_beams/pallas_call | solution.py:272
  27.2 0.7 %early_beams.3.part_ref = f32[1024,512]{1,0:T(8,128)S(1)} custom-call(bf16[2,512,1024]{2,1,0:T(8,128)(2,1)S(1)} %get-tuple-element.26.ours_ref, bf16[2,512,1024]{2,1,0:T(8,128)(2,1)S(1)} %their_weights.1.theirs_ref, f32[1024,512]{1,0:T(8,128)S(1)} %early_beams.2.refs_0_, bf16[2,256,256]{2,1,0:T(8,128)(2,1)S(1)} %collective-permute-done.3.refs_1_), custom_call_target="tpu_custom_call" | custom-call | tf_op jit(solution)/shard_map/early_beams/pallas_call | solution.py:272
  28.0 0.8 %collective-permute-done.4.chunk_ref = bf16[2,128,256]{2,1,0:T(8,128)(2,1)S(1)} collective-permute-done((bf16[2,128,256]{2,1,0:T(8,128)(2,1)}, bf16[2,128,256]{2,1,0:T(8,128)(2,1)S(1)}, u32[]{:S(2)}, u32[]{:S(2)}) %collective-permute-start.4) | collective-permute-done | bytes 131104 | tf_op jit(solution)/shard_map/ppermute | solution.py:29
  28.7 0.8 %last_levels.1 = (bf16[144,128]{1,0:T(8,128)(2,1)S(1)}, bf16[128,128]{1,0:T(8,128)(2,1)S(1)}, bf16[128,128]{1,0:T(8,128)(2,1)S(1)}) custom-call(bf16[2,512,1024]{2,1,0:T(8,128)(2,1)S(1)} %get-tuple-element.26.ours_ref, bf16[2,512,1024]{2,1,0:T(8,128)(2,1)S(1)} %their_weights.1.theirs_ref, f32[1024,512]{1,0:T(8,128)S(1)} %early_beams.3.part_ref, ...), custom_call_target="tpu_custom_call" | custom-call | tf_op jit(solution)/shard_map/last_levels/pallas_call | solution.py:341
  29.6 0.7 %collective-permute-start.6 = (bf16[144,128]{1,0:T(8,128)(2,1)S(1)}, bf16[144,128]{1,0:T(8,128)(2,1)S(1)}, u32[]{:S(2)}, u32[]{:S(2)}) collective-permute-start(bf16[144,128]{1,0:T(8,128)(2,1)S(1)} %get-tuple-element.34.refs_0_), channel_id=1, source_target_pairs={{0,8},{4,12},{8,0},{12,4},{1,9},{5,13},{9,1},{13,5},{2,10},{6,14},... | collective-permute-start | bytes 110600 | tf_op jit(solution)/shard_map/ppermute | solution.py:29
  30.3 2.4 %collective-permute-start.7 = (bf16[128,128]{1,0:T(8,128)(2,1)S(1)}, bf16[128,128]{1,0:T(8,128)(2,1)S(1)}, u32[]{:S(2)}, u32[]{:S(2)}) collective-permute-start(bf16[128,128]{1,0:T(8,128)(2,1)S(1)} %get-tuple-element.36), channel_id=1, source_target_pairs={{0,9},{1,8},{4,13},{5,12},{8,1},{9,0},{12,5},{13,4},{2,11},{3,10},... | collective-permute-start | bytes 98312 | tf_op jit(solution)/shard_map/ppermute | solution.py:29
  32.7 2.9 %collective-permute-done.7.refs_4_ = bf16[128,128]{1,0:T(8,128)(2,1)S(1)} collective-permute-done((bf16[128,128]{1,0:T(8,128)(2,1)S(1)}, bf16[128,128]{1,0:T(8,128)(2,1)S(1)}, u32[]{:S(2)}, u32[]{:S(2)}) %collective-permute-start.7) | collective-permute-done | bytes 32800 | tf_op jit(solution)/shard_map/ppermute | solution.py:29
  35.8 3.4 %collective-permute-start.10 = (bf16[288,128]{1,0:T(8,128)(2,1)S(1)}, bf16[288,128]{1,0:T(8,128)(2,1)S(1)}, u32[]{:S(2)}, u32[]{:S(2)}) collective-permute-start(bf16[288,128]{1,0:T(8,128)(2,1)S(1)} %get-tuple-element.40), channel_id=1, source_target_pairs={{0,6},{2,4},{4,2},{6,0},{8,14},{10,12},{12,10},{14,8},{1,7},{3,5},... | collective-permute-start | bytes 221192 | tf_op jit(solution)/shard_map/ppermute | solution.py:29
  39.2 0.6 %collective-permute-start.9 = (bf16[256,128]{1,0:T(8,128)(2,1)S(1)}, bf16[256,128]{1,0:T(8,128)(2,1)S(1)}, u32[]{:S(2)}, u32[]{:S(2)}) collective-permute-start(bf16[256,128]{1,0:T(8,128)(2,1)S(1)} %get-tuple-element.39), channel_id=1, source_target_pairs={{0,2},{2,0},{1,3},{3,1},{4,6},{6,4},{5,7},{7,5},{8,10},{10,8},{9,1... | collective-permute-start | bytes 196616 | tf_op jit(solution)/shard_map/ppermute | solution.py:29
  39.9 3.7 %collective-permute-done.9.refs_1_ = bf16[256,128]{1,0:T(8,128)(2,1)S(1)} collective-permute-done((bf16[256,128]{1,0:T(8,128)(2,1)S(1)}, bf16[256,128]{1,0:T(8,128)(2,1)S(1)}, u32[]{:S(2)}, u32[]{:S(2)}) %collective-permute-start.9) | collective-permute-done | bytes 65568 | tf_op jit(solution)/shard_map/ppermute | solution.py:29
  43.6 0.7 %tree_sum.1 = f32[2,32,512]{2,1,0:T(8,128)} custom-call(f32[2,32,512]{2,1,0:T(8,128)S(1)} %get-tuple-element.37.own_ref, bf16[272,128]{1,0:T(8,128)(2,1)S(1)} %collective-permute-done.8.refs_0_, bf16[256,128]{1,0:T(8,128)(2,1)S(1)} %collective-permute-done.9.refs_1_, bf16[288,128]{1,0:T(8,128)(2,1)S(1)} %collective-permute-done.10.refs_2_), custom_call_target="tpu_custom_call" | custom-call | tf_op jit(solution)/shard_map/tree_sum/pallas_call | solution.py:449
  (22 shorter events, 0.3 us)
Async XLA Ops:
  1.4 13.3 %copy-start.2 = (f32[3,1024]{1,0:T(4,128)S(1)}, f32[3,1024]{1,0:T(4,128)}, u32[]{:S(2)}) copy-start(f32[3,1024]{1,0:T(4,128)} %pos_ref) | copy-start | bytes 36868
  1.4 13.3 %copy-start.3 = (f32[2,1,2,1024]{3,2,1,0:T(2,128)S(1)}, f32[2,1,2,1024]{3,2,1,0:T(2,128)}, u32[]{:S(2)}) copy-start(f32[2,1,2,1024]{3,2,1,0:T(2,128)} %param.8) | copy-start | bytes 49156
  1.4 13.3 %copy-start.4 = (s32[1024]{0:T(1024)S(1)}, s32[1024]{0:T(1024)}, u32[]{:S(2)}) copy-start(s32[1024]{0:T(1024)} %param.11) | copy-start | bytes 12292
  1.4 13.3 %copy-start.5 = (s32[16]{0:T(128)S(1)}, s32[16]{0:T(128)}, u32[]{:S(2)}) copy-start(s32[16]{0:T(128)} %order_ref.1) | copy-start | bytes 196
  1.4 24.0 %collective-permute-start.2 = (bf16[2,128,256]{2,1,0:T(8,128)(2,1)S(1)}, bf16[2,128,256]{2,1,0:T(8,128)(2,1)S(1)}, u32[]{:S(2)}, u32[]{:S(2)}) collective-permute-start(bf16[2,128,256]{2,1,0:T(8,128)(2,1)S(1)} %split_channels.3.refs_0_), channel_id=1, source_target_pairs={{0,8},{4,12},{8,0},{12,4},{1,9},{5,13},{9,1},{13,5},{2,10},{6,14},... | collective-permute-start | bytes 393224 | tf_op jit(solution)/shard_map/ppermute | solution.py:29
  7.8 19.4 %collective-permute-start.3 = (bf16[2,256,256]{2,1,0:T(8,128)(2,1)S(1)}, bf16[2,256,256]{2,1,0:T(8,128)(2,1)S(1)}, u32[]{:S(2)}, u32[]{:S(2)}) collective-permute-start(bf16[2,256,256]{2,1,0:T(8,128)(2,1)S(1)} %get-tuple-element.23.refs_0_), channel_id=1, source_target_pairs={{0,12},{4,8},{8,4},{12,0},{1,13},{5,9},{9,5},{13,1},{2,14},{6,10},... | collective-permute-start | bytes 786440 | tf_op jit(solution)/shard_map/ppermute | solution.py:29
  11.6 13.8 %collective-permute-start.1 = (bf16[2,256,256]{2,1,0:T(8,128)(2,1)}, bf16[2,256,256]{2,1,0:T(8,128)(2,1)S(1)}, u32[]{:S(2)}, u32[]{:S(2)}) collective-permute-start(bf16[2,256,256]{2,1,0:T(8,128)(2,1)} %get-tuple-element.30), channel_id=1, source_target_pairs={{0,4},{4,0},{8,12},{12,8},{1,5},{5,1},{9,13},{13,9},{2,6},{6,2},{1... | collective-permute-start | bytes 786440 | tf_op jit(solution)/shard_map/ppermute | solution.py:29
  11.9 16.8 %collective-permute-start.4 = (bf16[2,128,256]{2,1,0:T(8,128)(2,1)}, bf16[2,128,256]{2,1,0:T(8,128)(2,1)S(1)}, u32[]{:S(2)}, u32[]{:S(2)}) collective-permute-start(bf16[2,128,256]{2,1,0:T(8,128)(2,1)} %get-tuple-element.33), channel_id=1, source_target_pairs={{0,8},{4,12},{8,0},{12,4},{1,9},{5,13},{9,1},{13,5},{2,10},{6,14},... | collective-permute-start | bytes 393224 | tf_op jit(solution)/shard_map/ppermute | solution.py:29
  19.3 0.6 %copy-start = (bf16[32,1024]{1,0:T(8,128)(2,1)}, bf16[32,1024]{1,0:T(8,128)(2,1)S(1)}, u32[]{:S(2)}) copy-start(bf16[32,1024]{1,0:T(8,128)(2,1)S(1)} %get-tuple-element.27.right_ref) | copy-start | bytes 196612
  19.9 1.5 %collective-permute-start = (f32[3,512]{1,0:T(4,128)}, f32[3,512]{1,0:T(4,128)S(1)}, u32[]{:S(2)}, u32[]{:S(2)}) collective-permute-start(f32[3,512]{1,0:T(4,128)} %dir_ref.1), channel_id=1, source_target_pairs={{0,1},{1,0},{2,3},{3,2},{4,5},{5,4},{6,7},{7,6},{8,9},{9,8},{10,11... | collective-permute-start | bytes 18440 | tf_op jit(solution)/shard_map/ppermute | solution.py:29
  21.4 0.8 %copy-start.1 = (bf16[32,1024]{1,0:T(8,128)(2,1)S(1)}, bf16[32,1024]{1,0:T(8,128)(2,1)}, u32[]{:S(2)}) copy-start(bf16[32,1024]{1,0:T(8,128)(2,1)} %copy-done) | copy-start | bytes 196612
  29.6 6.0 %collective-permute-start.6 = (bf16[144,128]{1,0:T(8,128)(2,1)S(1)}, bf16[144,128]{1,0:T(8,128)(2,1)S(1)}, u32[]{:S(2)}, u32[]{:S(2)}) collective-permute-start(bf16[144,128]{1,0:T(8,128)(2,1)S(1)} %get-tuple-element.34.refs_0_), channel_id=1, source_target_pairs={{0,8},{4,12},{8,0},{12,4},{1,9},{5,13},{9,1},{13,5},{2,10},{6,14},... | collective-permute-start | bytes 110600 | tf_op jit(solution)/shard_map/ppermute | solution.py:29
  30.3 2.4 %collective-permute-start.5 = (bf16[128,128]{1,0:T(8,128)(2,1)S(1)}, bf16[128,128]{1,0:T(8,128)(2,1)S(1)}, u32[]{:S(2)}, u32[]{:S(2)}) collective-permute-start(bf16[128,128]{1,0:T(8,128)(2,1)S(1)} %get-tuple-element.36), channel_id=1, source_target_pairs={{0,1},{1,0},{2,3},{3,2},{4,5},{5,4},{6,7},{7,6},{8,9},{9,8},{10,11... | collective-permute-start | bytes 98312 | tf_op jit(solution)/shard_map/ppermute | solution.py:29
  30.3 5.2 %collective-permute-start.7 = (bf16[128,128]{1,0:T(8,128)(2,1)S(1)}, bf16[128,128]{1,0:T(8,128)(2,1)S(1)}, u32[]{:S(2)}, u32[]{:S(2)}) collective-permute-start(bf16[128,128]{1,0:T(8,128)(2,1)S(1)} %get-tuple-element.36), channel_id=1, source_target_pairs={{0,9},{1,8},{4,13},{5,12},{8,1},{9,0},{12,5},{13,4},{2,11},{3,10},... | collective-permute-start | bytes 98312 | tf_op jit(solution)/shard_map/ppermute | solution.py:29
  35.8 7.7 %collective-permute-start.10 = (bf16[288,128]{1,0:T(8,128)(2,1)S(1)}, bf16[288,128]{1,0:T(8,128)(2,1)S(1)}, u32[]{:S(2)}, u32[]{:S(2)}) collective-permute-start(bf16[288,128]{1,0:T(8,128)(2,1)S(1)} %get-tuple-element.40), channel_id=1, source_target_pairs={{0,6},{2,4},{4,2},{6,0},{8,14},{10,12},{12,10},{14,8},{1,7},{3,5},... | collective-permute-start | bytes 221192 | tf_op jit(solution)/shard_map/ppermute | solution.py:29
  39.2 4.3 %collective-permute-start.8 = (bf16[272,128]{1,0:T(8,128)(2,1)S(1)}, bf16[272,128]{1,0:T(8,128)(2,1)S(1)}, u32[]{:S(2)}, u32[]{:S(2)}) collective-permute-start(bf16[272,128]{1,0:T(8,128)(2,1)S(1)} %get-tuple-element.38), channel_id=1, source_target_pairs={{0,4},{4,0},{8,12},{12,8},{1,5},{5,1},{9,13},{13,9},{2,6},{6,2},{1... | collective-permute-start | bytes 208904 | tf_op jit(solution)/shard_map/ppermute | solution.py:29
  39.2 4.3 %collective-permute-start.9 = (bf16[256,128]{1,0:T(8,128)(2,1)S(1)}, bf16[256,128]{1,0:T(8,128)(2,1)S(1)}, u32[]{:S(2)}, u32[]{:S(2)}) collective-permute-start(bf16[256,128]{1,0:T(8,128)(2,1)S(1)} %get-tuple-element.39), channel_id=1, source_target_pairs={{0,2},{2,0},{1,3},{3,1},{4,6},{6,4},{5,7},{7,5},{8,10},{10,8},{9,1... | collective-permute-start | bytes 196616 | tf_op jit(solution)/shard_map/ppermute | solution.py:29

commit v6 on v5

--- a/solution.py
+++ b/solution.py
@@ -153,21 +153,69 @@
     lax.fori_loop(0, beams // block, block_of_beams, 0)
 
 
-def our_weights(positions, lookup, gains, dirs, chan_order, masks, total, in_band):
+def subsets(bits):
+    return [[bit for k, bit in enumerate(bits) if pick >> k & 1] for pick in range(1 << len(bits))]
+
+
+def map_shapes(stages, per_dev, bins):
+    return [(per_dev, bins << len(sent), bins * (1 + (1 << len(got)))) for _, got, sent in stages]
+
+
+def fill_maps(delay_ref, outs, stages, bins):
+    per_dev = lax.axis_size("beam")
+
+    def place(flips):
+        at = {axis: lax.axis_index(axis) for axis in ("band", "chan", "beam")}
+        for axis, bit in flips:
+            at[axis] = at[axis] ^ (1 << bit)
+        return at
+
+    def total_delay(bits, first_round, target, source, slot):
+        moved = 0
+        for k, (axis, bit) in enumerate(bits):
+            later = [b for b in bits[k + 1 :] if b in target or b in source]
+            end = place(target + later)
+            start = place(target + later + [b for b in bits[k : k + 1] if b in target or b in source])
+            delay = delay_ref[first_round + k, end["band"], end["chan"] * per_dev + slot]
+            moved = moved + ((start[axis] >> bit) & 1) * delay
+        return moved
+
+    first_round = 0
+    for (bits, got, sent), out in zip(stages, outs):
+        sources = [[]] + subsets(got)
+        shape = (bins, out.shape[2])
+        row = lax.broadcasted_iota(jnp.int32, shape, 0)
+        col = lax.broadcasted_iota(jnp.int32, shape, 1)
+        for slot in range(per_dev):
+            for number, target in enumerate(subsets(sent)):
+                shift = jnp.zeros_like(col)
+                for place_no, source in enumerate(sources):
+                    moved = total_delay(bits, first_round, target, source, slot)
+                    shift = jnp.where(col // bins == place_no, moved, shift)
+                hit = lax.rem(row - col + len(bits) * bins + shape[1] - shift, bins) == 0
+                out[slot, pl.ds(number * bins, bins), :] = jnp.where(hit, 1.0, 0.0).astype(jnp.bfloat16)
+        first_round += len(bits)
+
+
+def our_weights(positions, lookup, gains, dirs, chan_order, delays, masks, stages, bins):
     ants, beams = positions.shape[1], dirs.shape[1]
     per_dev = lax.axis_size("beam")
     size = ants // len(masks)
     lanes = min(ants, 512)
+    _, band_count, in_band = delays.shape
+    shapes = map_shapes(stages, per_dev, bins)
 
     def in_order(x, z):
         x = xor_blocks(x, z, len(masks))
         return jnp.concatenate([x[..., m * size : m * size + size] for m in masks], axis=-1)
 
-    def kernel(order_ref, pos_ref, look_ref, gain_ref, dir_ref, out, right_ref, length_ref, left, turns):
+    def kernel(order_ref, delay_ref, pos_ref, look_ref, gain_ref, dir_ref, out, right_ref, length_ref, copy_ref, *refs):
+        maps, (left, turns) = refs[:-2], refs[-2:]
+        copy_ref[...] = dir_ref[...]
         z = lax.axis_index("chan")
         e = lax.axis_index("beam")
         slot = lax.axis_index("band") * in_band + z * per_dev + e
-        freq = 1.0 + order_ref[slot].astype(jnp.float32) * (1.0 / total)
+        freq = 1.0 + order_ref[slot].astype(jnp.float32) * (1.0 / (band_count * in_band))
 
         g_re = in_order(jnp.where(e == 0, gain_ref[0, 0:1, :], gain_ref[0, 1:2, :]), z)
         g_im = in_order(jnp.where(e == 0, gain_ref[1, 0:1, :], gain_ref[1, 1:2, :]), z)
@@ -193,16 +241,19 @@
             right_ref[:, pl.ds(lane, lanes)] = (rows + turn_parts[:, lane : lane + lanes]).astype(jnp.bfloat16)
         left[...] = phase_rows(dir_ref[...])
         fill_weights(left, right_ref, length_ref, turns, out)
-
-    return pl.pallas_call(
-        kernel,
-        in_specs=[SMEM] + [VMEM] * 4,
-        out_specs=[VMEM] * 3,
+        fill_maps(delay_ref, maps, stages, bins)
+
+    return pl.pallas_call(
+        kernel,
+        in_specs=[SMEM] * 2 + [VMEM] * 4,
+        out_specs=[VMEM] * (4 + len(shapes)),
         out_shape=[
             jax.ShapeDtypeStruct((2, beams, ants), jnp.bfloat16),
             jax.ShapeDtypeStruct((PHASE_ROWS, ants), jnp.bfloat16),
             jax.ShapeDtypeStruct((1, ants), jnp.float32),
-        ],
+            jax.ShapeDtypeStruct(dirs.shape, jnp.float32),
+        ]
+        + [jax.ShapeDtypeStruct(shape, jnp.bfloat16) for shape in shapes],
         scratch_shapes=[
             pltpu.VMEM((PHASE_ROWS, beams), jnp.bfloat16),
             pltpu.VMEM((min(beams, 128), ants), jnp.float32),
@@ -210,7 +261,7 @@
         compiler_params=PARAMS,
         cost_estimate=LONG,
         name="our_weights",
-    )(chan_order, positions, lookup, gains, dirs)
+    )(chan_order, delays, positions, lookup, gains, dirs)
 
 
 def their_weights(right, length, dirs):
@@ -245,7 +296,7 @@
     return dot(w_ref[0, beam_rows, cols], straight) + dot(w_ref[1, beam_rows, cols], turned)
 
 
-HIGH_EXTRA, OTHER_EXTRA = 1, 0
+HIGH_EXTRA, OTHER_EXTRA = 1, (0, 2)
 SUM_EXTRA = (1, 0, 2)
 
 
@@ -315,7 +366,7 @@
     count = chunk.shape[1]
     first = ants - count
 
-    def kernel(ours_ref, theirs_ref, part_ref, chunk_ref, high_ref, low_ref, sent_ref):
+    def kernel(ours_ref, theirs_ref, part_ref, chunk_ref, high_ref, low_ref, *sent_refs):
         re, im = chunk_ref[0], chunk_ref[1]
         antennas = jnp.concatenate(
             [jnp.concatenate([re, im], axis=1), jnp.concatenate([-im, re], axis=1)], axis=0
@@ -336,70 +387,20 @@
                 pad(high_ref, put(high_ref, 0, high))
                 put(low_ref, 0, low)
             else:
-                pad(sent_ref, put(sent_ref, 0, high))
+                for sent_ref in sent_refs:
+                    pad(sent_ref, put(sent_ref, 0, high))
 
     return pl.pallas_call(
         kernel,
         in_specs=[VMEM] * 4,
-        out_specs=[VMEM] * 3,
-        out_shape=[message(bins, half, HIGH_EXTRA), message(bins, half, 0), message(bins, half, OTHER_EXTRA)],
+        out_specs=[VMEM] * 4,
+        out_shape=[message(bins, half, extra) for extra in (HIGH_EXTRA, 0, *OTHER_EXTRA)],
         compiler_params=PARAMS,
         name="last_levels",
     )(*weights, partial, chunk)
 
 
-def subsets(bits):
-    return [[bit for k, bit in enumerate(bits) if pick >> k & 1] for pick in range(1 << len(bits))]
-
-
-def tree_maps(delays, stages, bins, in_band):
-    per_dev = lax.axis_size("beam")
-    shapes = [(per_dev, bins << len(sent), bins * (1 + (1 << len(got)))) for _, got, sent in stages]
-
-    def kernel(delay_ref, *outs):
-        def place(flips):
-            at = {axis: lax.axis_index(axis) for axis in ("band", "chan", "beam")}
-            for axis, bit in flips:
-                at[axis] = at[axis] ^ (1 << bit)
-            return at
-
-        def total_delay(bits, first_round, target, source, slot):
-            moved = 0
-            for k, (axis, bit) in enumerate(bits):
-                later = [b for b in bits[k + 1 :] if b in target or b in source]
-                end = place(target + later)
-                start = place(target + later + [b for b in bits[k : k + 1] if b in target or b in source])
-                delay = delay_ref[first_round + k, end["band"] * in_band + end["chan"] * per_dev + slot]
-                moved = moved + ((start[axis] >> bit) & 1) * delay
-            return moved
-
-        first_round = 0
-        for (bits, got, sent), out in zip(stages, outs):
-            sources = [[]] + subsets(got)
-            shape = (bins, out.shape[2])
-            row = lax.broadcasted_iota(jnp.int32, shape, 0)
-            col = lax.broadcasted_iota(jnp.int32, shape, 1)
-            for slot in range(per_dev):
-                for number, target in enumerate(subsets(sent)):
-                    shift = jnp.zeros_like(col)
-                    for place_no, source in enumerate(sources):
-                        moved = total_delay(bits, first_round, target, source, slot)
-                        shift = jnp.where(col // bins == place_no, moved, shift)
-                    hit = lax.rem(row - col + len(bits) * bins + shape[1] - shift, bins) == 0
-                    out[slot, pl.ds(number * bins, bins), :] = jnp.where(hit, 1.0, 0.0).astype(jnp.bfloat16)
-            first_round += len(bits)
-
-    return pl.pallas_call(
-        kernel,
-        in_specs=[SMEM],
-        out_specs=[VMEM] * len(stages),
-        out_shape=[jax.ShapeDtypeStruct(shape, jnp.bfloat16) for shape in shapes],
-        compiler_params=PARAMS,
-        name="tree_maps",
-    )(delays)
-
-
-def tree_stage(matrix, states, bins, width, final):
+def tree_stage(matrix, states, bins, width, first, final):
     slots, rows, _ = matrix.shape
     targets = rows // bins
     blocks = bins * slots
@@ -413,7 +414,7 @@
         ins, outs = refs[: len(states)], refs[len(states) :]
         row = 0
         for slot in range(slots):
-            column = [take(ref, slot if ref.shape[0] >= blocks * width // 128 else 0, bins, width) for ref in ins]
+            column = [take(ref, 0 if first else slot, bins, width) for ref in ins]
             value = jnp.dot(map_ref[slot], jnp.concatenate(column, axis=0), preferred_element_type=jnp.float32)
             if final:
                 outs[0][slot] = value[:bins]
@@ -440,17 +441,23 @@
     slots, bins, width = own.shape
 
     def kernel(own_ref, *refs):
-        for slot in range(slots):
-            total = own_ref[slot]
-            for ref in refs[:-1]:
-                total = total + take(ref, slot, bins, width).astype(jnp.float32)
-            refs[-1][slot] = total
+        out, total, sems = refs[-3:]
+        copies = [pltpu.make_async_copy(total.at[slot], out.at[slot], sems.at[slot]) for slot in range(slots)]
+        for slot, copy in enumerate(copies):
+            value = own_ref[slot]
+            for ref in refs[:-3]:
+                value = value + take(ref, slot, bins, width).astype(jnp.float32)
+            total[slot] = value
+            copy.start()
+        for copy in copies:
+            copy.wait()
 
     return pl.pallas_call(
         kernel,
         in_specs=[VMEM] * (1 + len(received)),
-        out_specs=VMEM,
+        out_specs=pl.BlockSpec(memory_space=pltpu.HBM),
         out_shape=jax.ShapeDtypeStruct(own.shape, jnp.float32),
+        scratch_shapes=[pltpu.VMEM(own.shape, jnp.float32), pltpu.SemaphoreType.DMA((slots,))],
         compiler_params=PARAMS,
         name="tree_sum",
     )(own, *received)
@@ -468,24 +475,17 @@
 
     middle = chan_count // 2
     near = list(range(middle))
-    distant = list(range(chan_count - 1, middle, -1))
-    masks = distant + near + [middle]
+    distant = list(range(chan_count - 2, middle - 1, -1))
+    middle = chan_count - 1
+    masks = distant + near[1:] + [0, middle]
     cut = ants // 2
-    first = list(split_channels(voltages, [(middle, 0, cut)], True))
-    across = split_channels(voltages, [(m, 0, ants) for m in distant] + [(middle, cut, ants)], True, first[0])
-    beside = split_channels(voltages, [(m, 0, ants) for m in near], True, across[0])
+    first = split_channels(voltages, [(middle, 0, cut)], True)
+    across = split_channels(voltages, [(m, 0, ants) for m in distant], True, first[0])
+    *beside, rest = split_channels(voltages, [(m, 0, ants) for m in near] + [(middle, cut, ants)], True, across[0])
     first = [chan_partner(first[0], middle)]
-    across = [chan_partner(v, m) for v, m in zip(across, distant + [middle])]
-    chunks = [beside[0]] + [chan_partner(v, m) for v, m in zip(beside[1:], near[1:])]
-    chunks += first
-
-    lookup = antenna_row_lookup.reshape(1, -1)
-    placed, _ = lax.optimization_barrier((positions, beside[0]))
-    ours, right, length = our_weights(placed, lookup, gains[:, 0], directions, chan_order, masks, total, in_band)
-    held, _ = lax.optimization_barrier((directions, length))
-    weights = [ours, their_weights(right, length, partner(held, [("beam", 0)]))]
-    partial = early_beams(weights, chunks, ants * len(distant), ants - cut)
-    partial = early_beams(weights, across[:-1], 0, 0, partial) if distant else partial
+    across = [chan_partner(v, m) for v, m in zip(across, distant)]
+    rest = chan_partner(rest, middle)
+    beside = [beside[0]] + [chan_partner(v, m) for v, m in zip(beside[1:], near[1:])]
 
     bits = [("beam", 0)]
     for axis, count in (("chan", chan_count), ("band", band_count)):
@@ -493,17 +493,25 @@
     last = bits[-4:]
     got = [bit for bit in last if bit in (("beam", 0), ("chan", chan_count.bit_length() - 2))]
     got += [bit for bit in last[::-1] if bit not in got][: 2 - len(got)]
-    stages = [(pair, pair, []) for pair in (bits[i : i + 2] for i in range(0, len(bits) - 4, 2))]
+    stages = [(pair, pair, []) for pair in (bits[:-4][i : i + 2] for i in range(0, len(bits) - 4, 2))]
     stages.append((last, got, [bit for bit in last if bit not in got]))
-    maps = tree_maps(delays.reshape(delays.shape[0], total), stages, bins, in_band)
-    partial, *maps = lax.optimization_barrier((partial, *maps))
-
-    high, low, other = last_levels(weights, across[-1], partial, total)
-    for (_, got, sent), matrix in zip(stages, maps):
+
+    lookup = antenna_row_lookup.reshape(1, -1)
+    placed, _ = lax.optimization_barrier((positions, beside[0]))
+    ours, right, length, dirs, *maps = our_weights(
+        placed, lookup, gains[:, 0], directions, chan_order, delays, masks, stages, bins
+    )
+    weights = [ours, their_weights(right, length, partner(dirs, [("beam", 0)]))]
+    partial = early_beams(weights, [beside[0]] + first, ants * (chan_count - 2), ants - cut)
+    partial = early_beams(weights, beside[1:], ants * len(distant), 0, partial)
+    partial = early_beams(weights, across, 0, 0, partial)
+
+    high, low, *other = last_levels(weights, rest, partial, total)
+    for number, ((_, got, sent), matrix) in enumerate(zip(stages, maps)):
         states = [high, low]
         for flips in subsets(got)[1:]:
-            states.append(partner(other if ("beam", 0) in flips else high, flips))
-        result = tree_stage(matrix, states, bins, directions.shape[1], bool(sent))
+            states.append(partner(other[len(flips) - 1] if ("beam", 0) in flips else high, flips))
+        result = tree_stage(matrix, states, bins, directions.shape[1], number == 0, bool(sent))
         if not sent:
             high, low = result
     received = [partner(value, flips) for value, flips in zip(result[1:], subsets(sent)[1:])]

time: 44.6 us -> 44.3 us (level)
  waiting for transfers between devices: 7.4 us -> 11.8 us
  local copies, waits for them, and re-layouts: 2.23 us -> 0.04 us
  Pallas kernels: 18.7 us -> 16.9 us
  starting transfers between devices: 15.8 us -> 15.2 us
    ppermute x11, waiting for transfers between devices: 7.4 us -> 11.8 us  [partner(): return lax.ppermute(value, axes, pairs)]
    unnamed x12, local copies, waits for them, and re-layouts: 1.47 us -> 0.04 us
    pallas_call x3, Pallas kernels: 5.99 us -> 4.66 us  [split_channels(): pl.pallas_call(kernel, in_specs=[pl.BlockSpec(memory_space=place)] + [pl....]
    reshape x1 -> x0, local copies, waits for them, and re-layouts: 0.77 us -> none  [shards(): delays.reshape(delays.shape[0], total)]
    pallas_call x4 -> x3, Pallas kernels: 6.78 us -> 6.11 us  [the longest x1 4.57 us: our_weights(): pl.pallas_call(kernel, in_specs=[SMEM] * 2 + [VMEM] * 4, out_specs=[VMEM]...]
    ppermute x11, starting transfers between devices: 15.8 us -> 15.2 us  [partner(): return lax.ppermute(value, axes, pairs)]
    pallas_call x2 -> x3, Pallas kernels: 2.49 us -> 2.67 us  [early_beams(): pl.pallas_call(kernel, in_specs=[VMEM] * (2 + len(before) + len(chunks)),...]
  transfers between devices with their start and end apart: 11 -> 11, of which waited for: 3 -> 5; matrix products, arithmetic and copies ran while one was open for 2% -> 0% of each run, Pallas kernels for 35% -> 31%
where the time goes in v6:
time: 44.3 us; the launch traced here: 44.1 us
  Pallas kernels  16.9 us (38%)
  starting transfers between devices  15.2 us (34%)
  waiting for transfers between devices  11.8 us (27%)
    ppermute x11, starting transfers between devices, partner(): return lax.ppermute(value, axes, pairs)  15.2 us
    ppermute x11, waiting for transfers between devices, partner(): return lax.ppermute(value, axes, pairs)  11.8 us
    pallas_call x3, Pallas kernels, split_channels(): pl.pallas_call(kernel, in_specs=[pl.BlockSpec(memory_space=place)] + [pl....  4.66 us
    pallas_call x1, Pallas kernels, our_weights(): pl.pallas_call(kernel, in_specs=[SMEM] * 2 + [VMEM] * 4, out_specs=[VMEM]...  4.57 us
    pallas_call x1, Pallas kernels, their_weights(): pl.pallas_call(kernel, in_specs=[VMEM] * 3, out_specs=VMEM, out_shape=jax...  3.21 us
    pallas_call x3, Pallas kernels, early_beams(): pl.pallas_call(kernel, in_specs=[VMEM] * (2 + len(before) + len(chunks)),...  2.67 us
  transfers between devices with their start and end apart: 11, of which 5 were waited for; matrix products, arithmetic and copies ran while one was open for 0% of the time, Pallas kernels for 31%

profile of v6, /device:TPU:0, one launch (start us, length us, event | category | flops | bytes accessed | tf_op | source)
XLA Modules:
  0.0 44.1 jit_solution(650936856311074465)
XLA Ops:
  0.0 1.4 %split_channels.3.refs_0_ = bf16[2,128,256]{2,1,0:T(8,128)(2,1)S(1)} custom-call(bf16[2,2048,256]{2,1,0:T(8,128)(2,1)} %bitcast.6), custom_call_target="tpu_custom_call" | custom-call | tf_op jit(solution)/shard_map/split_channels/pallas_call | solution.py:78
  1.5 5.1 %collective-permute-start.1 = (bf16[2,128,256]{2,1,0:T(8,128)(2,1)S(1)}, bf16[2,128,256]{2,1,0:T(8,128)(2,1)S(1)}, u32[]{:S(2)}, u32[]{:S(2)}) collective-permute-start(bf16[2,128,256]{2,1,0:T(8,128)(2,1)S(1)} %split_channels.3.refs_0_), channel_id=1, source_target_pairs={{0,12},{4,8},{8,4},{12,0},{1,13},{5,9},{9,5},{13,1},{2,14},{6,10},... | collective-permute-start | bytes 393224 | tf_op jit(solution)/shard_map/ppermute | solution.py:29
  6.6 1.6 %split_channels.4.refs_0_ = bf16[2,256,256]{2,1,0:T(8,128)(2,1)S(1)} custom-call(bf16[2,2048,256]{2,1,0:T(8,128)(2,1)} %bitcast.7, bf16[2,128,256]{2,1,0:T(8,128)(2,1)S(1)} %split_channels.3.refs_0_), custom_call_target="tpu_custom_call" | custom-call | tf_op jit(solution)/shard_map/split_channels/pallas_call | solution.py:78
  8.3 1.7 %split_channels.5 = (bf16[2,256,256]{2,1,0:T(8,128)(2,1)S(1)}, bf16[2,256,256]{2,1,0:T(8,128)(2,1)S(1)}, bf16[2,128,256]{2,1,0:T(8,128)(2,1)S(1)}) custom-call(bf16[2,2048,256]{2,1,0:T(8,128)(2,1)} %bitcast.8, bf16[2,256,256]{2,1,0:T(8,128)(2,1)S(1)} %split_channels.4.refs_0_), custom_call_target="tpu_custom_call" | custom-call | tf_op jit(solution)/shard_map/split_channels/pallas_call | solution.py:78
  10.0 2.0 %collective-permute-start.4 = (bf16[2,128,256]{2,1,0:T(8,128)(2,1)S(1)}, bf16[2,128,256]{2,1,0:T(8,128)(2,1)S(1)}, u32[]{:S(2)}, u32[]{:S(2)}) collective-permute-start(bf16[2,128,256]{2,1,0:T(8,128)(2,1)S(1)} %get-tuple-element.30), channel_id=1, source_target_pairs={{0,12},{4,8},{8,4},{12,0},{1,13},{5,9},{9,5},{13,1},{2,14},{6,10},... | collective-permute-start | bytes 393224 | tf_op jit(solution)/shard_map/ppermute | solution.py:29
  11.9 1.6 %collective-permute-start.2 = (bf16[2,256,256]{2,1,0:T(8,128)(2,1)S(1)}, bf16[2,256,256]{2,1,0:T(8,128)(2,1)S(1)}, u32[]{:S(2)}, u32[]{:S(2)}) collective-permute-start(bf16[2,256,256]{2,1,0:T(8,128)(2,1)S(1)} %get-tuple-element.29), channel_id=1, source_target_pairs={{0,4},{4,0},{8,12},{12,8},{1,5},{5,1},{9,13},{13,9},{2,6},{6,2},{1... | collective-permute-start | bytes 786440 | tf_op jit(solution)/shard_map/ppermute | solution.py:29
  13.5 4.6 %our_weights.1 = (bf16[2,512,1024]{2,1,0:T(8,128)(2,1)S(1)}, bf16[32,1024]{1,0:T(8,128)(2,1)S(1)}, f32[1,1024]{1,0:T(1,128)S(1)}, f32[3,512]{1,0:T(4,128)S(1)}, bf16[2,128,160]{2,1,0:T(8,128)(2,1)S(1)}) custom-call(s32[16]{0:T(128)S(1)} %copy-done.5, s32[4,2,8]{2,1,0:T(2,128)S(1)} %copy-done.3, f32[3,1024]{1,0:T(4,128)S(1)} %copy-done, ...), custom_call_target="tpu_custom_call" | custom-call | flops 10000000000 | bytes 100000000 | tf_op jit(solution)/shard_map/our_weights/pallas_call | solution.py:246
  18.2 1.2 %collective-permute-done.dir_ref = f32[3,512]{1,0:T(4,128)S(1)} collective-permute-done((f32[3,512]{1,0:T(4,128)S(1)}, f32[3,512]{1,0:T(4,128)S(1)}, u32[]{:S(2)}, u32[]{:S(2)}) %collective-permute-start) | collective-permute-done | bytes 6176 | tf_op jit(solution)/shard_map/ppermute | solution.py:29
  19.3 3.2 %their_weights.1.theirs_ref = bf16[2,512,1024]{2,1,0:T(8,128)(2,1)S(1)} custom-call(bf16[32,1024]{1,0:T(8,128)(2,1)S(1)} %get-tuple-element.26.right_ref, f32[1,1024]{1,0:T(1,128)S(1)} %get-tuple-element.27.length_ref, f32[3,512]{1,0:T(4,128)S(1)} %collective-permute-done.dir_ref), custom_call_target="tpu_custom_call" | custom-call | tf_op jit(solution)/shard_map/their_weights/pallas_call | solution.py:274
  22.6 1.2 %early_beams.3.refs_0_ = f32[1024,512]{1,0:T(8,128)S(1)} custom-call(bf16[2,512,1024]{2,1,0:T(8,128)(2,1)S(1)} %get-tuple-element.25.ours_ref, bf16[2,512,1024]{2,1,0:T(8,128)(2,1)S(1)} %their_weights.1.theirs_ref, bf16[2,256,256]{2,1,0:T(8,128)(2,1)S(1)} %get-tuple-element.22.refs_0_, bf16[2,128,256]{2,1,0:T(8,128)(2,1)S(1)} %collective-permute-done.1.refs_1_), custom_call_target="tpu_custom_call" | custom-call | tf_op jit(solution)/shard_map/early_beams/pallas_call | solution.py:323
  23.8 3.7 %collective-permute-done.2.refs_1_ = bf16[2,256,256]{2,1,0:T(8,128)(2,1)S(1)} collective-permute-done((bf16[2,256,256]{2,1,0:T(8,128)(2,1)S(1)}, bf16[2,256,256]{2,1,0:T(8,128)(2,1)S(1)}, u32[]{:S(2)}, u32[]{:S(2)}) %collective-permute-start.2) | collective-permute-done | bytes 262176 | tf_op jit(solution)/shard_map/ppermute | solution.py:29
  27.5 0.7 %early_beams.4.refs_0_ = f32[1024,512]{1,0:T(8,128)S(1)} custom-call(bf16[2,512,1024]{2,1,0:T(8,128)(2,1)S(1)} %get-tuple-element.25.ours_ref, bf16[2,512,1024]{2,1,0:T(8,128)(2,1)S(1)} %their_weights.1.theirs_ref, f32[1024,512]{1,0:T(8,128)S(1)} %early_beams.3.refs_0_, bf16[2,256,256]{2,1,0:T(8,128)(2,1)S(1)} %collective-permute-done.2.refs_1_), custom_call_target="tpu_custom_call" | custom-call | tf_op jit(solution)/shard_map/early_beams/pallas_call | solution.py:323
  28.3 0.7 %early_beams.5.part_ref = f32[1024,512]{1,0:T(8,128)S(1)} custom-call(bf16[2,512,1024]{2,1,0:T(8,128)(2,1)S(1)} %get-tuple-element.25.ours_ref, bf16[2,512,1024]{2,1,0:T(8,128)(2,1)S(1)} %their_weights.1.theirs_ref, f32[1024,512]{1,0:T(8,128)S(1)} %early_beams.4.refs_0_, bf16[2,256,256]{2,1,0:T(8,128)(2,1)S(1)} %collective-permute-done.3.refs_1_), custom_call_target="tpu_custom_call" | custom-call | tf_op jit(solution)/shard_map/early_beams/pallas_call | solution.py:323
  29.0 0.8 %last_levels.1 = (bf16[144,128]{1,0:T(8,128)(2,1)S(1)}, bf16[128,128]{1,0:T(8,128)(2,1)S(1)}, bf16[128,128]{1,0:T(8,128)(2,1)S(1)}, bf16[160,128]{1,0:T(8,128)(2,1)S(1)}) custom-call(bf16[2,512,1024]{2,1,0:T(8,128)(2,1)S(1)} %get-tuple-element.25.ours_ref, bf16[2,512,1024]{2,1,0:T(8,128)(2,1)S(1)} %their_weights.1.theirs_ref, ...), custom_call_target="tpu_custom_call" | custom-call | tf_op jit(solution)/shard_map/last_levels/pallas_call | solution.py:393
  29.8 0.5 %collective-permute-start.7 = (bf16[160,128]{1,0:T(8,128)(2,1)S(1)}, bf16[160,128]{1,0:T(8,128)(2,1)S(1)}, u32[]{:S(2)}, u32[]{:S(2)}) collective-permute-start(bf16[160,128]{1,0:T(8,128)(2,1)S(1)} %get-tuple-element.34), channel_id=1, source_target_pairs={{0,9},{1,8},{4,13},{5,12},{8,1},{9,0},{12,5},{13,4},{2,11},{3,10},... | collective-permute-start | bytes 122888 | tf_op jit(solution)/shard_map/ppermute | solution.py:29
  30.4 1.1 %collective-permute-start.6 = (bf16[144,128]{1,0:T(8,128)(2,1)S(1)}, bf16[144,128]{1,0:T(8,128)(2,1)S(1)}, u32[]{:S(2)}, u32[]{:S(2)}) collective-permute-start(bf16[144,128]{1,0:T(8,128)(2,1)S(1)} %get-tuple-element.31.refs_0_), channel_id=1, source_target_pairs={{0,8},{4,12},{8,0},{12,4},{1,9},{5,13},{9,1},{13,5},{2,10},{6,14},... | collective-permute-start | bytes 110600 | tf_op jit(solution)/shard_map/ppermute | solution.py:29
  31.5 1.2 %collective-permute-start.5 = (bf16[128,128]{1,0:T(8,128)(2,1)S(1)}, bf16[128,128]{1,0:T(8,128)(2,1)S(1)}, u32[]{:S(2)}, u32[]{:S(2)}) collective-permute-start(bf16[128,128]{1,0:T(8,128)(2,1)S(1)} %get-tuple-element.33), channel_id=1, source_target_pairs={{0,1},{1,0},{2,3},{3,2},{4,5},{5,4},{6,7},{7,6},{8,9},{9,8},{10,11... | collective-permute-start | bytes 98312 | tf_op jit(solution)/shard_map/ppermute | solution.py:29
  32.7 0.9 %collective-permute-done.5.refs_2_ = bf16[128,128]{1,0:T(8,128)(2,1)S(1)} collective-permute-done((bf16[128,128]{1,0:T(8,128)(2,1)S(1)}, bf16[128,128]{1,0:T(8,128)(2,1)S(1)}, u32[]{:S(2)}, u32[]{:S(2)}) %collective-permute-start.5) | collective-permute-done | bytes 32800 | tf_op jit(solution)/shard_map/ppermute | solution.py:29
  33.5 2.3 %collective-permute-done.6.refs_3_ = bf16[144,128]{1,0:T(8,128)(2,1)S(1)} collective-permute-done((bf16[144,128]{1,0:T(8,128)(2,1)S(1)}, bf16[144,128]{1,0:T(8,128)(2,1)S(1)}, u32[]{:S(2)}, u32[]{:S(2)}) %collective-permute-start.6) | collective-permute-done | bytes 36896 | tf_op jit(solution)/shard_map/ppermute | solution.py:29
  36.1 0.8 %collective-permute-start.10 = (bf16[288,128]{1,0:T(8,128)(2,1)S(1)}, bf16[288,128]{1,0:T(8,128)(2,1)S(1)}, u32[]{:S(2)}, u32[]{:S(2)}) collective-permute-start(bf16[288,128]{1,0:T(8,128)(2,1)S(1)} %get-tuple-element.38), channel_id=1, source_target_pairs={{0,6},{2,4},{4,2},{6,0},{8,14},{10,12},{12,10},{14,8},{1,7},{3,5},... | collective-permute-start | bytes 221192 | tf_op jit(solution)/shard_map/ppermute | solution.py:29
  36.8 2.3 %collective-permute-start.8 = (bf16[272,128]{1,0:T(8,128)(2,1)S(1)}, bf16[272,128]{1,0:T(8,128)(2,1)S(1)}, u32[]{:S(2)}, u32[]{:S(2)}) collective-permute-start(bf16[272,128]{1,0:T(8,128)(2,1)S(1)} %get-tuple-element.36), channel_id=1, source_target_pairs={{0,4},{4,0},{8,12},{12,8},{1,5},{5,1},{9,13},{13,9},{2,6},{6,2},{1... | collective-permute-start | bytes 208904 | tf_op jit(solution)/shard_map/ppermute | solution.py:29
  39.1 0.5 %collective-permute-start.9 = (bf16[256,128]{1,0:T(8,128)(2,1)S(1)}, bf16[256,128]{1,0:T(8,128)(2,1)S(1)}, u32[]{:S(2)}, u32[]{:S(2)}) collective-permute-start(bf16[256,128]{1,0:T(8,128)(2,1)S(1)} %get-tuple-element.37), channel_id=1, source_target_pairs={{0,2},{2,0},{1,3},{3,1},{4,6},{6,4},{5,7},{7,5},{8,10},{10,8},{9,1... | collective-permute-start | bytes 196616 | tf_op jit(solution)/shard_map/ppermute | solution.py:29
  39.6 3.7 %collective-permute-done.9.refs_1_ = bf16[256,128]{1,0:T(8,128)(2,1)S(1)} collective-permute-done((bf16[256,128]{1,0:T(8,128)(2,1)S(1)}, bf16[256,128]{1,0:T(8,128)(2,1)S(1)}, u32[]{:S(2)}, u32[]{:S(2)}) %collective-permute-start.9) | collective-permute-done | bytes 65568 | tf_op jit(solution)/shard_map/ppermute | solution.py:29
  43.4 0.7 %tree_sum.1 = f32[2,32,512]{2,1,0:T(8,128)} custom-call(f32[2,32,512]{2,1,0:T(8,128)S(1)} %get-tuple-element.35.own_ref, bf16[272,128]{1,0:T(8,128)(2,1)S(1)} %collective-permute-done.8.refs_0_, bf16[256,128]{1,0:T(8,128)(2,1)S(1)} %collective-permute-done.9.refs_1_, bf16[288,128]{1,0:T(8,128)(2,1)S(1)} %collective-permute-done.10.refs_2_), custom_call_target="tpu_custom_call" | custom-call | tf_op jit(solution)/shard_map/tree_sum/pallas_call | solution.py:455
  (21 shorter events, 0.4 us)
Async XLA Ops:
  1.4 12.1 %copy-start = (f32[3,1024]{1,0:T(4,128)S(1)}, f32[3,1024]{1,0:T(4,128)}, u32[]{:S(2)}) copy-start(f32[3,1024]{1,0:T(4,128)} %pos_ref) | copy-start | bytes 36868
  1.4 12.1 %copy-start.1 = (f32[2,1,2,1024]{3,2,1,0:T(2,128)S(1)}, f32[2,1,2,1024]{3,2,1,0:T(2,128)}, u32[]{:S(2)}) copy-start(f32[2,1,2,1024]{3,2,1,0:T(2,128)} %param.8) | copy-start | bytes 49156
  1.4 12.1 %copy-start.2 = (f32[3,512]{1,0:T(4,128)S(1)}, f32[3,512]{1,0:T(4,128)}, u32[]{:S(2)}) copy-start(f32[3,512]{1,0:T(4,128)} %dir_ref.1) | copy-start | bytes 18436
  1.4 12.1 %copy-start.3 = (s32[4,2,8]{2,1,0:T(2,128)S(1)}, s32[4,2,8]{2,1,0:T(2,128)}, u32[]{:S(2)}) copy-start(s32[4,2,8]{2,1,0:T(2,128)} %delay_ref.1) | copy-start | bytes 772
  1.4 12.1 %copy-start.4 = (s32[1024]{0:T(1024)S(1)}, s32[1024]{0:T(1024)}, u32[]{:S(2)}) copy-start(s32[1024]{0:T(1024)} %param.11) | copy-start | bytes 12292
  1.4 12.1 %copy-start.5 = (s32[16]{0:T(128)S(1)}, s32[16]{0:T(128)}, u32[]{:S(2)}) copy-start(s32[16]{0:T(128)} %order_ref.1) | copy-start | bytes 196
  1.5 21.1 %collective-permute-start.1 = (bf16[2,128,256]{2,1,0:T(8,128)(2,1)S(1)}, bf16[2,128,256]{2,1,0:T(8,128)(2,1)S(1)}, u32[]{:S(2)}, u32[]{:S(2)}) collective-permute-start(bf16[2,128,256]{2,1,0:T(8,128)(2,1)S(1)} %split_channels.3.refs_0_), channel_id=1, source_target_pairs={{0,12},{4,8},{8,4},{12,0},{1,13},{5,9},{9,5},{13,1},{2,14},{6,10},... | collective-permute-start | bytes 393224 | tf_op jit(solution)/shard_map/ppermute | solution.py:29
  8.2 20.1 %collective-permute-start.3 = (bf16[2,256,256]{2,1,0:T(8,128)(2,1)S(1)}, bf16[2,256,256]{2,1,0:T(8,128)(2,1)S(1)}, u32[]{:S(2)}, u32[]{:S(2)}) collective-permute-start(bf16[2,256,256]{2,1,0:T(8,128)(2,1)S(1)} %split_channels.4.refs_0_), channel_id=1, source_target_pairs={{0,8},{4,12},{8,0},{12,4},{1,9},{5,13},{9,1},{13,5},{2,10},{6,14},... | collective-permute-start | bytes 786440 | tf_op jit(solution)/shard_map/ppermute | solution.py:29
  10.0 19.0 %collective-permute-start.4 = (bf16[2,128,256]{2,1,0:T(8,128)(2,1)S(1)}, bf16[2,128,256]{2,1,0:T(8,128)(2,1)S(1)}, u32[]{:S(2)}, u32[]{:S(2)}) collective-permute-start(bf16[2,128,256]{2,1,0:T(8,128)(2,1)S(1)} %get-tuple-element.30), channel_id=1, source_target_pairs={{0,12},{4,8},{8,4},{12,0},{1,13},{5,9},{9,5},{13,1},{2,14},{6,10},... | collective-permute-start | bytes 393224 | tf_op jit(solution)/shard_map/ppermute | solution.py:29
  11.9 15.6 %collective-permute-start.2 = (bf16[2,256,256]{2,1,0:T(8,128)(2,1)S(1)}, bf16[2,256,256]{2,1,0:T(8,128)(2,1)S(1)}, u32[]{:S(2)}, u32[]{:S(2)}) collective-permute-start(bf16[2,256,256]{2,1,0:T(8,128)(2,1)S(1)} %get-tuple-element.29), channel_id=1, source_target_pairs={{0,4},{4,0},{8,12},{12,8},{1,5},{5,1},{9,13},{13,9},{2,6},{6,2},{1... | collective-permute-start | bytes 786440 | tf_op jit(solution)/shard_map/ppermute | solution.py:29
  18.1 1.2 %collective-permute-start = (f32[3,512]{1,0:T(4,128)S(1)}, f32[3,512]{1,0:T(4,128)S(1)}, u32[]{:S(2)}, u32[]{:S(2)}) collective-permute-start(f32[3,512]{1,0:T(4,128)S(1)} %get-tuple-element.28), channel_id=1, source_target_pairs={{0,1},{1,0},{2,3},{3,2},{4,5},{5,4},{6,7},{7,6},{8,9},{9,8},{10,11... | collective-permute-start | bytes 18440 | tf_op jit(solution)/shard_map/ppermute | solution.py:29
  29.8 6.0 %collective-permute-start.7 = (bf16[160,128]{1,0:T(8,128)(2,1)S(1)}, bf16[160,128]{1,0:T(8,128)(2,1)S(1)}, u32[]{:S(2)}, u32[]{:S(2)}) collective-permute-start(bf16[160,128]{1,0:T(8,128)(2,1)S(1)} %get-tuple-element.34), channel_id=1, source_target_pairs={{0,9},{1,8},{4,13},{5,12},{8,1},{9,0},{12,5},{13,4},{2,11},{3,10},... | collective-permute-start | bytes 122888 | tf_op jit(solution)/shard_map/ppermute | solution.py:29
  30.4 5.5 %collective-permute-start.6 = (bf16[144,128]{1,0:T(8,128)(2,1)S(1)}, bf16[144,128]{1,0:T(8,128)(2,1)S(1)}, u32[]{:S(2)}, u32[]{:S(2)}) collective-permute-start(bf16[144,128]{1,0:T(8,128)(2,1)S(1)} %get-tuple-element.31.refs_0_), channel_id=1, source_target_pairs={{0,8},{4,12},{8,0},{12,4},{1,9},{5,13},{9,1},{13,5},{2,10},{6,14},... | collective-permute-start | bytes 110600 | tf_op jit(solution)/shard_map/ppermute | solution.py:29
  31.5 2.1 %collective-permute-start.5 = (bf16[128,128]{1,0:T(8,128)(2,1)S(1)}, bf16[128,128]{1,0:T(8,128)(2,1)S(1)}, u32[]{:S(2)}, u32[]{:S(2)}) collective-permute-start(bf16[128,128]{1,0:T(8,128)(2,1)S(1)} %get-tuple-element.33), channel_id=1, source_target_pairs={{0,1},{1,0},{2,3},{3,2},{4,5},{5,4},{6,7},{7,6},{8,9},{9,8},{10,11... | collective-permute-start | bytes 98312 | tf_op jit(solution)/shard_map/ppermute | solution.py:29
  36.1 7.3 %collective-permute-start.10 = (bf16[288,128]{1,0:T(8,128)(2,1)S(1)}, bf16[288,128]{1,0:T(8,128)(2,1)S(1)}, u32[]{:S(2)}, u32[]{:S(2)}) collective-permute-start(bf16[288,128]{1,0:T(8,128)(2,1)S(1)} %get-tuple-element.38), channel_id=1, source_target_pairs={{0,6},{2,4},{4,2},{6,0},{8,14},{10,12},{12,10},{14,8},{1,7},{3,5},... | collective-permute-start | bytes 221192 | tf_op jit(solution)/shard_map/ppermute | solution.py:29
  36.8 6.5 %collective-permute-start.8 = (bf16[272,128]{1,0:T(8,128)(2,1)S(1)}, bf16[272,128]{1,0:T(8,128)(2,1)S(1)}, u32[]{:S(2)}, u32[]{:S(2)}) collective-permute-start(bf16[272,128]{1,0:T(8,128)(2,1)S(1)} %get-tuple-element.36), channel_id=1, source_target_pairs={{0,4},{4,0},{8,12},{12,8},{1,5},{5,1},{9,13},{13,9},{2,6},{6,2},{1... | collective-permute-start | bytes 208904 | tf_op jit(solution)/shard_map/ppermute | solution.py:29
  39.1 4.3 %collective-permute-start.9 = (bf16[256,128]{1,0:T(8,128)(2,1)S(1)}, bf16[256,128]{1,0:T(8,128)(2,1)S(1)}, u32[]{:S(2)}, u32[]{:S(2)}) collective-permute-start(bf16[256,128]{1,0:T(8,128)(2,1)S(1)} %get-tuple-element.37), channel_id=1, source_target_pairs={{0,2},{2,0},{1,3},{3,1},{4,6},{6,4},{5,7},{7,5},{8,10},{10,8},{9,1... | collective-permute-start | bytes 196616 | tf_op jit(solution)/shard_map/ppermute | solution.py:29

commit v7 on v6

--- a/solution.py
+++ b/solution.py
@@ -13,7 +13,6 @@
 PARAMS = pltpu.CompilerParams(vmem_limit_bytes=40 * 1024 * 1024)
 SIN = (6.283184915580925, -41.34158901325128, 81.59993513909575, -76.61436771142901, 41.342343389037076, -12.470285565721209)
 COS = (0.9999992089426497, -19.738979914331107, 64.92864094416844, -85.27141067260794, 58.789407905427666, -21.069178520245686)
-ROUNDER = 1.5 * 2.0**23
 PHASE_ROWS = 32
 LONG = pl.CostEstimate(flops=10**10, bytes_accessed=10**8, transcendentals=10**8)
 SHORT = pl.CostEstimate(flops=0, bytes_accessed=0, transcendentals=0)
@@ -141,7 +140,7 @@
             for lane in range(0, ants, lanes):
                 cols = pl.ds(lane, lanes)
                 x = turns[at, cols]
-                t = x - ((x + ROUNDER) - ROUNDER)
+                t = x - jnp.round(x)
                 u = t * t
                 scale = length_ref[:, cols]
                 out[0, to, cols] = (horner(COS, u) * scale).astype(jnp.bfloat16)
@@ -375,12 +374,14 @@
         time = lax.broadcasted_iota(jnp.int32, (bins, samples), 1)
         centre = jnp.where(time // INTEG == bin_no, 1.0 / INTEG, 0.0) - 1.0 / samples
         centre = jnp.concatenate([centre, centre], axis=1).astype(jnp.bfloat16)
+        beams = []
         for number, w_ref in enumerate((ours_ref, theirs_ref)):
             both = jnp.concatenate([w_ref[0, :, pl.ds(first, count)], w_ref[1, :, pl.ds(first, count)]], axis=1)
-            beam = part_ref[pl.ds(number * half, half), :] + jnp.dot(both, antennas, preferred_element_type=jnp.float32)
+            product = jnp.dot(both, antennas, preferred_element_type=jnp.float32)
+            beams.append(part_ref[pl.ds(number * half, half), :] + product)
+        for number, beam in enumerate(beams):
             re, im = beam[:, :samples], beam[:, samples:]
-            high, low = two_parts(re * re + im * im)
-            parts = jnp.concatenate([high, low], axis=1)
+            parts = jnp.concatenate(two_parts(re * re + im * im), axis=1)
             level = lax.dot_general(centre, parts, (((1,), (1,)), ((), ())), preferred_element_type=jnp.float32)
             high, low = two_parts(level * (1.0 / math.sqrt(total)))
             if number == 0:
@@ -503,8 +504,7 @@
     )
     weights = [ours, their_weights(right, length, partner(dirs, [("beam", 0)]))]
     partial = early_beams(weights, [beside[0]] + first, ants * (chan_count - 2), ants - cut)
-    partial = early_beams(weights, beside[1:], ants * len(distant), 0, partial)
-    partial = early_beams(weights, across, 0, 0, partial)
+    partial = early_beams(weights, across + beside[1:], 0, 0, partial)
 
     high, low, *other = last_levels(weights, rest, partial, total)
     for number, ((_, got, sent), matrix) in enumerate(zip(stages, maps)):

time: 44.3 us -> 43.9 us (level)
  Pallas kernels: 16.9 us -> 16.4 us
    pallas_call x3 -> x2, Pallas kernels: 2.67 us -> 2.5 us  [early_beams(): pl.pallas_call(kernel, in_specs=[VMEM] * (2 + len(before) + len(chunks)),...]
  transfers between devices with their start and end apart: 11 -> 11, of which waited for: 5 -> 6; matrix products, arithmetic and copies ran while one was open for 0% -> 0% of each run, Pallas kernels for 31% -> 31%
where the time goes in v7:
time: 43.9 us; the launch traced here: 43.7 us
  Pallas kernels  16.4 us (37%)
  starting transfers between devices  15.2 us (35%)
  waiting for transfers between devices  11.9 us (27%)
    ppermute x11, starting transfers between devices, partner(): return lax.ppermute(value, axes, pairs)  15.2 us
    ppermute x11, waiting for transfers between devices, partner(): return lax.ppermute(value, axes, pairs)  11.9 us
    pallas_call x3, Pallas kernels, split_channels(): pl.pallas_call(kernel, in_specs=[pl.BlockSpec(memory_space=place)] + [pl....  4.66 us
    pallas_call x1, Pallas kernels, our_weights(): pl.pallas_call(kernel, in_specs=[SMEM] * 2 + [VMEM] * 4, out_specs=[VMEM]...  4.5 us
    pallas_call x1, Pallas kernels, their_weights(): pl.pallas_call(kernel, in_specs=[VMEM] * 3, out_specs=VMEM, out_shape=jax...  3.15 us
    pallas_call x2, Pallas kernels, early_beams(): pl.pallas_call(kernel, in_specs=[VMEM] * (2 + len(before) + len(chunks)),...  2.5 us
  transfers between devices with their start and end apart: 11, of which 6 were waited for; matrix products, arithmetic and copies ran while one was open for 0% of the time, Pallas kernels for 31%

profile of v7, /device:TPU:0, one launch (start us, length us, event | category | flops | bytes accessed | tf_op | source)
XLA Modules:
  0.0 43.7 jit_solution(12335897636211186017)
XLA Ops:
  0.0 1.4 %split_channels.3.refs_0_ = bf16[2,128,256]{2,1,0:T(8,128)(2,1)S(1)} custom-call(bf16[2,2048,256]{2,1,0:T(8,128)(2,1)} %bitcast.6), custom_call_target="tpu_custom_call" | custom-call | tf_op jit(solution)/shard_map/split_channels/pallas_call | solution.py:77
  1.5 5.1 %collective-permute-start.1 = (bf16[2,128,256]{2,1,0:T(8,128)(2,1)S(1)}, bf16[2,128,256]{2,1,0:T(8,128)(2,1)S(1)}, u32[]{:S(2)}, u32[]{:S(2)}) collective-permute-start(bf16[2,128,256]{2,1,0:T(8,128)(2,1)S(1)} %split_channels.3.refs_0_), channel_id=1, source_target_pairs={{0,12},{4,8},{8,4},{12,0},{1,13},{5,9},{9,5},{13,1},{2,14},{6,10},... | collective-permute-start | bytes 393224 | tf_op jit(solution)/shard_map/ppermute | solution.py:28
  6.6 1.6 %split_channels.4.refs_0_ = bf16[2,256,256]{2,1,0:T(8,128)(2,1)S(1)} custom-call(bf16[2,2048,256]{2,1,0:T(8,128)(2,1)} %bitcast.7, bf16[2,128,256]{2,1,0:T(8,128)(2,1)S(1)} %split_channels.3.refs_0_), custom_call_target="tpu_custom_call" | custom-call | tf_op jit(solution)/shard_map/split_channels/pallas_call | solution.py:77
  8.3 1.7 %split_channels.5 = (bf16[2,256,256]{2,1,0:T(8,128)(2,1)S(1)}, bf16[2,256,256]{2,1,0:T(8,128)(2,1)S(1)}, bf16[2,128,256]{2,1,0:T(8,128)(2,1)S(1)}) custom-call(bf16[2,2048,256]{2,1,0:T(8,128)(2,1)} %bitcast.8, bf16[2,256,256]{2,1,0:T(8,128)(2,1)S(1)} %split_channels.4.refs_0_), custom_call_target="tpu_custom_call" | custom-call | tf_op jit(solution)/shard_map/split_channels/pallas_call | solution.py:77
  10.0 2.0 %collective-permute-start.4 = (bf16[2,128,256]{2,1,0:T(8,128)(2,1)S(1)}, bf16[2,128,256]{2,1,0:T(8,128)(2,1)S(1)}, u32[]{:S(2)}, u32[]{:S(2)}) collective-permute-start(bf16[2,128,256]{2,1,0:T(8,128)(2,1)S(1)} %get-tuple-element.30), channel_id=1, source_target_pairs={{0,12},{4,8},{8,4},{12,0},{1,13},{5,9},{9,5},{13,1},{2,14},{6,10},... | collective-permute-start | bytes 393224 | tf_op jit(solution)/shard_map/ppermute | solution.py:28
  11.9 1.6 %collective-permute-start.3 = (bf16[2,256,256]{2,1,0:T(8,128)(2,1)S(1)}, bf16[2,256,256]{2,1,0:T(8,128)(2,1)S(1)}, u32[]{:S(2)}, u32[]{:S(2)}) collective-permute-start(bf16[2,256,256]{2,1,0:T(8,128)(2,1)S(1)} %get-tuple-element.29), channel_id=1, source_target_pairs={{0,4},{4,0},{8,12},{12,8},{1,5},{5,1},{9,13},{13,9},{2,6},{6,2},{1... | collective-permute-start | bytes 786440 | tf_op jit(solution)/shard_map/ppermute | solution.py:28
  13.5 4.5 %our_weights.1 = (bf16[2,512,1024]{2,1,0:T(8,128)(2,1)S(1)}, bf16[32,1024]{1,0:T(8,128)(2,1)S(1)}, f32[1,1024]{1,0:T(1,128)S(1)}, f32[3,512]{1,0:T(4,128)S(1)}, bf16[2,128,160]{2,1,0:T(8,128)(2,1)S(1)}) custom-call(s32[16]{0:T(128)S(1)} %copy-done.5, s32[4,2,8]{2,1,0:T(2,128)S(1)} %copy-done.3, f32[3,1024]{1,0:T(4,128)S(1)} %copy-done, ...), custom_call_target="tpu_custom_call" | custom-call | flops 10000000000 | bytes 100000000 | tf_op jit(solution)/shard_map/our_weights/pallas_call | solution.py:245
  18.1 1.2 %collective-permute-done.dir_ref = f32[3,512]{1,0:T(4,128)S(1)} collective-permute-done((f32[3,512]{1,0:T(4,128)S(1)}, f32[3,512]{1,0:T(4,128)S(1)}, u32[]{:S(2)}, u32[]{:S(2)}) %collective-permute-start) | collective-permute-done | bytes 6176 | tf_op jit(solution)/shard_map/ppermute | solution.py:28
  19.3 3.1 %their_weights.1.theirs_ref = bf16[2,512,1024]{2,1,0:T(8,128)(2,1)S(1)} custom-call(bf16[32,1024]{1,0:T(8,128)(2,1)S(1)} %get-tuple-element.26.right_ref, f32[1,1024]{1,0:T(1,128)S(1)} %get-tuple-element.27.length_ref, f32[3,512]{1,0:T(4,128)S(1)} %collective-permute-done.dir_ref), custom_call_target="tpu_custom_call" | custom-call | tf_op jit(solution)/shard_map/their_weights/pallas_call | solution.py:273
  22.4 1.2 %early_beams.2.refs_0_ = f32[1024,512]{1,0:T(8,128)S(1)} custom-call(bf16[2,512,1024]{2,1,0:T(8,128)(2,1)S(1)} %get-tuple-element.25.ours_ref, bf16[2,512,1024]{2,1,0:T(8,128)(2,1)S(1)} %their_weights.1.theirs_ref, bf16[2,256,256]{2,1,0:T(8,128)(2,1)S(1)} %get-tuple-element.22.refs_0_, bf16[2,128,256]{2,1,0:T(8,128)(2,1)S(1)} %collective-permute-done.1.refs_1_), custom_call_target="tpu_custom_call" | custom-call | tf_op jit(solution)/shard_map/early_beams/pallas_call | solution.py:322
  23.7 3.3 %collective-permute-done.2.refs_1_ = bf16[2,256,256]{2,1,0:T(8,128)(2,1)S(1)} collective-permute-done((bf16[2,256,256]{2,1,0:T(8,128)(2,1)S(1)}, bf16[2,256,256]{2,1,0:T(8,128)(2,1)S(1)}, u32[]{:S(2)}, u32[]{:S(2)}) %collective-permute-start.2) | collective-permute-done | bytes 262176 | tf_op jit(solution)/shard_map/ppermute | solution.py:28
  27.0 0.5 %collective-permute-done.3.refs_2_ = bf16[2,256,256]{2,1,0:T(8,128)(2,1)S(1)} collective-permute-done((bf16[2,256,256]{2,1,0:T(8,128)(2,1)S(1)}, bf16[2,256,256]{2,1,0:T(8,128)(2,1)S(1)}, u32[]{:S(2)}, u32[]{:S(2)}) %collective-permute-start.3) | collective-permute-done | bytes 262176 | tf_op jit(solution)/shard_map/ppermute | solution.py:28
  27.5 1.2 %early_beams.3.part_ref = f32[1024,512]{1,0:T(8,128)S(1)} custom-call(bf16[2,512,1024]{2,1,0:T(8,128)(2,1)S(1)} %get-tuple-element.25.ours_ref, bf16[2,512,1024]{2,1,0:T(8,128)(2,1)S(1)} %their_weights.1.theirs_ref, f32[1024,512]{1,0:T(8,128)S(1)} %early_beams.2.refs_0_, bf16[2,256,256]{2,1,0:T(8,128)(2,1)S(1)} %collective-permute-done.2.refs_1_, ...), custom_call_target="tpu_custom_call" | custom-call | tf_op jit(solution)/shard_map/early_beams/pallas_call | solution.py:322
  28.8 0.7 %last_levels.1 = (bf16[144,128]{1,0:T(8,128)(2,1)S(1)}, bf16[128,128]{1,0:T(8,128)(2,1)S(1)}, bf16[128,128]{1,0:T(8,128)(2,1)S(1)}, bf16[160,128]{1,0:T(8,128)(2,1)S(1)}) custom-call(bf16[2,512,1024]{2,1,0:T(8,128)(2,1)S(1)} %get-tuple-element.25.ours_ref, bf16[2,512,1024]{2,1,0:T(8,128)(2,1)S(1)} %their_weights.1.theirs_ref, ...), custom_call_target="tpu_custom_call" | custom-call | tf_op jit(solution)/shard_map/last_levels/pallas_call | solution.py:394
  29.5 0.7 %collective-permute-start.7 = (bf16[160,128]{1,0:T(8,128)(2,1)S(1)}, bf16[160,128]{1,0:T(8,128)(2,1)S(1)}, u32[]{:S(2)}, u32[]{:S(2)}) collective-permute-start(bf16[160,128]{1,0:T(8,128)(2,1)S(1)} %get-tuple-element.34), channel_id=1, source_target_pairs={{0,9},{1,8},{4,13},{5,12},{8,1},{9,0},{12,5},{13,4},{2,11},{3,10},... | collective-permute-start | bytes 122888 | tf_op jit(solution)/shard_map/ppermute | solution.py:28
  30.2 1.1 %collective-permute-start.6 = (bf16[144,128]{1,0:T(8,128)(2,1)S(1)}, bf16[144,128]{1,0:T(8,128)(2,1)S(1)}, u32[]{:S(2)}, u32[]{:S(2)}) collective-permute-start(bf16[144,128]{1,0:T(8,128)(2,1)S(1)} %get-tuple-element.31.refs_0_), channel_id=1, source_target_pairs={{0,8},{4,12},{8,0},{12,4},{1,9},{5,13},{9,1},{13,5},{2,10},{6,14},... | collective-permute-start | bytes 110600 | tf_op jit(solution)/shard_map/ppermute | solution.py:28
  31.3 1.0 %collective-permute-start.5 = (bf16[128,128]{1,0:T(8,128)(2,1)S(1)}, bf16[128,128]{1,0:T(8,128)(2,1)S(1)}, u32[]{:S(2)}, u32[]{:S(2)}) collective-permute-start(bf16[128,128]{1,0:T(8,128)(2,1)S(1)} %get-tuple-element.33), channel_id=1, source_target_pairs={{0,1},{1,0},{2,3},{3,2},{4,5},{5,4},{6,7},{7,6},{8,9},{9,8},{10,11... | collective-permute-start | bytes 98312 | tf_op jit(solution)/shard_map/ppermute | solution.py:28
  32.3 0.9 %collective-permute-done.5.refs_2_ = bf16[128,128]{1,0:T(8,128)(2,1)S(1)} collective-permute-done((bf16[128,128]{1,0:T(8,128)(2,1)S(1)}, bf16[128,128]{1,0:T(8,128)(2,1)S(1)}, u32[]{:S(2)}, u32[]{:S(2)}) %collective-permute-start.5) | collective-permute-done | bytes 32800 | tf_op jit(solution)/shard_map/ppermute | solution.py:28
  33.2 2.3 %collective-permute-done.6.refs_3_ = bf16[144,128]{1,0:T(8,128)(2,1)S(1)} collective-permute-done((bf16[144,128]{1,0:T(8,128)(2,1)S(1)}, bf16[144,128]{1,0:T(8,128)(2,1)S(1)}, u32[]{:S(2)}, u32[]{:S(2)}) %collective-permute-start.6) | collective-permute-done | bytes 36896 | tf_op jit(solution)/shard_map/ppermute | solution.py:28
  35.7 0.8 %collective-permute-start.10 = (bf16[288,128]{1,0:T(8,128)(2,1)S(1)}, bf16[288,128]{1,0:T(8,128)(2,1)S(1)}, u32[]{:S(2)}, u32[]{:S(2)}) collective-permute-start(bf16[288,128]{1,0:T(8,128)(2,1)S(1)} %get-tuple-element.38), channel_id=1, source_target_pairs={{0,6},{2,4},{4,2},{6,0},{8,14},{10,12},{12,10},{14,8},{1,7},{3,5},... | collective-permute-start | bytes 221192 | tf_op jit(solution)/shard_map/ppermute | solution.py:28
  36.5 2.2 %collective-permute-start.8 = (bf16[272,128]{1,0:T(8,128)(2,1)S(1)}, bf16[272,128]{1,0:T(8,128)(2,1)S(1)}, u32[]{:S(2)}, u32[]{:S(2)}) collective-permute-start(bf16[272,128]{1,0:T(8,128)(2,1)S(1)} %get-tuple-element.36), channel_id=1, source_target_pairs={{0,4},{4,0},{8,12},{12,8},{1,5},{5,1},{9,13},{13,9},{2,6},{6,2},{1... | collective-permute-start | bytes 208904 | tf_op jit(solution)/shard_map/ppermute | solution.py:28
  38.7 0.5 %collective-permute-start.9 = (bf16[256,128]{1,0:T(8,128)(2,1)S(1)}, bf16[256,128]{1,0:T(8,128)(2,1)S(1)}, u32[]{:S(2)}, u32[]{:S(2)}) collective-permute-start(bf16[256,128]{1,0:T(8,128)(2,1)S(1)} %get-tuple-element.37), channel_id=1, source_target_pairs={{0,2},{2,0},{1,3},{3,1},{4,6},{6,4},{5,7},{7,5},{8,10},{10,8},{9,1... | collective-permute-start | bytes 196616 | tf_op jit(solution)/shard_map/ppermute | solution.py:28
  39.3 3.7 %collective-permute-done.9.refs_1_ = bf16[256,128]{1,0:T(8,128)(2,1)S(1)} collective-permute-done((bf16[256,128]{1,0:T(8,128)(2,1)S(1)}, bf16[256,128]{1,0:T(8,128)(2,1)S(1)}, u32[]{:S(2)}, u32[]{:S(2)}) %collective-permute-start.9) | collective-permute-done | bytes 65568 | tf_op jit(solution)/shard_map/ppermute | solution.py:28
  43.0 0.7 %tree_sum.1 = f32[2,32,512]{2,1,0:T(8,128)} custom-call(f32[2,32,512]{2,1,0:T(8,128)S(1)} %get-tuple-element.35.own_ref, bf16[272,128]{1,0:T(8,128)(2,1)S(1)} %collective-permute-done.8.refs_0_, bf16[256,128]{1,0:T(8,128)(2,1)S(1)} %collective-permute-done.9.refs_1_, bf16[288,128]{1,0:T(8,128)(2,1)S(1)} %collective-permute-done.10.refs_2_), custom_call_target="tpu_custom_call" | custom-call | tf_op jit(solution)/shard_map/tree_sum/pallas_call | solution.py:456
  (20 shorter events, 0.4 us)
Async XLA Ops:
  1.4 12.1 %copy-start = (f32[3,1024]{1,0:T(4,128)S(1)}, f32[3,1024]{1,0:T(4,128)}, u32[]{:S(2)}) copy-start(f32[3,1024]{1,0:T(4,128)} %pos_ref) | copy-start | bytes 36868
  1.4 12.1 %copy-start.1 = (f32[2,1,2,1024]{3,2,1,0:T(2,128)S(1)}, f32[2,1,2,1024]{3,2,1,0:T(2,128)}, u32[]{:S(2)}) copy-start(f32[2,1,2,1024]{3,2,1,0:T(2,128)} %param.8) | copy-start | bytes 49156
  1.4 12.1 %copy-start.2 = (f32[3,512]{1,0:T(4,128)S(1)}, f32[3,512]{1,0:T(4,128)}, u32[]{:S(2)}) copy-start(f32[3,512]{1,0:T(4,128)} %dir_ref.1) | copy-start | bytes 18436
  1.4 12.1 %copy-start.3 = (s32[4,2,8]{2,1,0:T(2,128)S(1)}, s32[4,2,8]{2,1,0:T(2,128)}, u32[]{:S(2)}) copy-start(s32[4,2,8]{2,1,0:T(2,128)} %delay_ref.1) | copy-start | bytes 772
  1.4 12.1 %copy-start.4 = (s32[1024]{0:T(1024)S(1)}, s32[1024]{0:T(1024)}, u32[]{:S(2)}) copy-start(s32[1024]{0:T(1024)} %param.11) | copy-start | bytes 12292
  1.4 12.1 %copy-start.5 = (s32[16]{0:T(128)S(1)}, s32[16]{0:T(128)}, u32[]{:S(2)}) copy-start(s32[16]{0:T(128)} %order_ref.1) | copy-start | bytes 196
  1.5 21.0 %collective-permute-start.1 = (bf16[2,128,256]{2,1,0:T(8,128)(2,1)S(1)}, bf16[2,128,256]{2,1,0:T(8,128)(2,1)S(1)}, u32[]{:S(2)}, u32[]{:S(2)}) collective-permute-start(bf16[2,128,256]{2,1,0:T(8,128)(2,1)S(1)} %split_channels.3.refs_0_), channel_id=1, source_target_pairs={{0,12},{4,8},{8,4},{12,0},{1,13},{5,9},{9,5},{13,1},{2,14},{6,10},... | collective-permute-start | bytes 393224 | tf_op jit(solution)/shard_map/ppermute | solution.py:28
  8.2 18.8 %collective-permute-start.2 = (bf16[2,256,256]{2,1,0:T(8,128)(2,1)S(1)}, bf16[2,256,256]{2,1,0:T(8,128)(2,1)S(1)}, u32[]{:S(2)}, u32[]{:S(2)}) collective-permute-start(bf16[2,256,256]{2,1,0:T(8,128)(2,1)S(1)} %split_channels.4.refs_0_), channel_id=1, source_target_pairs={{0,8},{4,12},{8,0},{12,4},{1,9},{5,13},{9,1},{13,5},{2,10},{6,14},... | collective-permute-start | bytes 786440 | tf_op jit(solution)/shard_map/ppermute | solution.py:28
  10.0 18.8 %collective-permute-start.4 = (bf16[2,128,256]{2,1,0:T(8,128)(2,1)S(1)}, bf16[2,128,256]{2,1,0:T(8,128)(2,1)S(1)}, u32[]{:S(2)}, u32[]{:S(2)}) collective-permute-start(bf16[2,128,256]{2,1,0:T(8,128)(2,1)S(1)} %get-tuple-element.30), channel_id=1, source_target_pairs={{0,12},{4,8},{8,4},{12,0},{1,13},{5,9},{9,5},{13,1},{2,14},{6,10},... | collective-permute-start | bytes 393224 | tf_op jit(solution)/shard_map/ppermute | solution.py:28
  11.9 15.6 %collective-permute-start.3 = (bf16[2,256,256]{2,1,0:T(8,128)(2,1)S(1)}, bf16[2,256,256]{2,1,0:T(8,128)(2,1)S(1)}, u32[]{:S(2)}, u32[]{:S(2)}) collective-permute-start(bf16[2,256,256]{2,1,0:T(8,128)(2,1)S(1)} %get-tuple-element.29), channel_id=1, source_target_pairs={{0,4},{4,0},{8,12},{12,8},{1,5},{5,1},{9,13},{13,9},{2,6},{6,2},{1... | collective-permute-start | bytes 786440 | tf_op jit(solution)/shard_map/ppermute | solution.py:28
  18.0 1.2 %collective-permute-start = (f32[3,512]{1,0:T(4,128)S(1)}, f32[3,512]{1,0:T(4,128)S(1)}, u32[]{:S(2)}, u32[]{:S(2)}) collective-permute-start(f32[3,512]{1,0:T(4,128)S(1)} %get-tuple-element.28), channel_id=1, source_target_pairs={{0,1},{1,0},{2,3},{3,2},{4,5},{5,4},{6,7},{7,6},{8,9},{9,8},{10,11... | collective-permute-start | bytes 18440 | tf_op jit(solution)/shard_map/ppermute | solution.py:28
  29.5 6.0 %collective-permute-start.7 = (bf16[160,128]{1,0:T(8,128)(2,1)S(1)}, bf16[160,128]{1,0:T(8,128)(2,1)S(1)}, u32[]{:S(2)}, u32[]{:S(2)}) collective-permute-start(bf16[160,128]{1,0:T(8,128)(2,1)S(1)} %get-tuple-element.34), channel_id=1, source_target_pairs={{0,9},{1,8},{4,13},{5,12},{8,1},{9,0},{12,5},{13,4},{2,11},{3,10},... | collective-permute-start | bytes 122888 | tf_op jit(solution)/shard_map/ppermute | solution.py:28
  30.2 5.3 %collective-permute-start.6 = (bf16[144,128]{1,0:T(8,128)(2,1)S(1)}, bf16[144,128]{1,0:T(8,128)(2,1)S(1)}, u32[]{:S(2)}, u32[]{:S(2)}) collective-permute-start(bf16[144,128]{1,0:T(8,128)(2,1)S(1)} %get-tuple-element.31.refs_0_), channel_id=1, source_target_pairs={{0,8},{4,12},{8,0},{12,4},{1,9},{5,13},{9,1},{13,5},{2,10},{6,14},... | collective-permute-start | bytes 110600 | tf_op jit(solution)/shard_map/ppermute | solution.py:28
  31.3 1.9 %collective-permute-start.5 = (bf16[128,128]{1,0:T(8,128)(2,1)S(1)}, bf16[128,128]{1,0:T(8,128)(2,1)S(1)}, u32[]{:S(2)}, u32[]{:S(2)}) collective-permute-start(bf16[128,128]{1,0:T(8,128)(2,1)S(1)} %get-tuple-element.33), channel_id=1, source_target_pairs={{0,1},{1,0},{2,3},{3,2},{4,5},{5,4},{6,7},{7,6},{8,9},{9,8},{10,11... | collective-permute-start | bytes 98312 | tf_op jit(solution)/shard_map/ppermute | solution.py:28
  35.7 7.3 %collective-permute-start.10 = (bf16[288,128]{1,0:T(8,128)(2,1)S(1)}, bf16[288,128]{1,0:T(8,128)(2,1)S(1)}, u32[]{:S(2)}, u32[]{:S(2)}) collective-permute-start(bf16[288,128]{1,0:T(8,128)(2,1)S(1)} %get-tuple-element.38), channel_id=1, source_target_pairs={{0,6},{2,4},{4,2},{6,0},{8,14},{10,12},{12,10},{14,8},{1,7},{3,5},... | collective-permute-start | bytes 221192 | tf_op jit(solution)/shard_map/ppermute | solution.py:28
  36.5 6.5 %collective-permute-start.8 = (bf16[272,128]{1,0:T(8,128)(2,1)S(1)}, bf16[272,128]{1,0:T(8,128)(2,1)S(1)}, u32[]{:S(2)}, u32[]{:S(2)}) collective-permute-start(bf16[272,128]{1,0:T(8,128)(2,1)S(1)} %get-tuple-element.36), channel_id=1, source_target_pairs={{0,4},{4,0},{8,12},{12,8},{1,5},{5,1},{9,13},{13,9},{2,6},{6,2},{1... | collective-permute-start | bytes 208904 | tf_op jit(solution)/shard_map/ppermute | solution.py:28
  38.7 4.3 %collective-permute-start.9 = (bf16[256,128]{1,0:T(8,128)(2,1)S(1)}, bf16[256,128]{1,0:T(8,128)(2,1)S(1)}, u32[]{:S(2)}, u32[]{:S(2)}) collective-permute-start(bf16[256,128]{1,0:T(8,128)(2,1)S(1)} %get-tuple-element.37), channel_id=1, source_target_pairs={{0,2},{2,0},{1,3},{3,1},{4,6},{6,4},{5,7},{7,5},{8,10},{10,8},{9,1... | collective-permute-start | bytes 196616 | tf_op jit(solution)/shard_map/ppermute | solution.py:28

commit v8 on v7

--- a/solution.py
+++ b/solution.py
@@ -64,7 +64,7 @@
             block = raw.at[number] if from_hbm else rows(number)
             slot = number % 2
             for lane, half in zip(lanes, wide):
-                half[slot] = block[:, pl.ds(lane, 128)].astype(jnp.float32)
+                half[slot, pl.ds(0, group * chans), :] = block[:, pl.ds(lane, 128)].astype(jnp.float32)
             for (mask, piece_first, piece_last), out in zip(pieces, outs):
                 if piece_first <= first < piece_last:
                     chan = (z ^ mask) * per_dev + e
@@ -81,7 +81,7 @@
         out_shape=[
             jax.ShapeDtypeStruct((parts, last - first, samples), jnp.bfloat16) for _, first, last in pieces
         ],
-        scratch_shapes=[pltpu.VMEM((2, group * chans, 128), jnp.float32)] * len(lanes)
+        scratch_shapes=[pltpu.VMEM((2, (group + 1) * chans, 128), jnp.float32)] * len(lanes)
         + [
             pltpu.VMEM((raw_slots, group * chans, samples), jnp.bfloat16),
             pltpu.SemaphoreType.DMA((raw_slots,)),

time: 43.9 us -> 43.9 us (level)
  no operation moved by 1% of the time
where the time goes in v8:
time: 43.9 us; the launch traced here: 43.7 us
  Pallas kernels  16.4 us (37%)
  starting transfers between devices  15.2 us (35%)
  waiting for transfers between devices  11.9 us (27%)
    ppermute x11, starting transfers between devices, partner(): return lax.ppermute(value, axes, pairs)  15.2 us
    ppermute x11, waiting for transfers between devices, partner(): return lax.ppermute(value, axes, pairs)  11.9 us
    pallas_call x3, Pallas kernels, split_channels(): pl.pallas_call(kernel, in_specs=[pl.BlockSpec(memory_space=place)] + [pl....  4.66 us
    pallas_call x1, Pallas kernels, our_weights(): pl.pallas_call(kernel, in_specs=[SMEM] * 2 + [VMEM] * 4, out_specs=[VMEM]...  4.5 us
    pallas_call x1, Pallas kernels, their_weights(): pl.pallas_call(kernel, in_specs=[VMEM] * 3, out_specs=VMEM, out_shape=jax...  3.15 us
    pallas_call x2, Pallas kernels, early_beams(): pl.pallas_call(kernel, in_specs=[VMEM] * (2 + len(before) + len(chunks)),...  2.5 us
  transfers between devices with their start and end apart: 11, of which 6 were waited for; matrix products, arithmetic and copies ran while one was open for 0% of the time, Pallas kernels for 31%

profile of v8, /device:TPU:0, one launch (start us, length us, event | category | flops | bytes accessed | tf_op | source)
XLA Modules:
  0.0 43.7 jit_solution(5158009090773185633)
XLA Ops:
  0.0 1.4 %split_channels.3.refs_0_ = bf16[2,128,256]{2,1,0:T(8,128)(2,1)S(1)} custom-call(bf16[2,2048,256]{2,1,0:T(8,128)(2,1)} %bitcast.6), custom_call_target="tpu_custom_call" | custom-call | tf_op jit(solution)/shard_map/split_channels/pallas_call | solution.py:77
  1.5 5.1 %collective-permute-start.1 = (bf16[2,128,256]{2,1,0:T(8,128)(2,1)S(1)}, bf16[2,128,256]{2,1,0:T(8,128)(2,1)S(1)}, u32[]{:S(2)}, u32[]{:S(2)}) collective-permute-start(bf16[2,128,256]{2,1,0:T(8,128)(2,1)S(1)} %split_channels.3.refs_0_), channel_id=1, source_target_pairs={{0,12},{4,8},{8,4},{12,0},{1,13},{5,9},{9,5},{13,1},{2,14},{6,10},... | collective-permute-start | bytes 393224 | tf_op jit(solution)/shard_map/ppermute | solution.py:28
  6.6 1.6 %split_channels.4.refs_0_ = bf16[2,256,256]{2,1,0:T(8,128)(2,1)S(1)} custom-call(bf16[2,2048,256]{2,1,0:T(8,128)(2,1)} %bitcast.7, bf16[2,128,256]{2,1,0:T(8,128)(2,1)S(1)} %split_channels.3.refs_0_), custom_call_target="tpu_custom_call" | custom-call | tf_op jit(solution)/shard_map/split_channels/pallas_call | solution.py:77
  8.3 1.7 %split_channels.5 = (bf16[2,256,256]{2,1,0:T(8,128)(2,1)S(1)}, bf16[2,256,256]{2,1,0:T(8,128)(2,1)S(1)}, bf16[2,128,256]{2,1,0:T(8,128)(2,1)S(1)}) custom-call(bf16[2,2048,256]{2,1,0:T(8,128)(2,1)} %bitcast.8, bf16[2,256,256]{2,1,0:T(8,128)(2,1)S(1)} %split_channels.4.refs_0_), custom_call_target="tpu_custom_call" | custom-call | tf_op jit(solution)/shard_map/split_channels/pallas_call | solution.py:77
  10.0 2.0 %collective-permute-start.4 = (bf16[2,128,256]{2,1,0:T(8,128)(2,1)S(1)}, bf16[2,128,256]{2,1,0:T(8,128)(2,1)S(1)}, u32[]{:S(2)}, u32[]{:S(2)}) collective-permute-start(bf16[2,128,256]{2,1,0:T(8,128)(2,1)S(1)} %get-tuple-element.30), channel_id=1, source_target_pairs={{0,12},{4,8},{8,4},{12,0},{1,13},{5,9},{9,5},{13,1},{2,14},{6,10},... | collective-permute-start | bytes 393224 | tf_op jit(solution)/shard_map/ppermute | solution.py:28
  11.9 1.6 %collective-permute-start.3 = (bf16[2,256,256]{2,1,0:T(8,128)(2,1)S(1)}, bf16[2,256,256]{2,1,0:T(8,128)(2,1)S(1)}, u32[]{:S(2)}, u32[]{:S(2)}) collective-permute-start(bf16[2,256,256]{2,1,0:T(8,128)(2,1)S(1)} %get-tuple-element.29), channel_id=1, source_target_pairs={{0,4},{4,0},{8,12},{12,8},{1,5},{5,1},{9,13},{13,9},{2,6},{6,2},{1... | collective-permute-start | bytes 786440 | tf_op jit(solution)/shard_map/ppermute | solution.py:28
  13.5 4.5 %our_weights.1 = (bf16[2,512,1024]{2,1,0:T(8,128)(2,1)S(1)}, bf16[32,1024]{1,0:T(8,128)(2,1)S(1)}, f32[1,1024]{1,0:T(1,128)S(1)}, f32[3,512]{1,0:T(4,128)S(1)}, bf16[2,128,160]{2,1,0:T(8,128)(2,1)S(1)}) custom-call(s32[16]{0:T(128)S(1)} %copy-done.5, s32[4,2,8]{2,1,0:T(2,128)S(1)} %copy-done.3, f32[3,1024]{1,0:T(4,128)S(1)} %copy-done, ...), custom_call_target="tpu_custom_call" | custom-call | flops 10000000000 | bytes 100000000 | tf_op jit(solution)/shard_map/our_weights/pallas_call | solution.py:245
  18.1 1.2 %collective-permute-done.dir_ref = f32[3,512]{1,0:T(4,128)S(1)} collective-permute-done((f32[3,512]{1,0:T(4,128)S(1)}, f32[3,512]{1,0:T(4,128)S(1)}, u32[]{:S(2)}, u32[]{:S(2)}) %collective-permute-start) | collective-permute-done | bytes 6176 | tf_op jit(solution)/shard_map/ppermute | solution.py:28
  19.3 3.1 %their_weights.1.theirs_ref = bf16[2,512,1024]{2,1,0:T(8,128)(2,1)S(1)} custom-call(bf16[32,1024]{1,0:T(8,128)(2,1)S(1)} %get-tuple-element.26.right_ref, f32[1,1024]{1,0:T(1,128)S(1)} %get-tuple-element.27.length_ref, f32[3,512]{1,0:T(4,128)S(1)} %collective-permute-done.dir_ref), custom_call_target="tpu_custom_call" | custom-call | tf_op jit(solution)/shard_map/their_weights/pallas_call | solution.py:273
  22.4 1.2 %early_beams.2.refs_0_ = f32[1024,512]{1,0:T(8,128)S(1)} custom-call(bf16[2,512,1024]{2,1,0:T(8,128)(2,1)S(1)} %get-tuple-element.25.ours_ref, bf16[2,512,1024]{2,1,0:T(8,128)(2,1)S(1)} %their_weights.1.theirs_ref, bf16[2,256,256]{2,1,0:T(8,128)(2,1)S(1)} %get-tuple-element.22.refs_0_, bf16[2,128,256]{2,1,0:T(8,128)(2,1)S(1)} %collective-permute-done.1.refs_1_), custom_call_target="tpu_custom_call" | custom-call | tf_op jit(solution)/shard_map/early_beams/pallas_call | solution.py:322
  23.7 3.3 %collective-permute-done.2.refs_1_ = bf16[2,256,256]{2,1,0:T(8,128)(2,1)S(1)} collective-permute-done((bf16[2,256,256]{2,1,0:T(8,128)(2,1)S(1)}, bf16[2,256,256]{2,1,0:T(8,128)(2,1)S(1)}, u32[]{:S(2)}, u32[]{:S(2)}) %collective-permute-start.2) | collective-permute-done | bytes 262176 | tf_op jit(solution)/shard_map/ppermute | solution.py:28
  27.0 0.5 %collective-permute-done.3.refs_2_ = bf16[2,256,256]{2,1,0:T(8,128)(2,1)S(1)} collective-permute-done((bf16[2,256,256]{2,1,0:T(8,128)(2,1)S(1)}, bf16[2,256,256]{2,1,0:T(8,128)(2,1)S(1)}, u32[]{:S(2)}, u32[]{:S(2)}) %collective-permute-start.3) | collective-permute-done | bytes 262176 | tf_op jit(solution)/shard_map/ppermute | solution.py:28
  27.5 1.2 %early_beams.3.part_ref = f32[1024,512]{1,0:T(8,128)S(1)} custom-call(bf16[2,512,1024]{2,1,0:T(8,128)(2,1)S(1)} %get-tuple-element.25.ours_ref, bf16[2,512,1024]{2,1,0:T(8,128)(2,1)S(1)} %their_weights.1.theirs_ref, f32[1024,512]{1,0:T(8,128)S(1)} %early_beams.2.refs_0_, bf16[2,256,256]{2,1,0:T(8,128)(2,1)S(1)} %collective-permute-done.2.refs_1_, ...), custom_call_target="tpu_custom_call" | custom-call | tf_op jit(solution)/shard_map/early_beams/pallas_call | solution.py:322
  28.8 0.7 %last_levels.1 = (bf16[144,128]{1,0:T(8,128)(2,1)S(1)}, bf16[128,128]{1,0:T(8,128)(2,1)S(1)}, bf16[128,128]{1,0:T(8,128)(2,1)S(1)}, bf16[160,128]{1,0:T(8,128)(2,1)S(1)}) custom-call(bf16[2,512,1024]{2,1,0:T(8,128)(2,1)S(1)} %get-tuple-element.25.ours_ref, bf16[2,512,1024]{2,1,0:T(8,128)(2,1)S(1)} %their_weights.1.theirs_ref, ...), custom_call_target="tpu_custom_call" | custom-call | tf_op jit(solution)/shard_map/last_levels/pallas_call | solution.py:394
  29.5 0.7 %collective-permute-start.7 = (bf16[160,128]{1,0:T(8,128)(2,1)S(1)}, bf16[160,128]{1,0:T(8,128)(2,1)S(1)}, u32[]{:S(2)}, u32[]{:S(2)}) collective-permute-start(bf16[160,128]{1,0:T(8,128)(2,1)S(1)} %get-tuple-element.34), channel_id=1, source_target_pairs={{0,9},{1,8},{4,13},{5,12},{8,1},{9,0},{12,5},{13,4},{2,11},{3,10},... | collective-permute-start | bytes 122888 | tf_op jit(solution)/shard_map/ppermute | solution.py:28
  30.2 1.1 %collective-permute-start.6 = (bf16[144,128]{1,0:T(8,128)(2,1)S(1)}, bf16[144,128]{1,0:T(8,128)(2,1)S(1)}, u32[]{:S(2)}, u32[]{:S(2)}) collective-permute-start(bf16[144,128]{1,0:T(8,128)(2,1)S(1)} %get-tuple-element.31.refs_0_), channel_id=1, source_target_pairs={{0,8},{4,12},{8,0},{12,4},{1,9},{5,13},{9,1},{13,5},{2,10},{6,14},... | collective-permute-start | bytes 110600 | tf_op jit(solution)/shard_map/ppermute | solution.py:28
  31.3 1.0 %collective-permute-start.5 = (bf16[128,128]{1,0:T(8,128)(2,1)S(1)}, bf16[128,128]{1,0:T(8,128)(2,1)S(1)}, u32[]{:S(2)}, u32[]{:S(2)}) collective-permute-start(bf16[128,128]{1,0:T(8,128)(2,1)S(1)} %get-tuple-element.33), channel_id=1, source_target_pairs={{0,1},{1,0},{2,3},{3,2},{4,5},{5,4},{6,7},{7,6},{8,9},{9,8},{10,11... | collective-permute-start | bytes 98312 | tf_op jit(solution)/shard_map/ppermute | solution.py:28
  32.3 0.9 %collective-permute-done.5.refs_2_ = bf16[128,128]{1,0:T(8,128)(2,1)S(1)} collective-permute-done((bf16[128,128]{1,0:T(8,128)(2,1)S(1)}, bf16[128,128]{1,0:T(8,128)(2,1)S(1)}, u32[]{:S(2)}, u32[]{:S(2)}) %collective-permute-start.5) | collective-permute-done | bytes 32800 | tf_op jit(solution)/shard_map/ppermute | solution.py:28
  33.2 2.3 %collective-permute-done.6.refs_3_ = bf16[144,128]{1,0:T(8,128)(2,1)S(1)} collective-permute-done((bf16[144,128]{1,0:T(8,128)(2,1)S(1)}, bf16[144,128]{1,0:T(8,128)(2,1)S(1)}, u32[]{:S(2)}, u32[]{:S(2)}) %collective-permute-start.6) | collective-permute-done | bytes 36896 | tf_op jit(solution)/shard_map/ppermute | solution.py:28
  35.7 0.8 %collective-permute-start.10 = (bf16[288,128]{1,0:T(8,128)(2,1)S(1)}, bf16[288,128]{1,0:T(8,128)(2,1)S(1)}, u32[]{:S(2)}, u32[]{:S(2)}) collective-permute-start(bf16[288,128]{1,0:T(8,128)(2,1)S(1)} %get-tuple-element.38), channel_id=1, source_target_pairs={{0,6},{2,4},{4,2},{6,0},{8,14},{10,12},{12,10},{14,8},{1,7},{3,5},... | collective-permute-start | bytes 221192 | tf_op jit(solution)/shard_map/ppermute | solution.py:28
  36.5 2.2 %collective-permute-start.8 = (bf16[272,128]{1,0:T(8,128)(2,1)S(1)}, bf16[272,128]{1,0:T(8,128)(2,1)S(1)}, u32[]{:S(2)}, u32[]{:S(2)}) collective-permute-start(bf16[272,128]{1,0:T(8,128)(2,1)S(1)} %get-tuple-element.36), channel_id=1, source_target_pairs={{0,4},{4,0},{8,12},{12,8},{1,5},{5,1},{9,13},{13,9},{2,6},{6,2},{1... | collective-permute-start | bytes 208904 | tf_op jit(solution)/shard_map/ppermute | solution.py:28
  38.7 0.5 %collective-permute-start.9 = (bf16[256,128]{1,0:T(8,128)(2,1)S(1)}, bf16[256,128]{1,0:T(8,128)(2,1)S(1)}, u32[]{:S(2)}, u32[]{:S(2)}) collective-permute-start(bf16[256,128]{1,0:T(8,128)(2,1)S(1)} %get-tuple-element.37), channel_id=1, source_target_pairs={{0,2},{2,0},{1,3},{3,1},{4,6},{6,4},{5,7},{7,5},{8,10},{10,8},{9,1... | collective-permute-start | bytes 196616 | tf_op jit(solution)/shard_map/ppermute | solution.py:28
  39.3 3.7 %collective-permute-done.9.refs_1_ = bf16[256,128]{1,0:T(8,128)(2,1)S(1)} collective-permute-done((bf16[256,128]{1,0:T(8,128)(2,1)S(1)}, bf16[256,128]{1,0:T(8,128)(2,1)S(1)}, u32[]{:S(2)}, u32[]{:S(2)}) %collective-permute-start.9) | collective-permute-done | bytes 65568 | tf_op jit(solution)/shard_map/ppermute | solution.py:28
  43.0 0.7 %tree_sum.1 = f32[2,32,512]{2,1,0:T(8,128)} custom-call(f32[2,32,512]{2,1,0:T(8,128)S(1)} %get-tuple-element.35.own_ref, bf16[272,128]{1,0:T(8,128)(2,1)S(1)} %collective-permute-done.8.refs_0_, bf16[256,128]{1,0:T(8,128)(2,1)S(1)} %collective-permute-done.9.refs_1_, bf16[288,128]{1,0:T(8,128)(2,1)S(1)} %collective-permute-done.10.refs_2_), custom_call_target="tpu_custom_call" | custom-call | tf_op jit(solution)/shard_map/tree_sum/pallas_call | solution.py:456
  (20 shorter events, 0.4 us)
Async XLA Ops:
  1.4 12.1 %copy-start = (f32[3,1024]{1,0:T(4,128)S(1)}, f32[3,1024]{1,0:T(4,128)}, u32[]{:S(2)}) copy-start(f32[3,1024]{1,0:T(4,128)} %pos_ref) | copy-start | bytes 36868
  1.4 12.1 %copy-start.1 = (f32[2,1,2,1024]{3,2,1,0:T(2,128)S(1)}, f32[2,1,2,1024]{3,2,1,0:T(2,128)}, u32[]{:S(2)}) copy-start(f32[2,1,2,1024]{3,2,1,0:T(2,128)} %param.8) | copy-start | bytes 49156
  1.4 12.1 %copy-start.2 = (f32[3,512]{1,0:T(4,128)S(1)}, f32[3,512]{1,0:T(4,128)}, u32[]{:S(2)}) copy-start(f32[3,512]{1,0:T(4,128)} %dir_ref.1) | copy-start | bytes 18436
  1.4 12.1 %copy-start.3 = (s32[4,2,8]{2,1,0:T(2,128)S(1)}, s32[4,2,8]{2,1,0:T(2,128)}, u32[]{:S(2)}) copy-start(s32[4,2,8]{2,1,0:T(2,128)} %delay_ref.1) | copy-start | bytes 772
  1.4 12.1 %copy-start.4 = (s32[1024]{0:T(1024)S(1)}, s32[1024]{0:T(1024)}, u32[]{:S(2)}) copy-start(s32[1024]{0:T(1024)} %param.11) | copy-start | bytes 12292
  1.4 12.1 %copy-start.5 = (s32[16]{0:T(128)S(1)}, s32[16]{0:T(128)}, u32[]{:S(2)}) copy-start(s32[16]{0:T(128)} %order_ref.1) | copy-start | bytes 196
  1.5 21.0 %collective-permute-start.1 = (bf16[2,128,256]{2,1,0:T(8,128)(2,1)S(1)}, bf16[2,128,256]{2,1,0:T(8,128)(2,1)S(1)}, u32[]{:S(2)}, u32[]{:S(2)}) collective-permute-start(bf16[2,128,256]{2,1,0:T(8,128)(2,1)S(1)} %split_channels.3.refs_0_), channel_id=1, source_target_pairs={{0,12},{4,8},{8,4},{12,0},{1,13},{5,9},{9,5},{13,1},{2,14},{6,10},... | collective-permute-start | bytes 393224 | tf_op jit(solution)/shard_map/ppermute | solution.py:28
  8.2 18.8 %collective-permute-start.2 = (bf16[2,256,256]{2,1,0:T(8,128)(2,1)S(1)}, bf16[2,256,256]{2,1,0:T(8,128)(2,1)S(1)}, u32[]{:S(2)}, u32[]{:S(2)}) collective-permute-start(bf16[2,256,256]{2,1,0:T(8,128)(2,1)S(1)} %split_channels.4.refs_0_), channel_id=1, source_target_pairs={{0,8},{4,12},{8,0},{12,4},{1,9},{5,13},{9,1},{13,5},{2,10},{6,14},... | collective-permute-start | bytes 786440 | tf_op jit(solution)/shard_map/ppermute | solution.py:28
  10.0 18.8 %collective-permute-start.4 = (bf16[2,128,256]{2,1,0:T(8,128)(2,1)S(1)}, bf16[2,128,256]{2,1,0:T(8,128)(2,1)S(1)}, u32[]{:S(2)}, u32[]{:S(2)}) collective-permute-start(bf16[2,128,256]{2,1,0:T(8,128)(2,1)S(1)} %get-tuple-element.30), channel_id=1, source_target_pairs={{0,12},{4,8},{8,4},{12,0},{1,13},{5,9},{9,5},{13,1},{2,14},{6,10},... | collective-permute-start | bytes 393224 | tf_op jit(solution)/shard_map/ppermute | solution.py:28
  11.9 15.6 %collective-permute-start.3 = (bf16[2,256,256]{2,1,0:T(8,128)(2,1)S(1)}, bf16[2,256,256]{2,1,0:T(8,128)(2,1)S(1)}, u32[]{:S(2)}, u32[]{:S(2)}) collective-permute-start(bf16[2,256,256]{2,1,0:T(8,128)(2,1)S(1)} %get-tuple-element.29), channel_id=1, source_target_pairs={{0,4},{4,0},{8,12},{12,8},{1,5},{5,1},{9,13},{13,9},{2,6},{6,2},{1... | collective-permute-start | bytes 786440 | tf_op jit(solution)/shard_map/ppermute | solution.py:28
  18.0 1.2 %collective-permute-start = (f32[3,512]{1,0:T(4,128)S(1)}, f32[3,512]{1,0:T(4,128)S(1)}, u32[]{:S(2)}, u32[]{:S(2)}) collective-permute-start(f32[3,512]{1,0:T(4,128)S(1)} %get-tuple-element.28), channel_id=1, source_target_pairs={{0,1},{1,0},{2,3},{3,2},{4,5},{5,4},{6,7},{7,6},{8,9},{9,8},{10,11... | collective-permute-start | bytes 18440 | tf_op jit(solution)/shard_map/ppermute | solution.py:28
  29.5 6.0 %collective-permute-start.7 = (bf16[160,128]{1,0:T(8,128)(2,1)S(1)}, bf16[160,128]{1,0:T(8,128)(2,1)S(1)}, u32[]{:S(2)}, u32[]{:S(2)}) collective-permute-start(bf16[160,128]{1,0:T(8,128)(2,1)S(1)} %get-tuple-element.34), channel_id=1, source_target_pairs={{0,9},{1,8},{4,13},{5,12},{8,1},{9,0},{12,5},{13,4},{2,11},{3,10},... | collective-permute-start | bytes 122888 | tf_op jit(solution)/shard_map/ppermute | solution.py:28
  30.2 5.3 %collective-permute-start.6 = (bf16[144,128]{1,0:T(8,128)(2,1)S(1)}, bf16[144,128]{1,0:T(8,128)(2,1)S(1)}, u32[]{:S(2)}, u32[]{:S(2)}) collective-permute-start(bf16[144,128]{1,0:T(8,128)(2,1)S(1)} %get-tuple-element.31.refs_0_), channel_id=1, source_target_pairs={{0,8},{4,12},{8,0},{12,4},{1,9},{5,13},{9,1},{13,5},{2,10},{6,14},... | collective-permute-start | bytes 110600 | tf_op jit(solution)/shard_map/ppermute | solution.py:28
  31.3 1.9 %collective-permute-start.5 = (bf16[128,128]{1,0:T(8,128)(2,1)S(1)}, bf16[128,128]{1,0:T(8,128)(2,1)S(1)}, u32[]{:S(2)}, u32[]{:S(2)}) collective-permute-start(bf16[128,128]{1,0:T(8,128)(2,1)S(1)} %get-tuple-element.33), channel_id=1, source_target_pairs={{0,1},{1,0},{2,3},{3,2},{4,5},{5,4},{6,7},{7,6},{8,9},{9,8},{10,11... | collective-permute-start | bytes 98312 | tf_op jit(solution)/shard_map/ppermute | solution.py:28
  35.7 7.3 %collective-permute-start.10 = (bf16[288,128]{1,0:T(8,128)(2,1)S(1)}, bf16[288,128]{1,0:T(8,128)(2,1)S(1)}, u32[]{:S(2)}, u32[]{:S(2)}) collective-permute-start(bf16[288,128]{1,0:T(8,128)(2,1)S(1)} %get-tuple-element.38), channel_id=1, source_target_pairs={{0,6},{2,4},{4,2},{6,0},{8,14},{10,12},{12,10},{14,8},{1,7},{3,5},... | collective-permute-start | bytes 221192 | tf_op jit(solution)/shard_map/ppermute | solution.py:28
  36.5 6.5 %collective-permute-start.8 = (bf16[272,128]{1,0:T(8,128)(2,1)S(1)}, bf16[272,128]{1,0:T(8,128)(2,1)S(1)}, u32[]{:S(2)}, u32[]{:S(2)}) collective-permute-start(bf16[272,128]{1,0:T(8,128)(2,1)S(1)} %get-tuple-element.36), channel_id=1, source_target_pairs={{0,4},{4,0},{8,12},{12,8},{1,5},{5,1},{9,13},{13,9},{2,6},{6,2},{1... | collective-permute-start | bytes 208904 | tf_op jit(solution)/shard_map/ppermute | solution.py:28
  38.7 4.3 %collective-permute-start.9 = (bf16[256,128]{1,0:T(8,128)(2,1)S(1)}, bf16[256,128]{1,0:T(8,128)(2,1)S(1)}, u32[]{:S(2)}, u32[]{:S(2)}) collective-permute-start(bf16[256,128]{1,0:T(8,128)(2,1)S(1)} %get-tuple-element.37), channel_id=1, source_target_pairs={{0,2},{2,0},{1,3},{3,1},{4,6},{6,4},{5,7},{7,5},{8,10},{10,8},{9,1... | collective-permute-start | bytes 196616 | tf_op jit(solution)/shard_map/ppermute | solution.py:28

commit v9 on v8

--- a/solution.py
+++ b/solution.py
@@ -37,7 +37,7 @@
     per_dev = lax.axis_size("beam")
     start = min(first for _, first, _ in pieces)
     stop = max(last for _, _, last in pieces)
-    group = max(16, (stop - start) // 4)
+    group = max(16, (stop - start) // 2)
     jobs = [(p, first) for first in range(start, stop, group) for p in range(parts)]
     lanes = range(0, samples, 128)
     tokens = [] if token is None else [token]

time: 43.9 us -> 43.8 us (level)
  no operation moved by 1% of the time
where the time goes in v9:
time: 43.8 us; the launch traced here: 43.7 us
  Pallas kernels  16.4 us (37%)
  starting transfers between devices  15.2 us (35%)
  waiting for transfers between devices  11.9 us (27%)
    ppermute x11, starting transfers between devices, partner(): return lax.ppermute(value, axes, pairs)  15.2 us
    ppermute x11, waiting for transfers between devices, partner(): return lax.ppermute(value, axes, pairs)  11.9 us
    pallas_call x3, Pallas kernels, split_channels(): pl.pallas_call(kernel, in_specs=[pl.BlockSpec(memory_space=place)] + [pl....  4.62 us
    pallas_call x1, Pallas kernels, our_weights(): pl.pallas_call(kernel, in_specs=[SMEM] * 2 + [VMEM] * 4, out_specs=[VMEM]...  4.52 us
    pallas_call x1, Pallas kernels, their_weights(): pl.pallas_call(kernel, in_specs=[VMEM] * 3, out_specs=VMEM, out_shape=jax...  3.15 us
    pallas_call x2, Pallas kernels, early_beams(): pl.pallas_call(kernel, in_specs=[VMEM] * (2 + len(before) + len(chunks)),...  2.49 us
  transfers between devices with their start and end apart: 11, of which 6 were waited for; matrix products, arithmetic and copies ran while one was open for 0% of the time, Pallas kernels for 31%

profile of v9, /device:TPU:0, one launch (start us, length us, event | category | flops | bytes accessed | tf_op | source)
XLA Modules:
  0.0 43.7 jit_solution(14353856631434893958)
XLA Ops:
  0.0 1.3 %split_channels.3.refs_0_ = bf16[2,128,256]{2,1,0:T(8,128)(2,1)S(1)} custom-call(bf16[2,2048,256]{2,1,0:T(8,128)(2,1)} %bitcast.6), custom_call_target="tpu_custom_call" | custom-call | tf_op jit(solution)/shard_map/split_channels/pallas_call | solution.py:77
  1.3 5.1 %collective-permute-start.1 = (bf16[2,128,256]{2,1,0:T(8,128)(2,1)S(1)}, bf16[2,128,256]{2,1,0:T(8,128)(2,1)S(1)}, u32[]{:S(2)}, u32[]{:S(2)}) collective-permute-start(bf16[2,128,256]{2,1,0:T(8,128)(2,1)S(1)} %split_channels.3.refs_0_), channel_id=1, source_target_pairs={{0,12},{4,8},{8,4},{12,0},{1,13},{5,9},{9,5},{13,1},{2,14},{6,10},... | collective-permute-start | bytes 393224 | tf_op jit(solution)/shard_map/ppermute | solution.py:28
  6.5 1.6 %split_channels.4.refs_0_ = bf16[2,256,256]{2,1,0:T(8,128)(2,1)S(1)} custom-call(bf16[2,2048,256]{2,1,0:T(8,128)(2,1)} %bitcast.7, bf16[2,128,256]{2,1,0:T(8,128)(2,1)S(1)} %split_channels.3.refs_0_), custom_call_target="tpu_custom_call" | custom-call | tf_op jit(solution)/shard_map/split_channels/pallas_call | solution.py:77
  8.2 1.7 %split_channels.5 = (bf16[2,256,256]{2,1,0:T(8,128)(2,1)S(1)}, bf16[2,256,256]{2,1,0:T(8,128)(2,1)S(1)}, bf16[2,128,256]{2,1,0:T(8,128)(2,1)S(1)}) custom-call(bf16[2,2048,256]{2,1,0:T(8,128)(2,1)} %bitcast.8, bf16[2,256,256]{2,1,0:T(8,128)(2,1)S(1)} %split_channels.4.refs_0_), custom_call_target="tpu_custom_call" | custom-call | tf_op jit(solution)/shard_map/split_channels/pallas_call | solution.py:77
  9.9 2.0 %collective-permute-start.4 = (bf16[2,128,256]{2,1,0:T(8,128)(2,1)S(1)}, bf16[2,128,256]{2,1,0:T(8,128)(2,1)S(1)}, u32[]{:S(2)}, u32[]{:S(2)}) collective-permute-start(bf16[2,128,256]{2,1,0:T(8,128)(2,1)S(1)} %get-tuple-element.30), channel_id=1, source_target_pairs={{0,12},{4,8},{8,4},{12,0},{1,13},{5,9},{9,5},{13,1},{2,14},{6,10},... | collective-permute-start | bytes 393224 | tf_op jit(solution)/shard_map/ppermute | solution.py:28
  11.9 1.6 %collective-permute-start.3 = (bf16[2,256,256]{2,1,0:T(8,128)(2,1)S(1)}, bf16[2,256,256]{2,1,0:T(8,128)(2,1)S(1)}, u32[]{:S(2)}, u32[]{:S(2)}) collective-permute-start(bf16[2,256,256]{2,1,0:T(8,128)(2,1)S(1)} %get-tuple-element.29), channel_id=1, source_target_pairs={{0,4},{4,0},{8,12},{12,8},{1,5},{5,1},{9,13},{13,9},{2,6},{6,2},{1... | collective-permute-start | bytes 786440 | tf_op jit(solution)/shard_map/ppermute | solution.py:28
  13.5 4.5 %our_weights.1 = (bf16[2,512,1024]{2,1,0:T(8,128)(2,1)S(1)}, bf16[32,1024]{1,0:T(8,128)(2,1)S(1)}, f32[1,1024]{1,0:T(1,128)S(1)}, f32[3,512]{1,0:T(4,128)S(1)}, bf16[2,128,160]{2,1,0:T(8,128)(2,1)S(1)}) custom-call(s32[16]{0:T(128)S(1)} %copy-done.5, s32[4,2,8]{2,1,0:T(2,128)S(1)} %copy-done.3, f32[3,1024]{1,0:T(4,128)S(1)} %copy-done, ...), custom_call_target="tpu_custom_call" | custom-call | flops 10000000000 | bytes 100000000 | tf_op jit(solution)/shard_map/our_weights/pallas_call | solution.py:245
  18.1 1.2 %collective-permute-done.dir_ref = f32[3,512]{1,0:T(4,128)S(1)} collective-permute-done((f32[3,512]{1,0:T(4,128)S(1)}, f32[3,512]{1,0:T(4,128)S(1)}, u32[]{:S(2)}, u32[]{:S(2)}) %collective-permute-start) | collective-permute-done | bytes 6176 | tf_op jit(solution)/shard_map/ppermute | solution.py:28
  19.2 3.1 %their_weights.1.theirs_ref = bf16[2,512,1024]{2,1,0:T(8,128)(2,1)S(1)} custom-call(bf16[32,1024]{1,0:T(8,128)(2,1)S(1)} %get-tuple-element.26.right_ref, f32[1,1024]{1,0:T(1,128)S(1)} %get-tuple-element.27.length_ref, f32[3,512]{1,0:T(4,128)S(1)} %collective-permute-done.dir_ref), custom_call_target="tpu_custom_call" | custom-call | tf_op jit(solution)/shard_map/their_weights/pallas_call | solution.py:273
  22.4 1.2 %early_beams.2.refs_0_ = f32[1024,512]{1,0:T(8,128)S(1)} custom-call(bf16[2,512,1024]{2,1,0:T(8,128)(2,1)S(1)} %get-tuple-element.25.ours_ref, bf16[2,512,1024]{2,1,0:T(8,128)(2,1)S(1)} %their_weights.1.theirs_ref, bf16[2,256,256]{2,1,0:T(8,128)(2,1)S(1)} %get-tuple-element.22.refs_0_, bf16[2,128,256]{2,1,0:T(8,128)(2,1)S(1)} %collective-permute-done.1.refs_1_), custom_call_target="tpu_custom_call" | custom-call | tf_op jit(solution)/shard_map/early_beams/pallas_call | solution.py:322
  23.7 3.3 %collective-permute-done.2.refs_1_ = bf16[2,256,256]{2,1,0:T(8,128)(2,1)S(1)} collective-permute-done((bf16[2,256,256]{2,1,0:T(8,128)(2,1)S(1)}, bf16[2,256,256]{2,1,0:T(8,128)(2,1)S(1)}, u32[]{:S(2)}, u32[]{:S(2)}) %collective-permute-start.2) | collective-permute-done | bytes 262176 | tf_op jit(solution)/shard_map/ppermute | solution.py:28
  26.9 0.6 %collective-permute-done.3.refs_2_ = bf16[2,256,256]{2,1,0:T(8,128)(2,1)S(1)} collective-permute-done((bf16[2,256,256]{2,1,0:T(8,128)(2,1)S(1)}, bf16[2,256,256]{2,1,0:T(8,128)(2,1)S(1)}, u32[]{:S(2)}, u32[]{:S(2)}) %collective-permute-start.3) | collective-permute-done | bytes 262176 | tf_op jit(solution)/shard_map/ppermute | solution.py:28
  27.5 1.2 %early_beams.3.part_ref = f32[1024,512]{1,0:T(8,128)S(1)} custom-call(bf16[2,512,1024]{2,1,0:T(8,128)(2,1)S(1)} %get-tuple-element.25.ours_ref, bf16[2,512,1024]{2,1,0:T(8,128)(2,1)S(1)} %their_weights.1.theirs_ref, f32[1024,512]{1,0:T(8,128)S(1)} %early_beams.2.refs_0_, bf16[2,256,256]{2,1,0:T(8,128)(2,1)S(1)} %collective-permute-done.2.refs_1_, ...), custom_call_target="tpu_custom_call" | custom-call | tf_op jit(solution)/shard_map/early_beams/pallas_call | solution.py:322
  28.8 0.7 %last_levels.1 = (bf16[144,128]{1,0:T(8,128)(2,1)S(1)}, bf16[128,128]{1,0:T(8,128)(2,1)S(1)}, bf16[128,128]{1,0:T(8,128)(2,1)S(1)}, bf16[160,128]{1,0:T(8,128)(2,1)S(1)}) custom-call(bf16[2,512,1024]{2,1,0:T(8,128)(2,1)S(1)} %get-tuple-element.25.ours_ref, bf16[2,512,1024]{2,1,0:T(8,128)(2,1)S(1)} %their_weights.1.theirs_ref, ...), custom_call_target="tpu_custom_call" | custom-call | tf_op jit(solution)/shard_map/last_levels/pallas_call | solution.py:394
  29.5 0.6 %collective-permute-start.7 = (bf16[160,128]{1,0:T(8,128)(2,1)S(1)}, bf16[160,128]{1,0:T(8,128)(2,1)S(1)}, u32[]{:S(2)}, u32[]{:S(2)}) collective-permute-start(bf16[160,128]{1,0:T(8,128)(2,1)S(1)} %get-tuple-element.34), channel_id=1, source_target_pairs={{0,9},{1,8},{4,13},{5,12},{8,1},{9,0},{12,5},{13,4},{2,11},{3,10},... | collective-permute-start | bytes 122888 | tf_op jit(solution)/shard_map/ppermute | solution.py:28
  30.1 1.1 %collective-permute-start.6 = (bf16[144,128]{1,0:T(8,128)(2,1)S(1)}, bf16[144,128]{1,0:T(8,128)(2,1)S(1)}, u32[]{:S(2)}, u32[]{:S(2)}) collective-permute-start(bf16[144,128]{1,0:T(8,128)(2,1)S(1)} %get-tuple-element.31.refs_0_), channel_id=1, source_target_pairs={{0,8},{4,12},{8,0},{12,4},{1,9},{5,13},{9,1},{13,5},{2,10},{6,14},... | collective-permute-start | bytes 110600 | tf_op jit(solution)/shard_map/ppermute | solution.py:28
  31.2 1.1 %collective-permute-start.5 = (bf16[128,128]{1,0:T(8,128)(2,1)S(1)}, bf16[128,128]{1,0:T(8,128)(2,1)S(1)}, u32[]{:S(2)}, u32[]{:S(2)}) collective-permute-start(bf16[128,128]{1,0:T(8,128)(2,1)S(1)} %get-tuple-element.33), channel_id=1, source_target_pairs={{0,1},{1,0},{2,3},{3,2},{4,5},{5,4},{6,7},{7,6},{8,9},{9,8},{10,11... | collective-permute-start | bytes 98312 | tf_op jit(solution)/shard_map/ppermute | solution.py:28
  32.3 0.9 %collective-permute-done.5.refs_2_ = bf16[128,128]{1,0:T(8,128)(2,1)S(1)} collective-permute-done((bf16[128,128]{1,0:T(8,128)(2,1)S(1)}, bf16[128,128]{1,0:T(8,128)(2,1)S(1)}, u32[]{:S(2)}, u32[]{:S(2)}) %collective-permute-start.5) | collective-permute-done | bytes 32800 | tf_op jit(solution)/shard_map/ppermute | solution.py:28
  33.1 2.3 %collective-permute-done.6.refs_3_ = bf16[144,128]{1,0:T(8,128)(2,1)S(1)} collective-permute-done((bf16[144,128]{1,0:T(8,128)(2,1)S(1)}, bf16[144,128]{1,0:T(8,128)(2,1)S(1)}, u32[]{:S(2)}, u32[]{:S(2)}) %collective-permute-start.6) | collective-permute-done | bytes 36896 | tf_op jit(solution)/shard_map/ppermute | solution.py:28
  35.7 0.8 %collective-permute-start.10 = (bf16[288,128]{1,0:T(8,128)(2,1)S(1)}, bf16[288,128]{1,0:T(8,128)(2,1)S(1)}, u32[]{:S(2)}, u32[]{:S(2)}) collective-permute-start(bf16[288,128]{1,0:T(8,128)(2,1)S(1)} %get-tuple-element.38), channel_id=1, source_target_pairs={{0,6},{2,4},{4,2},{6,0},{8,14},{10,12},{12,10},{14,8},{1,7},{3,5},... | collective-permute-start | bytes 221192 | tf_op jit(solution)/shard_map/ppermute | solution.py:28
  36.4 2.3 %collective-permute-start.8 = (bf16[272,128]{1,0:T(8,128)(2,1)S(1)}, bf16[272,128]{1,0:T(8,128)(2,1)S(1)}, u32[]{:S(2)}, u32[]{:S(2)}) collective-permute-start(bf16[272,128]{1,0:T(8,128)(2,1)S(1)} %get-tuple-element.36), channel_id=1, source_target_pairs={{0,4},{4,0},{8,12},{12,8},{1,5},{5,1},{9,13},{13,9},{2,6},{6,2},{1... | collective-permute-start | bytes 208904 | tf_op jit(solution)/shard_map/ppermute | solution.py:28
  38.7 0.5 %collective-permute-start.9 = (bf16[256,128]{1,0:T(8,128)(2,1)S(1)}, bf16[256,128]{1,0:T(8,128)(2,1)S(1)}, u32[]{:S(2)}, u32[]{:S(2)}) collective-permute-start(bf16[256,128]{1,0:T(8,128)(2,1)S(1)} %get-tuple-element.37), channel_id=1, source_target_pairs={{0,2},{2,0},{1,3},{3,1},{4,6},{6,4},{5,7},{7,5},{8,10},{10,8},{9,1... | collective-permute-start | bytes 196616 | tf_op jit(solution)/shard_map/ppermute | solution.py:28
  39.2 3.7 %collective-permute-done.9.refs_1_ = bf16[256,128]{1,0:T(8,128)(2,1)S(1)} collective-permute-done((bf16[256,128]{1,0:T(8,128)(2,1)S(1)}, bf16[256,128]{1,0:T(8,128)(2,1)S(1)}, u32[]{:S(2)}, u32[]{:S(2)}) %collective-permute-start.9) | collective-permute-done | bytes 65568 | tf_op jit(solution)/shard_map/ppermute | solution.py:28
  43.0 0.7 %tree_sum.1 = f32[2,32,512]{2,1,0:T(8,128)} custom-call(f32[2,32,512]{2,1,0:T(8,128)S(1)} %get-tuple-element.35.own_ref, bf16[272,128]{1,0:T(8,128)(2,1)S(1)} %collective-permute-done.8.refs_0_, bf16[256,128]{1,0:T(8,128)(2,1)S(1)} %collective-permute-done.9.refs_1_, bf16[288,128]{1,0:T(8,128)(2,1)S(1)} %collective-permute-done.10.refs_2_), custom_call_target="tpu_custom_call" | custom-call | tf_op jit(solution)/shard_map/tree_sum/pallas_call | solution.py:456
  (20 shorter events, 0.4 us)
Async XLA Ops:
  1.3 12.2 %copy-start = (f32[3,1024]{1,0:T(4,128)S(1)}, f32[3,1024]{1,0:T(4,128)}, u32[]{:S(2)}) copy-start(f32[3,1024]{1,0:T(4,128)} %pos_ref) | copy-start | bytes 36868
  1.3 12.2 %copy-start.1 = (f32[2,1,2,1024]{3,2,1,0:T(2,128)S(1)}, f32[2,1,2,1024]{3,2,1,0:T(2,128)}, u32[]{:S(2)}) copy-start(f32[2,1,2,1024]{3,2,1,0:T(2,128)} %param.8) | copy-start | bytes 49156
  1.3 12.1 %copy-start.2 = (f32[3,512]{1,0:T(4,128)S(1)}, f32[3,512]{1,0:T(4,128)}, u32[]{:S(2)}) copy-start(f32[3,512]{1,0:T(4,128)} %dir_ref.1) | copy-start | bytes 18436
  1.3 12.1 %copy-start.3 = (s32[4,2,8]{2,1,0:T(2,128)S(1)}, s32[4,2,8]{2,1,0:T(2,128)}, u32[]{:S(2)}) copy-start(s32[4,2,8]{2,1,0:T(2,128)} %delay_ref.1) | copy-start | bytes 772
  1.3 12.1 %copy-start.4 = (s32[1024]{0:T(1024)S(1)}, s32[1024]{0:T(1024)}, u32[]{:S(2)}) copy-start(s32[1024]{0:T(1024)} %param.11) | copy-start | bytes 12292
  1.3 12.1 %copy-start.5 = (s32[16]{0:T(128)S(1)}, s32[16]{0:T(128)}, u32[]{:S(2)}) copy-start(s32[16]{0:T(128)} %order_ref.1) | copy-start | bytes 196
  1.3 21.0 %collective-permute-start.1 = (bf16[2,128,256]{2,1,0:T(8,128)(2,1)S(1)}, bf16[2,128,256]{2,1,0:T(8,128)(2,1)S(1)}, u32[]{:S(2)}, u32[]{:S(2)}) collective-permute-start(bf16[2,128,256]{2,1,0:T(8,128)(2,1)S(1)} %split_channels.3.refs_0_), channel_id=1, source_target_pairs={{0,12},{4,8},{8,4},{12,0},{1,13},{5,9},{9,5},{13,1},{2,14},{6,10},... | collective-permute-start | bytes 393224 | tf_op jit(solution)/shard_map/ppermute | solution.py:28
  8.1 18.8 %collective-permute-start.2 = (bf16[2,256,256]{2,1,0:T(8,128)(2,1)S(1)}, bf16[2,256,256]{2,1,0:T(8,128)(2,1)S(1)}, u32[]{:S(2)}, u32[]{:S(2)}) collective-permute-start(bf16[2,256,256]{2,1,0:T(8,128)(2,1)S(1)} %split_channels.4.refs_0_), channel_id=1, source_target_pairs={{0,8},{4,12},{8,0},{12,4},{1,9},{5,13},{9,1},{13,5},{2,10},{6,14},... | collective-permute-start | bytes 786440 | tf_op jit(solution)/shard_map/ppermute | solution.py:28
  9.9 18.8 %collective-permute-start.4 = (bf16[2,128,256]{2,1,0:T(8,128)(2,1)S(1)}, bf16[2,128,256]{2,1,0:T(8,128)(2,1)S(1)}, u32[]{:S(2)}, u32[]{:S(2)}) collective-permute-start(bf16[2,128,256]{2,1,0:T(8,128)(2,1)S(1)} %get-tuple-element.30), channel_id=1, source_target_pairs={{0,12},{4,8},{8,4},{12,0},{1,13},{5,9},{9,5},{13,1},{2,14},{6,10},... | collective-permute-start | bytes 393224 | tf_op jit(solution)/shard_map/ppermute | solution.py:28
  11.9 15.6 %collective-permute-start.3 = (bf16[2,256,256]{2,1,0:T(8,128)(2,1)S(1)}, bf16[2,256,256]{2,1,0:T(8,128)(2,1)S(1)}, u32[]{:S(2)}, u32[]{:S(2)}) collective-permute-start(bf16[2,256,256]{2,1,0:T(8,128)(2,1)S(1)} %get-tuple-element.29), channel_id=1, source_target_pairs={{0,4},{4,0},{8,12},{12,8},{1,5},{5,1},{9,13},{13,9},{2,6},{6,2},{1... | collective-permute-start | bytes 786440 | tf_op jit(solution)/shard_map/ppermute | solution.py:28
  18.0 1.2 %collective-permute-start = (f32[3,512]{1,0:T(4,128)S(1)}, f32[3,512]{1,0:T(4,128)S(1)}, u32[]{:S(2)}, u32[]{:S(2)}) collective-permute-start(f32[3,512]{1,0:T(4,128)S(1)} %get-tuple-element.28), channel_id=1, source_target_pairs={{0,1},{1,0},{2,3},{3,2},{4,5},{5,4},{6,7},{7,6},{8,9},{9,8},{10,11... | collective-permute-start | bytes 18440 | tf_op jit(solution)/shard_map/ppermute | solution.py:28
  29.5 6.0 %collective-permute-start.7 = (bf16[160,128]{1,0:T(8,128)(2,1)S(1)}, bf16[160,128]{1,0:T(8,128)(2,1)S(1)}, u32[]{:S(2)}, u32[]{:S(2)}) collective-permute-start(bf16[160,128]{1,0:T(8,128)(2,1)S(1)} %get-tuple-element.34), channel_id=1, source_target_pairs={{0,9},{1,8},{4,13},{5,12},{8,1},{9,0},{12,5},{13,4},{2,11},{3,10},... | collective-permute-start | bytes 122888 | tf_op jit(solution)/shard_map/ppermute | solution.py:28
  30.1 5.4 %collective-permute-start.6 = (bf16[144,128]{1,0:T(8,128)(2,1)S(1)}, bf16[144,128]{1,0:T(8,128)(2,1)S(1)}, u32[]{:S(2)}, u32[]{:S(2)}) collective-permute-start(bf16[144,128]{1,0:T(8,128)(2,1)S(1)} %get-tuple-element.31.refs_0_), channel_id=1, source_target_pairs={{0,8},{4,12},{8,0},{12,4},{1,9},{5,13},{9,1},{13,5},{2,10},{6,14},... | collective-permute-start | bytes 110600 | tf_op jit(solution)/shard_map/ppermute | solution.py:28
  31.2 2.0 %collective-permute-start.5 = (bf16[128,128]{1,0:T(8,128)(2,1)S(1)}, bf16[128,128]{1,0:T(8,128)(2,1)S(1)}, u32[]{:S(2)}, u32[]{:S(2)}) collective-permute-start(bf16[128,128]{1,0:T(8,128)(2,1)S(1)} %get-tuple-element.33), channel_id=1, source_target_pairs={{0,1},{1,0},{2,3},{3,2},{4,5},{5,4},{6,7},{7,6},{8,9},{9,8},{10,11... | collective-permute-start | bytes 98312 | tf_op jit(solution)/shard_map/ppermute | solution.py:28
  35.7 7.3 %collective-permute-start.10 = (bf16[288,128]{1,0:T(8,128)(2,1)S(1)}, bf16[288,128]{1,0:T(8,128)(2,1)S(1)}, u32[]{:S(2)}, u32[]{:S(2)}) collective-permute-start(bf16[288,128]{1,0:T(8,128)(2,1)S(1)} %get-tuple-element.38), channel_id=1, source_target_pairs={{0,6},{2,4},{4,2},{6,0},{8,14},{10,12},{12,10},{14,8},{1,7},{3,5},... | collective-permute-start | bytes 221192 | tf_op jit(solution)/shard_map/ppermute | solution.py:28
  36.4 6.5 %collective-permute-start.8 = (bf16[272,128]{1,0:T(8,128)(2,1)S(1)}, bf16[272,128]{1,0:T(8,128)(2,1)S(1)}, u32[]{:S(2)}, u32[]{:S(2)}) collective-permute-start(bf16[272,128]{1,0:T(8,128)(2,1)S(1)} %get-tuple-element.36), channel_id=1, source_target_pairs={{0,4},{4,0},{8,12},{12,8},{1,5},{5,1},{9,13},{13,9},{2,6},{6,2},{1... | collective-permute-start | bytes 208904 | tf_op jit(solution)/shard_map/ppermute | solution.py:28
  38.7 4.3 %collective-permute-start.9 = (bf16[256,128]{1,0:T(8,128)(2,1)S(1)}, bf16[256,128]{1,0:T(8,128)(2,1)S(1)}, u32[]{:S(2)}, u32[]{:S(2)}) collective-permute-start(bf16[256,128]{1,0:T(8,128)(2,1)S(1)} %get-tuple-element.37), channel_id=1, source_target_pairs={{0,2},{2,0},{1,3},{3,1},{4,6},{6,4},{5,7},{7,5},{8,10},{10,8},{9,1... | collective-permute-start | bytes 196616 | tf_op jit(solution)/shard_map/ppermute | solution.py:28

commit v10 on v9

--- a/solution.py
+++ b/solution.py
@@ -295,8 +295,8 @@
     return dot(w_ref[0, beam_rows, cols], straight) + dot(w_ref[1, beam_rows, cols], turned)
 
 
-HIGH_EXTRA, OTHER_EXTRA = 1, (0, 2)
-SUM_EXTRA = (1, 0, 2)
+HIGH_EXTRA, OTHER_EXTRA = 1, (1, 0)
+SUM_EXTRA = (0, 0, 1)
 
 
 def filled(ref, before, after):

time: 43.8 us -> 44 us (level)
  transfers between devices with their start and end apart: 11 -> 11, of which waited for: 6 -> 5; matrix products, arithmetic and copies ran while one was open for 0% -> 0% of each run, Pallas kernels for 31% -> 31%
where the time goes in v10:
time: 44 us; the launch traced here: 43.8 us
  Pallas kernels  16.4 us (37%)
  starting transfers between devices  15.2 us (35%)
  waiting for transfers between devices  12 us (27%)
    ppermute x11, starting transfers between devices, partner(): return lax.ppermute(value, axes, pairs)  15.2 us
    ppermute x11, waiting for transfers between devices, partner(): return lax.ppermute(value, axes, pairs)  12 us
    pallas_call x3, Pallas kernels, split_channels(): pl.pallas_call(kernel, in_specs=[pl.BlockSpec(memory_space=place)] + [pl....  4.62 us
    pallas_call x1, Pallas kernels, our_weights(): pl.pallas_call(kernel, in_specs=[SMEM] * 2 + [VMEM] * 4, out_specs=[VMEM]...  4.52 us
    pallas_call x1, Pallas kernels, their_weights(): pl.pallas_call(kernel, in_specs=[VMEM] * 3, out_specs=VMEM, out_shape=jax...  3.15 us
    pallas_call x2, Pallas kernels, early_beams(): pl.pallas_call(kernel, in_specs=[VMEM] * (2 + len(before) + len(chunks)),...  2.49 us
  transfers between devices with their start and end apart: 11, of which 5 were waited for; matrix products, arithmetic and copies ran while one was open for 0% of the time, Pallas kernels for 31%

profile of v10, /device:TPU:0, one launch (start us, length us, event | category | flops | bytes accessed | tf_op | source)
XLA Modules:
  0.0 43.8 jit_solution(14768507613496130633)
XLA Ops:
  0.0 1.3 %split_channels.3.refs_0_ = bf16[2,128,256]{2,1,0:T(8,128)(2,1)S(1)} custom-call(bf16[2,2048,256]{2,1,0:T(8,128)(2,1)} %bitcast.6), custom_call_target="tpu_custom_call" | custom-call | tf_op jit(solution)/shard_map/split_channels/pallas_call | solution.py:77
  1.3 5.1 %collective-permute-start.1 = (bf16[2,128,256]{2,1,0:T(8,128)(2,1)S(1)}, bf16[2,128,256]{2,1,0:T(8,128)(2,1)S(1)}, u32[]{:S(2)}, u32[]{:S(2)}) collective-permute-start(bf16[2,128,256]{2,1,0:T(8,128)(2,1)S(1)} %split_channels.3.refs_0_), channel_id=1, source_target_pairs={{0,12},{4,8},{8,4},{12,0},{1,13},{5,9},{9,5},{13,1},{2,14},{6,10},... | collective-permute-start | bytes 393224 | tf_op jit(solution)/shard_map/ppermute | solution.py:28
  6.5 1.6 %split_channels.4.refs_0_ = bf16[2,256,256]{2,1,0:T(8,128)(2,1)S(1)} custom-call(bf16[2,2048,256]{2,1,0:T(8,128)(2,1)} %bitcast.7, bf16[2,128,256]{2,1,0:T(8,128)(2,1)S(1)} %split_channels.3.refs_0_), custom_call_target="tpu_custom_call" | custom-call | tf_op jit(solution)/shard_map/split_channels/pallas_call | solution.py:77
  8.1 0.1 collective-permute-start.2
  8.2 1.7 %split_channels.5 = (bf16[2,256,256]{2,1,0:T(8,128)(2,1)S(1)}, bf16[2,256,256]{2,1,0:T(8,128)(2,1)S(1)}, bf16[2,128,256]{2,1,0:T(8,128)(2,1)S(1)}) custom-call(bf16[2,2048,256]{2,1,0:T(8,128)(2,1)} %bitcast.8, bf16[2,256,256]{2,1,0:T(8,128)(2,1)S(1)} %split_channels.4.refs_0_), custom_call_target="tpu_custom_call" | custom-call | tf_op jit(solution)/shard_map/split_channels/pallas_call | solution.py:77
  9.9 2.0 %collective-permute-start.4 = (bf16[2,128,256]{2,1,0:T(8,128)(2,1)S(1)}, bf16[2,128,256]{2,1,0:T(8,128)(2,1)S(1)}, u32[]{:S(2)}, u32[]{:S(2)}) collective-permute-start(bf16[2,128,256]{2,1,0:T(8,128)(2,1)S(1)} %get-tuple-element.30), channel_id=1, source_target_pairs={{0,12},{4,8},{8,4},{12,0},{1,13},{5,9},{9,5},{13,1},{2,14},{6,10},... | collective-permute-start | bytes 393224 | tf_op jit(solution)/shard_map/ppermute | solution.py:28
  11.9 1.6 %collective-permute-start.3 = (bf16[2,256,256]{2,1,0:T(8,128)(2,1)S(1)}, bf16[2,256,256]{2,1,0:T(8,128)(2,1)S(1)}, u32[]{:S(2)}, u32[]{:S(2)}) collective-permute-start(bf16[2,256,256]{2,1,0:T(8,128)(2,1)S(1)} %get-tuple-element.29), channel_id=1, source_target_pairs={{0,4},{4,0},{8,12},{12,8},{1,5},{5,1},{9,13},{13,9},{2,6},{6,2},{1... | collective-permute-start | bytes 786440 | tf_op jit(solution)/shard_map/ppermute | solution.py:28
  13.5 4.5 %our_weights.1 = (bf16[2,512,1024]{2,1,0:T(8,128)(2,1)S(1)}, bf16[32,1024]{1,0:T(8,128)(2,1)S(1)}, f32[1,1024]{1,0:T(1,128)S(1)}, f32[3,512]{1,0:T(4,128)S(1)}, bf16[2,128,160]{2,1,0:T(8,128)(2,1)S(1)}) custom-call(s32[16]{0:T(128)S(1)} %copy-done.5, s32[4,2,8]{2,1,0:T(2,128)S(1)} %copy-done.3, f32[3,1024]{1,0:T(4,128)S(1)} %copy-done, ...), custom_call_target="tpu_custom_call" | custom-call | flops 10000000000 | bytes 100000000 | tf_op jit(solution)/shard_map/our_weights/pallas_call | solution.py:245
  18.1 1.2 %collective-permute-done.dir_ref = f32[3,512]{1,0:T(4,128)S(1)} collective-permute-done((f32[3,512]{1,0:T(4,128)S(1)}, f32[3,512]{1,0:T(4,128)S(1)}, u32[]{:S(2)}, u32[]{:S(2)}) %collective-permute-start) | collective-permute-done | bytes 6176 | tf_op jit(solution)/shard_map/ppermute | solution.py:28
  19.2 3.1 %their_weights.1.theirs_ref = bf16[2,512,1024]{2,1,0:T(8,128)(2,1)S(1)} custom-call(bf16[32,1024]{1,0:T(8,128)(2,1)S(1)} %get-tuple-element.26.right_ref, f32[1,1024]{1,0:T(1,128)S(1)} %get-tuple-element.27.length_ref, f32[3,512]{1,0:T(4,128)S(1)} %collective-permute-done.dir_ref), custom_call_target="tpu_custom_call" | custom-call | tf_op jit(solution)/shard_map/their_weights/pallas_call | solution.py:273
  22.4 1.2 %early_beams.2.refs_0_ = f32[1024,512]{1,0:T(8,128)S(1)} custom-call(bf16[2,512,1024]{2,1,0:T(8,128)(2,1)S(1)} %get-tuple-element.25.ours_ref, bf16[2,512,1024]{2,1,0:T(8,128)(2,1)S(1)} %their_weights.1.theirs_ref, bf16[2,256,256]{2,1,0:T(8,128)(2,1)S(1)} %get-tuple-element.22.refs_0_, bf16[2,128,256]{2,1,0:T(8,128)(2,1)S(1)} %collective-permute-done.1.refs_1_), custom_call_target="tpu_custom_call" | custom-call | tf_op jit(solution)/shard_map/early_beams/pallas_call | solution.py:322
  23.7 3.3 %collective-permute-done.2.refs_1_ = bf16[2,256,256]{2,1,0:T(8,128)(2,1)S(1)} collective-permute-done((bf16[2,256,256]{2,1,0:T(8,128)(2,1)S(1)}, bf16[2,256,256]{2,1,0:T(8,128)(2,1)S(1)}, u32[]{:S(2)}, u32[]{:S(2)}) %collective-permute-start.2) | collective-permute-done | bytes 262176 | tf_op jit(solution)/shard_map/ppermute | solution.py:28
  26.9 0.6 %collective-permute-done.3.refs_2_ = bf16[2,256,256]{2,1,0:T(8,128)(2,1)S(1)} collective-permute-done((bf16[2,256,256]{2,1,0:T(8,128)(2,1)S(1)}, bf16[2,256,256]{2,1,0:T(8,128)(2,1)S(1)}, u32[]{:S(2)}, u32[]{:S(2)}) %collective-permute-start.3) | collective-permute-done | bytes 262176 | tf_op jit(solution)/shard_map/ppermute | solution.py:28
  27.5 1.2 %early_beams.3.part_ref = f32[1024,512]{1,0:T(8,128)S(1)} custom-call(bf16[2,512,1024]{2,1,0:T(8,128)(2,1)S(1)} %get-tuple-element.25.ours_ref, bf16[2,512,1024]{2,1,0:T(8,128)(2,1)S(1)} %their_weights.1.theirs_ref, f32[1024,512]{1,0:T(8,128)S(1)} %early_beams.2.refs_0_, bf16[2,256,256]{2,1,0:T(8,128)(2,1)S(1)} %collective-permute-done.2.refs_1_, ...), custom_call_target="tpu_custom_call" | custom-call | tf_op jit(solution)/shard_map/early_beams/pallas_call | solution.py:322
  28.8 0.7 %last_levels.1 = (bf16[144,128]{1,0:T(8,128)(2,1)S(1)}, bf16[128,128]{1,0:T(8,128)(2,1)S(1)}, bf16[144,128]{1,0:T(8,128)(2,1)S(1)}, bf16[128,128]{1,0:T(8,128)(2,1)S(1)}) custom-call(bf16[2,512,1024]{2,1,0:T(8,128)(2,1)S(1)} %get-tuple-element.25.ours_ref, bf16[2,512,1024]{2,1,0:T(8,128)(2,1)S(1)} %their_weights.1.theirs_ref, ...), custom_call_target="tpu_custom_call" | custom-call | tf_op jit(solution)/shard_map/last_levels/pallas_call | solution.py:394
  29.5 1.7 %collective-permute-start.6 = (bf16[144,128]{1,0:T(8,128)(2,1)S(1)}, bf16[144,128]{1,0:T(8,128)(2,1)S(1)}, u32[]{:S(2)}, u32[]{:S(2)}) collective-permute-start(bf16[144,128]{1,0:T(8,128)(2,1)S(1)} %get-tuple-element.31.refs_0_), channel_id=1, source_target_pairs={{0,8},{4,12},{8,0},{12,4},{1,9},{5,13},{9,1},{13,5},{2,10},{6,14},... | collective-permute-start | bytes 110600 | tf_op jit(solution)/shard_map/ppermute | solution.py:28
  31.2 1.1 %collective-permute-start.7 = (bf16[128,128]{1,0:T(8,128)(2,1)S(1)}, bf16[128,128]{1,0:T(8,128)(2,1)S(1)}, u32[]{:S(2)}, u32[]{:S(2)}) collective-permute-start(bf16[128,128]{1,0:T(8,128)(2,1)S(1)} %get-tuple-element.34), channel_id=1, source_target_pairs={{0,9},{1,8},{4,13},{5,12},{8,1},{9,0},{12,5},{13,4},{2,11},{3,10},... | collective-permute-start | bytes 98312 | tf_op jit(solution)/shard_map/ppermute | solution.py:28
  32.3 3.2 %collective-permute-done.7.refs_4_ = bf16[128,128]{1,0:T(8,128)(2,1)S(1)} collective-permute-done((bf16[128,128]{1,0:T(8,128)(2,1)S(1)}, bf16[128,128]{1,0:T(8,128)(2,1)S(1)}, u32[]{:S(2)}, u32[]{:S(2)}) %collective-permute-start.7) | collective-permute-done | bytes 32800 | tf_op jit(solution)/shard_map/ppermute | solution.py:28
  35.5 0.2 tree_stage.1
  35.8 2.2 %collective-permute-start.10 = (bf16[272,128]{1,0:T(8,128)(2,1)S(1)}, bf16[272,128]{1,0:T(8,128)(2,1)S(1)}, u32[]{:S(2)}, u32[]{:S(2)}) collective-permute-start(bf16[272,128]{1,0:T(8,128)(2,1)S(1)} %get-tuple-element.38), channel_id=1, source_target_pairs={{0,6},{2,4},{4,2},{6,0},{8,14},{10,12},{12,10},{14,8},{1,7},{3,5},... | collective-permute-start | bytes 208904 | tf_op jit(solution)/shard_map/ppermute | solution.py:28
  38.0 0.8 %collective-permute-start.8 = (bf16[256,128]{1,0:T(8,128)(2,1)S(1)}, bf16[256,128]{1,0:T(8,128)(2,1)S(1)}, u32[]{:S(2)}, u32[]{:S(2)}) collective-permute-start(bf16[256,128]{1,0:T(8,128)(2,1)S(1)} %get-tuple-element.36), channel_id=1, source_target_pairs={{0,4},{4,0},{8,12},{12,8},{1,5},{5,1},{9,13},{13,9},{2,6},{6,2},{1... | collective-permute-start | bytes 196616 | tf_op jit(solution)/shard_map/ppermute | solution.py:28
  38.8 0.5 %collective-permute-start.9 = (bf16[256,128]{1,0:T(8,128)(2,1)S(1)}, bf16[256,128]{1,0:T(8,128)(2,1)S(1)}, u32[]{:S(2)}, u32[]{:S(2)}) collective-permute-start(bf16[256,128]{1,0:T(8,128)(2,1)S(1)} %get-tuple-element.37), channel_id=1, source_target_pairs={{0,2},{2,0},{1,3},{3,1},{4,6},{6,4},{5,7},{7,5},{8,10},{10,8},{9,1... | collective-permute-start | bytes 196616 | tf_op jit(solution)/shard_map/ppermute | solution.py:28
  39.3 3.7 %collective-permute-done.8.refs_0_ = bf16[256,128]{1,0:T(8,128)(2,1)S(1)} collective-permute-done((bf16[256,128]{1,0:T(8,128)(2,1)S(1)}, bf16[256,128]{1,0:T(8,128)(2,1)S(1)}, u32[]{:S(2)}, u32[]{:S(2)}) %collective-permute-start.8) | collective-permute-done | bytes 65568 | tf_op jit(solution)/shard_map/ppermute | solution.py:28
  43.1 0.7 %tree_sum.1 = f32[2,32,512]{2,1,0:T(8,128)} custom-call(f32[2,32,512]{2,1,0:T(8,128)S(1)} %get-tuple-element.35.own_ref, bf16[256,128]{1,0:T(8,128)(2,1)S(1)} %collective-permute-done.8.refs_0_, bf16[256,128]{1,0:T(8,128)(2,1)S(1)} %collective-permute-done.9.refs_1_, bf16[272,128]{1,0:T(8,128)(2,1)S(1)} %collective-permute-done.10.refs_2_), custom_call_target="tpu_custom_call" | custom-call | tf_op jit(solution)/shard_map/tree_sum/pallas_call | solution.py:456
  (20 shorter events, 0.2 us)
Async XLA Ops:
  1.3 12.2 %copy-start = (f32[3,1024]{1,0:T(4,128)S(1)}, f32[3,1024]{1,0:T(4,128)}, u32[]{:S(2)}) copy-start(f32[3,1024]{1,0:T(4,128)} %pos_ref) | copy-start | bytes 36868
  1.3 12.2 %copy-start.1 = (f32[2,1,2,1024]{3,2,1,0:T(2,128)S(1)}, f32[2,1,2,1024]{3,2,1,0:T(2,128)}, u32[]{:S(2)}) copy-start(f32[2,1,2,1024]{3,2,1,0:T(2,128)} %param.8) | copy-start | bytes 49156
  1.3 12.1 %copy-start.2 = (f32[3,512]{1,0:T(4,128)S(1)}, f32[3,512]{1,0:T(4,128)}, u32[]{:S(2)}) copy-start(f32[3,512]{1,0:T(4,128)} %dir_ref.1) | copy-start | bytes 18436
  1.3 12.1 %copy-start.3 = (s32[4,2,8]{2,1,0:T(2,128)S(1)}, s32[4,2,8]{2,1,0:T(2,128)}, u32[]{:S(2)}) copy-start(s32[4,2,8]{2,1,0:T(2,128)} %delay_ref.1) | copy-start | bytes 772
  1.3 12.1 %copy-start.4 = (s32[1024]{0:T(1024)S(1)}, s32[1024]{0:T(1024)}, u32[]{:S(2)}) copy-start(s32[1024]{0:T(1024)} %param.11) | copy-start | bytes 12292
  1.3 12.1 %copy-start.5 = (s32[16]{0:T(128)S(1)}, s32[16]{0:T(128)}, u32[]{:S(2)}) copy-start(s32[16]{0:T(128)} %order_ref.1) | copy-start | bytes 196
  1.3 21.0 %collective-permute-start.1 = (bf16[2,128,256]{2,1,0:T(8,128)(2,1)S(1)}, bf16[2,128,256]{2,1,0:T(8,128)(2,1)S(1)}, u32[]{:S(2)}, u32[]{:S(2)}) collective-permute-start(bf16[2,128,256]{2,1,0:T(8,128)(2,1)S(1)} %split_channels.3.refs_0_), channel_id=1, source_target_pairs={{0,12},{4,8},{8,4},{12,0},{1,13},{5,9},{9,5},{13,1},{2,14},{6,10},... | collective-permute-start | bytes 393224 | tf_op jit(solution)/shard_map/ppermute | solution.py:28
  8.1 18.8 %collective-permute-start.2 = (bf16[2,256,256]{2,1,0:T(8,128)(2,1)S(1)}, bf16[2,256,256]{2,1,0:T(8,128)(2,1)S(1)}, u32[]{:S(2)}, u32[]{:S(2)}) collective-permute-start(bf16[2,256,256]{2,1,0:T(8,128)(2,1)S(1)} %split_channels.4.refs_0_), channel_id=1, source_target_pairs={{0,8},{4,12},{8,0},{12,4},{1,9},{5,13},{9,1},{13,5},{2,10},{6,14},... | collective-permute-start | bytes 786440 | tf_op jit(solution)/shard_map/ppermute | solution.py:28
  9.9 18.8 %collective-permute-start.4 = (bf16[2,128,256]{2,1,0:T(8,128)(2,1)S(1)}, bf16[2,128,256]{2,1,0:T(8,128)(2,1)S(1)}, u32[]{:S(2)}, u32[]{:S(2)}) collective-permute-start(bf16[2,128,256]{2,1,0:T(8,128)(2,1)S(1)} %get-tuple-element.30), channel_id=1, source_target_pairs={{0,12},{4,8},{8,4},{12,0},{1,13},{5,9},{9,5},{13,1},{2,14},{6,10},... | collective-permute-start | bytes 393224 | tf_op jit(solution)/shard_map/ppermute | solution.py:28
  11.9 15.6 %collective-permute-start.3 = (bf16[2,256,256]{2,1,0:T(8,128)(2,1)S(1)}, bf16[2,256,256]{2,1,0:T(8,128)(2,1)S(1)}, u32[]{:S(2)}, u32[]{:S(2)}) collective-permute-start(bf16[2,256,256]{2,1,0:T(8,128)(2,1)S(1)} %get-tuple-element.29), channel_id=1, source_target_pairs={{0,4},{4,0},{8,12},{12,8},{1,5},{5,1},{9,13},{13,9},{2,6},{6,2},{1... | collective-permute-start | bytes 786440 | tf_op jit(solution)/shard_map/ppermute | solution.py:28
  18.0 1.2 %collective-permute-start = (f32[3,512]{1,0:T(4,128)S(1)}, f32[3,512]{1,0:T(4,128)S(1)}, u32[]{:S(2)}, u32[]{:S(2)}) collective-permute-start(f32[3,512]{1,0:T(4,128)S(1)} %get-tuple-element.28), channel_id=1, source_target_pairs={{0,1},{1,0},{2,3},{3,2},{4,5},{5,4},{6,7},{7,6},{8,9},{9,8},{10,11... | collective-permute-start | bytes 18440 | tf_op jit(solution)/shard_map/ppermute | solution.py:28
  29.5 6.1 %collective-permute-start.5 = (bf16[144,128]{1,0:T(8,128)(2,1)S(1)}, bf16[144,128]{1,0:T(8,128)(2,1)S(1)}, u32[]{:S(2)}, u32[]{:S(2)}) collective-permute-start(bf16[144,128]{1,0:T(8,128)(2,1)S(1)} %get-tuple-element.33), channel_id=1, source_target_pairs={{0,1},{1,0},{2,3},{3,2},{4,5},{5,4},{6,7},{7,6},{8,9},{9,8},{10,11... | collective-permute-start | bytes 110600 | tf_op jit(solution)/shard_map/ppermute | solution.py:28
  29.5 6.0 %collective-permute-start.6 = (bf16[144,128]{1,0:T(8,128)(2,1)S(1)}, bf16[144,128]{1,0:T(8,128)(2,1)S(1)}, u32[]{:S(2)}, u32[]{:S(2)}) collective-permute-start(bf16[144,128]{1,0:T(8,128)(2,1)S(1)} %get-tuple-element.31.refs_0_), channel_id=1, source_target_pairs={{0,8},{4,12},{8,0},{12,4},{1,9},{5,13},{9,1},{13,5},{2,10},{6,14},... | collective-permute-start | bytes 110600 | tf_op jit(solution)/shard_map/ppermute | solution.py:28
  31.2 4.3 %collective-permute-start.7 = (bf16[128,128]{1,0:T(8,128)(2,1)S(1)}, bf16[128,128]{1,0:T(8,128)(2,1)S(1)}, u32[]{:S(2)}, u32[]{:S(2)}) collective-permute-start(bf16[128,128]{1,0:T(8,128)(2,1)S(1)} %get-tuple-element.34), channel_id=1, source_target_pairs={{0,9},{1,8},{4,13},{5,12},{8,1},{9,0},{12,5},{13,4},{2,11},{3,10},... | collective-permute-start | bytes 98312 | tf_op jit(solution)/shard_map/ppermute | solution.py:28
  35.8 7.4 %collective-permute-start.10 = (bf16[272,128]{1,0:T(8,128)(2,1)S(1)}, bf16[272,128]{1,0:T(8,128)(2,1)S(1)}, u32[]{:S(2)}, u32[]{:S(2)}) collective-permute-start(bf16[272,128]{1,0:T(8,128)(2,1)S(1)} %get-tuple-element.38), channel_id=1, source_target_pairs={{0,6},{2,4},{4,2},{6,0},{8,14},{10,12},{12,10},{14,8},{1,7},{3,5},... | collective-permute-start | bytes 208904 | tf_op jit(solution)/shard_map/ppermute | solution.py:28
  38.0 5.1 %collective-permute-start.8 = (bf16[256,128]{1,0:T(8,128)(2,1)S(1)}, bf16[256,128]{1,0:T(8,128)(2,1)S(1)}, u32[]{:S(2)}, u32[]{:S(2)}) collective-permute-start(bf16[256,128]{1,0:T(8,128)(2,1)S(1)} %get-tuple-element.36), channel_id=1, source_target_pairs={{0,4},{4,0},{8,12},{12,8},{1,5},{5,1},{9,13},{13,9},{2,6},{6,2},{1... | collective-permute-start | bytes 196616 | tf_op jit(solution)/shard_map/ppermute | solution.py:28
  38.8 4.3 %collective-permute-start.9 = (bf16[256,128]{1,0:T(8,128)(2,1)S(1)}, bf16[256,128]{1,0:T(8,128)(2,1)S(1)}, u32[]{:S(2)}, u32[]{:S(2)}) collective-permute-start(bf16[256,128]{1,0:T(8,128)(2,1)S(1)} %get-tuple-element.37), channel_id=1, source_target_pairs={{0,2},{2,0},{1,3},{3,1},{4,6},{6,4},{5,7},{7,5},{8,10},{10,8},{9,1... | collective-permute-start | bytes 196616 | tf_op jit(solution)/shard_map/ppermute | solution.py:28

commit v11 on v10

--- a/solution.py
+++ b/solution.py
@@ -295,7 +295,7 @@
     return dot(w_ref[0, beam_rows, cols], straight) + dot(w_ref[1, beam_rows, cols], turned)
 
 
-HIGH_EXTRA, OTHER_EXTRA = 1, (1, 0)
+HIGH_EXTRA, OTHER_EXTRA = 1, (0, 2)
 SUM_EXTRA = (0, 0, 1)
 
 

time: 44 us -> 43.8 us (level)
  transfers between devices with their start and end apart: 11 -> 11, of which waited for: 5 -> 7; matrix products, arithmetic and copies ran while one was open for 0% -> 0% of each run, Pallas kernels for 31% -> 31%
where the time goes in v11:
time: 43.8 us; the launch traced here: 43.7 us
  Pallas kernels  16.4 us (37%)
  starting transfers between devices  15.2 us (35%)
  waiting for transfers between devices  11.9 us (27%)
    ppermute x11, starting transfers between devices, partner(): return lax.ppermute(value, axes, pairs)  15.2 us
    ppermute x11, waiting for transfers between devices, partner(): return lax.ppermute(value, axes, pairs)  11.9 us
    pallas_call x3, Pallas kernels, split_channels(): pl.pallas_call(kernel, in_specs=[pl.BlockSpec(memory_space=place)] + [pl....  4.62 us
    pallas_call x1, Pallas kernels, our_weights(): pl.pallas_call(kernel, in_specs=[SMEM] * 2 + [VMEM] * 4, out_specs=[VMEM]...  4.52 us
    pallas_call x1, Pallas kernels, their_weights(): pl.pallas_call(kernel, in_specs=[VMEM] * 3, out_specs=VMEM, out_shape=jax...  3.15 us
    pallas_call x2, Pallas kernels, early_beams(): pl.pallas_call(kernel, in_specs=[VMEM] * (2 + len(before) + len(chunks)),...  2.49 us
  transfers between devices with their start and end apart: 11, of which 7 were waited for; matrix products, arithmetic and copies ran while one was open for 0% of the time, Pallas kernels for 31%

profile of v11, /device:TPU:0, one launch (start us, length us, event | category | flops | bytes accessed | tf_op | source)
XLA Modules:
  0.0 43.7 jit_solution(13595502396160910664)
XLA Ops:
  0.0 1.3 %split_channels.3.refs_0_ = bf16[2,128,256]{2,1,0:T(8,128)(2,1)S(1)} custom-call(bf16[2,2048,256]{2,1,0:T(8,128)(2,1)} %bitcast.6), custom_call_target="tpu_custom_call" | custom-call | tf_op jit(solution)/shard_map/split_channels/pallas_call | solution.py:77
  1.3 5.1 %collective-permute-start.1 = (bf16[2,128,256]{2,1,0:T(8,128)(2,1)S(1)}, bf16[2,128,256]{2,1,0:T(8,128)(2,1)S(1)}, u32[]{:S(2)}, u32[]{:S(2)}) collective-permute-start(bf16[2,128,256]{2,1,0:T(8,128)(2,1)S(1)} %split_channels.3.refs_0_), channel_id=1, source_target_pairs={{0,12},{4,8},{8,4},{12,0},{1,13},{5,9},{9,5},{13,1},{2,14},{6,10},... | collective-permute-start | bytes 393224 | tf_op jit(solution)/shard_map/ppermute | solution.py:28
  6.5 1.6 %split_channels.4.refs_0_ = bf16[2,256,256]{2,1,0:T(8,128)(2,1)S(1)} custom-call(bf16[2,2048,256]{2,1,0:T(8,128)(2,1)} %bitcast.7, bf16[2,128,256]{2,1,0:T(8,128)(2,1)S(1)} %split_channels.3.refs_0_), custom_call_target="tpu_custom_call" | custom-call | tf_op jit(solution)/shard_map/split_channels/pallas_call | solution.py:77
  8.2 1.7 %split_channels.5 = (bf16[2,256,256]{2,1,0:T(8,128)(2,1)S(1)}, bf16[2,256,256]{2,1,0:T(8,128)(2,1)S(1)}, bf16[2,128,256]{2,1,0:T(8,128)(2,1)S(1)}) custom-call(bf16[2,2048,256]{2,1,0:T(8,128)(2,1)} %bitcast.8, bf16[2,256,256]{2,1,0:T(8,128)(2,1)S(1)} %split_channels.4.refs_0_), custom_call_target="tpu_custom_call" | custom-call | tf_op jit(solution)/shard_map/split_channels/pallas_call | solution.py:77
  9.9 2.0 %collective-permute-start.4 = (bf16[2,128,256]{2,1,0:T(8,128)(2,1)S(1)}, bf16[2,128,256]{2,1,0:T(8,128)(2,1)S(1)}, u32[]{:S(2)}, u32[]{:S(2)}) collective-permute-start(bf16[2,128,256]{2,1,0:T(8,128)(2,1)S(1)} %get-tuple-element.30), channel_id=1, source_target_pairs={{0,12},{4,8},{8,4},{12,0},{1,13},{5,9},{9,5},{13,1},{2,14},{6,10},... | collective-permute-start | bytes 393224 | tf_op jit(solution)/shard_map/ppermute | solution.py:28
  11.9 1.6 %collective-permute-start.3 = (bf16[2,256,256]{2,1,0:T(8,128)(2,1)S(1)}, bf16[2,256,256]{2,1,0:T(8,128)(2,1)S(1)}, u32[]{:S(2)}, u32[]{:S(2)}) collective-permute-start(bf16[2,256,256]{2,1,0:T(8,128)(2,1)S(1)} %get-tuple-element.29), channel_id=1, source_target_pairs={{0,4},{4,0},{8,12},{12,8},{1,5},{5,1},{9,13},{13,9},{2,6},{6,2},{1... | collective-permute-start | bytes 786440 | tf_op jit(solution)/shard_map/ppermute | solution.py:28
  13.5 4.5 %our_weights.1 = (bf16[2,512,1024]{2,1,0:T(8,128)(2,1)S(1)}, bf16[32,1024]{1,0:T(8,128)(2,1)S(1)}, f32[1,1024]{1,0:T(1,128)S(1)}, f32[3,512]{1,0:T(4,128)S(1)}, bf16[2,128,160]{2,1,0:T(8,128)(2,1)S(1)}) custom-call(s32[16]{0:T(128)S(1)} %copy-done.5, s32[4,2,8]{2,1,0:T(2,128)S(1)} %copy-done.3, f32[3,1024]{1,0:T(4,128)S(1)} %copy-done, ...), custom_call_target="tpu_custom_call" | custom-call | flops 10000000000 | bytes 100000000 | tf_op jit(solution)/shard_map/our_weights/pallas_call | solution.py:245
  18.1 1.2 %collective-permute-done.dir_ref = f32[3,512]{1,0:T(4,128)S(1)} collective-permute-done((f32[3,512]{1,0:T(4,128)S(1)}, f32[3,512]{1,0:T(4,128)S(1)}, u32[]{:S(2)}, u32[]{:S(2)}) %collective-permute-start) | collective-permute-done | bytes 6176 | tf_op jit(solution)/shard_map/ppermute | solution.py:28
  19.2 3.1 %their_weights.1.theirs_ref = bf16[2,512,1024]{2,1,0:T(8,128)(2,1)S(1)} custom-call(bf16[32,1024]{1,0:T(8,128)(2,1)S(1)} %get-tuple-element.26.right_ref, f32[1,1024]{1,0:T(1,128)S(1)} %get-tuple-element.27.length_ref, f32[3,512]{1,0:T(4,128)S(1)} %collective-permute-done.dir_ref), custom_call_target="tpu_custom_call" | custom-call | tf_op jit(solution)/shard_map/their_weights/pallas_call | solution.py:273
  22.4 1.2 %early_beams.2.refs_0_ = f32[1024,512]{1,0:T(8,128)S(1)} custom-call(bf16[2,512,1024]{2,1,0:T(8,128)(2,1)S(1)} %get-tuple-element.25.ours_ref, bf16[2,512,1024]{2,1,0:T(8,128)(2,1)S(1)} %their_weights.1.theirs_ref, bf16[2,256,256]{2,1,0:T(8,128)(2,1)S(1)} %get-tuple-element.22.refs_0_, bf16[2,128,256]{2,1,0:T(8,128)(2,1)S(1)} %collective-permute-done.1.refs_1_), custom_call_target="tpu_custom_call" | custom-call | tf_op jit(solution)/shard_map/early_beams/pallas_call | solution.py:322
  23.7 3.3 %collective-permute-done.2.refs_1_ = bf16[2,256,256]{2,1,0:T(8,128)(2,1)S(1)} collective-permute-done((bf16[2,256,256]{2,1,0:T(8,128)(2,1)S(1)}, bf16[2,256,256]{2,1,0:T(8,128)(2,1)S(1)}, u32[]{:S(2)}, u32[]{:S(2)}) %collective-permute-start.2) | collective-permute-done | bytes 262176 | tf_op jit(solution)/shard_map/ppermute | solution.py:28
  26.9 0.6 %collective-permute-done.3.refs_2_ = bf16[2,256,256]{2,1,0:T(8,128)(2,1)S(1)} collective-permute-done((bf16[2,256,256]{2,1,0:T(8,128)(2,1)S(1)}, bf16[2,256,256]{2,1,0:T(8,128)(2,1)S(1)}, u32[]{:S(2)}, u32[]{:S(2)}) %collective-permute-start.3) | collective-permute-done | bytes 262176 | tf_op jit(solution)/shard_map/ppermute | solution.py:28
  27.5 1.2 %early_beams.3.part_ref = f32[1024,512]{1,0:T(8,128)S(1)} custom-call(bf16[2,512,1024]{2,1,0:T(8,128)(2,1)S(1)} %get-tuple-element.25.ours_ref, bf16[2,512,1024]{2,1,0:T(8,128)(2,1)S(1)} %their_weights.1.theirs_ref, f32[1024,512]{1,0:T(8,128)S(1)} %early_beams.2.refs_0_, bf16[2,256,256]{2,1,0:T(8,128)(2,1)S(1)} %collective-permute-done.2.refs_1_, ...), custom_call_target="tpu_custom_call" | custom-call | tf_op jit(solution)/shard_map/early_beams/pallas_call | solution.py:322
  28.8 0.7 %last_levels.1 = (bf16[144,128]{1,0:T(8,128)(2,1)S(1)}, bf16[128,128]{1,0:T(8,128)(2,1)S(1)}, bf16[128,128]{1,0:T(8,128)(2,1)S(1)}, bf16[160,128]{1,0:T(8,128)(2,1)S(1)}) custom-call(bf16[2,512,1024]{2,1,0:T(8,128)(2,1)S(1)} %get-tuple-element.25.ours_ref, bf16[2,512,1024]{2,1,0:T(8,128)(2,1)S(1)} %their_weights.1.theirs_ref, ...), custom_call_target="tpu_custom_call" | custom-call | tf_op jit(solution)/shard_map/last_levels/pallas_call | solution.py:394
  29.5 0.6 %collective-permute-start.7 = (bf16[160,128]{1,0:T(8,128)(2,1)S(1)}, bf16[160,128]{1,0:T(8,128)(2,1)S(1)}, u32[]{:S(2)}, u32[]{:S(2)}) collective-permute-start(bf16[160,128]{1,0:T(8,128)(2,1)S(1)} %get-tuple-element.34), channel_id=1, source_target_pairs={{0,9},{1,8},{4,13},{5,12},{8,1},{9,0},{12,5},{13,4},{2,11},{3,10},... | collective-permute-start | bytes 122888 | tf_op jit(solution)/shard_map/ppermute | solution.py:28
  30.1 1.1 %collective-permute-start.6 = (bf16[144,128]{1,0:T(8,128)(2,1)S(1)}, bf16[144,128]{1,0:T(8,128)(2,1)S(1)}, u32[]{:S(2)}, u32[]{:S(2)}) collective-permute-start(bf16[144,128]{1,0:T(8,128)(2,1)S(1)} %get-tuple-element.31.refs_0_), channel_id=1, source_target_pairs={{0,8},{4,12},{8,0},{12,4},{1,9},{5,13},{9,1},{13,5},{2,10},{6,14},... | collective-permute-start | bytes 110600 | tf_op jit(solution)/shard_map/ppermute | solution.py:28
  31.2 1.1 %collective-permute-start.5 = (bf16[128,128]{1,0:T(8,128)(2,1)S(1)}, bf16[128,128]{1,0:T(8,128)(2,1)S(1)}, u32[]{:S(2)}, u32[]{:S(2)}) collective-permute-start(bf16[128,128]{1,0:T(8,128)(2,1)S(1)} %get-tuple-element.33), channel_id=1, source_target_pairs={{0,1},{1,0},{2,3},{3,2},{4,5},{5,4},{6,7},{7,6},{8,9},{9,8},{10,11... | collective-permute-start | bytes 98312 | tf_op jit(solution)/shard_map/ppermute | solution.py:28
  32.3 0.9 %collective-permute-done.5.refs_2_ = bf16[128,128]{1,0:T(8,128)(2,1)S(1)} collective-permute-done((bf16[128,128]{1,0:T(8,128)(2,1)S(1)}, bf16[128,128]{1,0:T(8,128)(2,1)S(1)}, u32[]{:S(2)}, u32[]{:S(2)}) %collective-permute-start.5) | collective-permute-done | bytes 32800 | tf_op jit(solution)/shard_map/ppermute | solution.py:28
  33.1 2.3 %collective-permute-done.6.refs_3_ = bf16[144,128]{1,0:T(8,128)(2,1)S(1)} collective-permute-done((bf16[144,128]{1,0:T(8,128)(2,1)S(1)}, bf16[144,128]{1,0:T(8,128)(2,1)S(1)}, u32[]{:S(2)}, u32[]{:S(2)}) %collective-permute-start.6) | collective-permute-done | bytes 36896 | tf_op jit(solution)/shard_map/ppermute | solution.py:28
  35.7 0.8 %collective-permute-start.10 = (bf16[272,128]{1,0:T(8,128)(2,1)S(1)}, bf16[272,128]{1,0:T(8,128)(2,1)S(1)}, u32[]{:S(2)}, u32[]{:S(2)}) collective-permute-start(bf16[272,128]{1,0:T(8,128)(2,1)S(1)} %get-tuple-element.38), channel_id=1, source_target_pairs={{0,6},{2,4},{4,2},{6,0},{8,14},{10,12},{12,10},{14,8},{1,7},{3,5},... | collective-permute-start | bytes 208904 | tf_op jit(solution)/shard_map/ppermute | solution.py:28
  36.4 2.3 %collective-permute-start.8 = (bf16[256,128]{1,0:T(8,128)(2,1)S(1)}, bf16[256,128]{1,0:T(8,128)(2,1)S(1)}, u32[]{:S(2)}, u32[]{:S(2)}) collective-permute-start(bf16[256,128]{1,0:T(8,128)(2,1)S(1)} %get-tuple-element.36), channel_id=1, source_target_pairs={{0,4},{4,0},{8,12},{12,8},{1,5},{5,1},{9,13},{13,9},{2,6},{6,2},{1... | collective-permute-start | bytes 196616 | tf_op jit(solution)/shard_map/ppermute | solution.py:28
  38.7 0.5 %collective-permute-start.9 = (bf16[256,128]{1,0:T(8,128)(2,1)S(1)}, bf16[256,128]{1,0:T(8,128)(2,1)S(1)}, u32[]{:S(2)}, u32[]{:S(2)}) collective-permute-start(bf16[256,128]{1,0:T(8,128)(2,1)S(1)} %get-tuple-element.37), channel_id=1, source_target_pairs={{0,2},{2,0},{1,3},{3,1},{4,6},{6,4},{5,7},{7,5},{8,10},{10,8},{9,1... | collective-permute-start | bytes 196616 | tf_op jit(solution)/shard_map/ppermute | solution.py:28
  39.2 3.5 %collective-permute-done.8.refs_0_ = bf16[256,128]{1,0:T(8,128)(2,1)S(1)} collective-permute-done((bf16[256,128]{1,0:T(8,128)(2,1)S(1)}, bf16[256,128]{1,0:T(8,128)(2,1)S(1)}, u32[]{:S(2)}, u32[]{:S(2)}) %collective-permute-start.8) | collective-permute-done | bytes 65568 | tf_op jit(solution)/shard_map/ppermute | solution.py:28
  43.0 0.7 %tree_sum.1 = f32[2,32,512]{2,1,0:T(8,128)} custom-call(f32[2,32,512]{2,1,0:T(8,128)S(1)} %get-tuple-element.35.own_ref, bf16[256,128]{1,0:T(8,128)(2,1)S(1)} %collective-permute-done.8.refs_0_, bf16[256,128]{1,0:T(8,128)(2,1)S(1)} %collective-permute-done.9.refs_1_, bf16[272,128]{1,0:T(8,128)(2,1)S(1)} %collective-permute-done.10.refs_2_), custom_call_target="tpu_custom_call" | custom-call | tf_op jit(solution)/shard_map/tree_sum/pallas_call | solution.py:456
  (20 shorter events, 0.7 us)
Async XLA Ops:
  1.3 12.2 %copy-start = (f32[3,1024]{1,0:T(4,128)S(1)}, f32[3,1024]{1,0:T(4,128)}, u32[]{:S(2)}) copy-start(f32[3,1024]{1,0:T(4,128)} %pos_ref) | copy-start | bytes 36868
  1.3 12.2 %copy-start.1 = (f32[2,1,2,1024]{3,2,1,0:T(2,128)S(1)}, f32[2,1,2,1024]{3,2,1,0:T(2,128)}, u32[]{:S(2)}) copy-start(f32[2,1,2,1024]{3,2,1,0:T(2,128)} %param.8) | copy-start | bytes 49156
  1.3 12.1 %copy-start.2 = (f32[3,512]{1,0:T(4,128)S(1)}, f32[3,512]{1,0:T(4,128)}, u32[]{:S(2)}) copy-start(f32[3,512]{1,0:T(4,128)} %dir_ref.1) | copy-start | bytes 18436
  1.3 12.1 %copy-start.3 = (s32[4,2,8]{2,1,0:T(2,128)S(1)}, s32[4,2,8]{2,1,0:T(2,128)}, u32[]{:S(2)}) copy-start(s32[4,2,8]{2,1,0:T(2,128)} %delay_ref.1) | copy-start | bytes 772
  1.3 12.1 %copy-start.4 = (s32[1024]{0:T(1024)S(1)}, s32[1024]{0:T(1024)}, u32[]{:S(2)}) copy-start(s32[1024]{0:T(1024)} %param.11) | copy-start | bytes 12292
  1.3 12.1 %copy-start.5 = (s32[16]{0:T(128)S(1)}, s32[16]{0:T(128)}, u32[]{:S(2)}) copy-start(s32[16]{0:T(128)} %order_ref.1) | copy-start | bytes 196
  1.3 21.0 %collective-permute-start.1 = (bf16[2,128,256]{2,1,0:T(8,128)(2,1)S(1)}, bf16[2,128,256]{2,1,0:T(8,128)(2,1)S(1)}, u32[]{:S(2)}, u32[]{:S(2)}) collective-permute-start(bf16[2,128,256]{2,1,0:T(8,128)(2,1)S(1)} %split_channels.3.refs_0_), channel_id=1, source_target_pairs={{0,12},{4,8},{8,4},{12,0},{1,13},{5,9},{9,5},{13,1},{2,14},{6,10},... | collective-permute-start | bytes 393224 | tf_op jit(solution)/shard_map/ppermute | solution.py:28
  8.1 18.8 %collective-permute-start.2 = (bf16[2,256,256]{2,1,0:T(8,128)(2,1)S(1)}, bf16[2,256,256]{2,1,0:T(8,128)(2,1)S(1)}, u32[]{:S(2)}, u32[]{:S(2)}) collective-permute-start(bf16[2,256,256]{2,1,0:T(8,128)(2,1)S(1)} %split_channels.4.refs_0_), channel_id=1, source_target_pairs={{0,8},{4,12},{8,0},{12,4},{1,9},{5,13},{9,1},{13,5},{2,10},{6,14},... | collective-permute-start | bytes 786440 | tf_op jit(solution)/shard_map/ppermute | solution.py:28
  9.9 18.8 %collective-permute-start.4 = (bf16[2,128,256]{2,1,0:T(8,128)(2,1)S(1)}, bf16[2,128,256]{2,1,0:T(8,128)(2,1)S(1)}, u32[]{:S(2)}, u32[]{:S(2)}) collective-permute-start(bf16[2,128,256]{2,1,0:T(8,128)(2,1)S(1)} %get-tuple-element.30), channel_id=1, source_target_pairs={{0,12},{4,8},{8,4},{12,0},{1,13},{5,9},{9,5},{13,1},{2,14},{6,10},... | collective-permute-start | bytes 393224 | tf_op jit(solution)/shard_map/ppermute | solution.py:28
  11.9 15.6 %collective-permute-start.3 = (bf16[2,256,256]{2,1,0:T(8,128)(2,1)S(1)}, bf16[2,256,256]{2,1,0:T(8,128)(2,1)S(1)}, u32[]{:S(2)}, u32[]{:S(2)}) collective-permute-start(bf16[2,256,256]{2,1,0:T(8,128)(2,1)S(1)} %get-tuple-element.29), channel_id=1, source_target_pairs={{0,4},{4,0},{8,12},{12,8},{1,5},{5,1},{9,13},{13,9},{2,6},{6,2},{1... | collective-permute-start | bytes 786440 | tf_op jit(solution)/shard_map/ppermute | solution.py:28
  18.0 1.2 %collective-permute-start = (f32[3,512]{1,0:T(4,128)S(1)}, f32[3,512]{1,0:T(4,128)S(1)}, u32[]{:S(2)}, u32[]{:S(2)}) collective-permute-start(f32[3,512]{1,0:T(4,128)S(1)} %get-tuple-element.28), channel_id=1, source_target_pairs={{0,1},{1,0},{2,3},{3,2},{4,5},{5,4},{6,7},{7,6},{8,9},{9,8},{10,11... | collective-permute-start | bytes 18440 | tf_op jit(solution)/shard_map/ppermute | solution.py:28
  29.5 6.0 %collective-permute-start.7 = (bf16[160,128]{1,0:T(8,128)(2,1)S(1)}, bf16[160,128]{1,0:T(8,128)(2,1)S(1)}, u32[]{:S(2)}, u32[]{:S(2)}) collective-permute-start(bf16[160,128]{1,0:T(8,128)(2,1)S(1)} %get-tuple-element.34), channel_id=1, source_target_pairs={{0,9},{1,8},{4,13},{5,12},{8,1},{9,0},{12,5},{13,4},{2,11},{3,10},... | collective-permute-start | bytes 122888 | tf_op jit(solution)/shard_map/ppermute | solution.py:28
  30.1 5.4 %collective-permute-start.6 = (bf16[144,128]{1,0:T(8,128)(2,1)S(1)}, bf16[144,128]{1,0:T(8,128)(2,1)S(1)}, u32[]{:S(2)}, u32[]{:S(2)}) collective-permute-start(bf16[144,128]{1,0:T(8,128)(2,1)S(1)} %get-tuple-element.31.refs_0_), channel_id=1, source_target_pairs={{0,8},{4,12},{8,0},{12,4},{1,9},{5,13},{9,1},{13,5},{2,10},{6,14},... | collective-permute-start | bytes 110600 | tf_op jit(solution)/shard_map/ppermute | solution.py:28
  31.2 2.0 %collective-permute-start.5 = (bf16[128,128]{1,0:T(8,128)(2,1)S(1)}, bf16[128,128]{1,0:T(8,128)(2,1)S(1)}, u32[]{:S(2)}, u32[]{:S(2)}) collective-permute-start(bf16[128,128]{1,0:T(8,128)(2,1)S(1)} %get-tuple-element.33), channel_id=1, source_target_pairs={{0,1},{1,0},{2,3},{3,2},{4,5},{5,4},{6,7},{7,6},{8,9},{9,8},{10,11... | collective-permute-start | bytes 98312 | tf_op jit(solution)/shard_map/ppermute | solution.py:28
  35.7 7.3 %collective-permute-start.10 = (bf16[272,128]{1,0:T(8,128)(2,1)S(1)}, bf16[272,128]{1,0:T(8,128)(2,1)S(1)}, u32[]{:S(2)}, u32[]{:S(2)}) collective-permute-start(bf16[272,128]{1,0:T(8,128)(2,1)S(1)} %get-tuple-element.38), channel_id=1, source_target_pairs={{0,6},{2,4},{4,2},{6,0},{8,14},{10,12},{12,10},{14,8},{1,7},{3,5},... | collective-permute-start | bytes 208904 | tf_op jit(solution)/shard_map/ppermute | solution.py:28
  36.4 6.3 %collective-permute-start.8 = (bf16[256,128]{1,0:T(8,128)(2,1)S(1)}, bf16[256,128]{1,0:T(8,128)(2,1)S(1)}, u32[]{:S(2)}, u32[]{:S(2)}) collective-permute-start(bf16[256,128]{1,0:T(8,128)(2,1)S(1)} %get-tuple-element.36), channel_id=1, source_target_pairs={{0,4},{4,0},{8,12},{12,8},{1,5},{5,1},{9,13},{13,9},{2,6},{6,2},{1... | collective-permute-start | bytes 196616 | tf_op jit(solution)/shard_map/ppermute | solution.py:28
  38.7 4.3 %collective-permute-start.9 = (bf16[256,128]{1,0:T(8,128)(2,1)S(1)}, bf16[256,128]{1,0:T(8,128)(2,1)S(1)}, u32[]{:S(2)}, u32[]{:S(2)}) collective-permute-start(bf16[256,128]{1,0:T(8,128)(2,1)S(1)} %get-tuple-element.37), channel_id=1, source_target_pairs={{0,2},{2,0},{1,3},{3,1},{4,6},{6,4},{5,7},{7,5},{8,10},{10,8},{9,1... | collective-permute-start | bytes 196616 | tf_op jit(solution)/shard_map/ppermute | solution.py:28
